TPU v7x, 32 devices: a whole 2x2x4 slice. The times are simulated.
32 devices in a mesh: seq: 8 (over y, x, core), head: 4 (over z).
Axes of the slice: x: 2, y: 2, z: 4, core: 2. Of those that a mesh axis runs over, the one named last changes fastest.
Arguments:
- queries: bfloat16 [1024, 6144], P('seq', 'head'), may hold values from -60 to 60
- keys: bfloat16 [1024, 6144], P('seq', 'head'), may hold values from -6 to 6
- values: bfloat16 [1024, 6144], P('seq', 'head'), may hold values from -6 to 6
- band: int32 [48], P('head'), may hold values from 16 to 64
- picks: int32 [8, 16], P('seq'), may hold values from 0 to 127, as said below
- w_out: bfloat16 [6144, 6144], P('seq', 'head'), may hold values from -0.078125 to 0.078125
Outputs:
- output: bfloat16 [1024, 6144], P(('seq', 'head'))
Inputs may be any that keep to these rules, and one draw needn't show every extreme that they name: The 16 entries of a row of picks are distinct.
All inputs are finite; a program needn't handle non-finite values.
Results may differ from a plain program's by a relative error of at most 0.015.
Values may be sent and summed in bfloat16 or wider, within the bound.
No kernel may reach another device: no remote copies, remote signals or barrier semaphores. Data moves between devices by JAX's collectives and lax.ppermute only.
A program may use at most 128 MiB of HBM per device.

v0:
```python
import math

import jax
import jax.numpy as jnp
from jax import lax
from jax.sharding import PartitionSpec as P

BLOCK = 128


NEGATIVE_FILL = -1e30


def passed_along(value, axis, steps):
    count = lax.axis_size(axis)
    first, last = (max(0, -steps), min(count, count - steps))
    return lax.ppermute(value, axis, [(source, source + steps) for source in range(first, last)])


def local(queries, keys, values, band, picks, w_out):
    heads = band.shape[0]
    tok_rows, feat_dev = queries.shape
    head_size = feat_dev // heads
    blocks = tok_rows // BLOCK
    half_block = BLOCK // 2
    per_block = picks.shape[1]
    place = lax.axis_index("seq")
    first_block = place * blocks
    scale = 1.0 / math.sqrt(head_size)
    query_blocks = queries.reshape(blocks, BLOCK, heads, head_size)
    back_keys, back_values = passed_along(
        (keys[tok_rows - half_block :], values[tok_rows - half_block :]), "seq", 1
    )
    filler = jnp.zeros((BLOCK - half_block, feat_dev), keys.dtype)
    back_keys = jnp.concatenate([filler, back_keys], 0)
    back_values = jnp.concatenate([filler, back_values], 0)

    def windows(current, behind):
        joined = jnp.concatenate([behind, current], 0)
        early = joined[:tok_rows].reshape(blocks, BLOCK, heads, head_size)
        late = joined[BLOCK:].reshape(blocks, BLOCK, heads, head_size)
        return jnp.concatenate([early, late], 1)

    near_keys = windows(keys, back_keys)
    near_values = windows(values, back_values)
    block_ids = first_block + jnp.arange(blocks, dtype=jnp.int32)
    query_pos = block_ids[:, None] * BLOCK + jnp.arange(BLOCK, dtype=jnp.int32)[None, :]
    key_pos = block_ids[:, None] * BLOCK - BLOCK + jnp.arange(2 * BLOCK, dtype=jnp.int32)[None, :]
    key_grid = key_pos[:, None, None, :]
    query_grid = query_pos[:, None, :, None]
    near_ok = (
        (key_grid <= query_grid)
        & (key_grid > query_grid - band[None, :, None, None])
        & (key_grid >= 0)
    )
    near_scores = (
        jnp.einsum("nuhd,nthd->nhut", query_blocks, near_keys, preferred_element_type=jnp.float32)
        * scale
    )
    near_scores = jnp.where(near_ok, near_scores, NEGATIVE_FILL)
    running_max = jnp.max(near_scores, axis=-1, keepdims=True)
    near_weights = jnp.where(near_ok, jnp.exp(near_scores - running_max), 0.0)
    running_total = jnp.sum(near_weights, axis=-1, keepdims=True)
    accumulated = jnp.einsum(
        "nhut,nthd->nhud",
        near_weights.astype(jnp.bfloat16),
        near_values,
        preferred_element_type=jnp.float32,
    )
    chosen = picks[:, :, None]
    summary_keys = jnp.take_along_axis(
        keys.reshape(blocks, BLOCK, feat_dev), chosen, axis=1
    ).reshape(blocks * per_block, feat_dev)
    summary_values = jnp.take_along_axis(
        values.reshape(blocks, BLOCK, feat_dev), chosen, axis=1
    ).reshape(blocks * per_block, feat_dev)

    def absorb(state, piece, start):
        old_max, old_total, old_sum = state
        piece_keys, piece_values = piece
        count = piece_keys.shape[0]
        shaped_keys = piece_keys.reshape(count, heads, head_size)
        shaped_values = piece_values.reshape(count, heads, head_size)
        source = (start + jnp.arange(count, dtype=jnp.int32)) // per_block
        allowed = (source[None, :] < block_ids[:, None]) & (source[None, :] >= 0)
        allowed = allowed[:, None, None, :]
        far_scores = (
            jnp.einsum(
                "nuhd,shd->nhus", query_blocks, shaped_keys, preferred_element_type=jnp.float32
            )
            * scale
        )
        far_scores = jnp.where(allowed, far_scores, NEGATIVE_FILL)
        new_max = jnp.maximum(old_max, jnp.max(far_scores, axis=-1, keepdims=True))
        factor = jnp.exp(old_max - new_max)
        far_weights = jnp.where(allowed, jnp.exp(far_scores - new_max), 0.0)
        new_total = old_total * factor + jnp.sum(far_weights, axis=-1, keepdims=True)
        new_sum = old_sum * factor + jnp.einsum(
            "nhus,shd->nhud",
            far_weights.astype(jnp.bfloat16),
            shaped_values,
            preferred_element_type=jnp.float32,
        )
        return (new_max, new_total, new_sum)

    state = (running_max, running_total, accumulated)
    summary_pair = (summary_keys, summary_values)
    state = absorb(state, summary_pair, first_block * per_block)

    def passing(hop_index, carry):
        inner, moving = carry
        moving = passed_along((moving[0], moving[1]), "seq", 1)
        inner = absorb(inner, moving, (place - hop_index) * blocks * per_block)
        return (inner, moving)

    state, unused = lax.fori_loop(1, lax.axis_size("seq"), passing, (state, summary_pair))
    final_max, final_total, final_sum = state
    attention = (
        (final_sum / final_total)
        .transpose(0, 2, 1, 3)
        .reshape(tok_rows, feat_dev)
        .astype(jnp.bfloat16)
    )
    partial_value = lax.dot_general(
        attention,
        lax.all_gather(w_out, "seq", axis=0, tiled=True),
        (((1,), (1,)), ((), ())),
        preferred_element_type=jnp.float32,
    )
    return lax.psum_scatter(
        partial_value.astype(jnp.bfloat16), "head", scatter_dimension=0, tiled=True
    )


def solution(mesh):
    placed = (
        P("seq", "head"),
        P("seq", "head"),
        P("seq", "head"),
        P("head"),
        P("seq", None),
        P("seq", "head"),
    )
    return jax.shard_map(
        local, mesh=mesh, in_specs=placed, out_specs=P(("seq", "head"), None), check_vma=False
    )
```

profile of v0, /device:TPU:0, one launch (start us, length us, event | category | flops | bytes accessed | tf_op | source)
XLA Modules:
  0.0 172.2 jit_solution(6068632970164104790)
XLA Ops:
  6.5 0.7 all-gather.2.cloned.1.call-update
  7.9 3.1 %collective-permute-start.2 = (bf16[64,1536]{0,1:T(8,128)(2,1)S(1)}, bf16[64,1536]{0,1:T(8,128)(2,1)}, u32[]{:S(2)}, u32[]{:S(2)}) collective-permute-start(bf16[64,1536]{0,1:T(8,128)(2,1)S(1)} %slice.12), channel_id=1, source_target_pairs={{0,4},{4,8},{8,12},{12,16},{16,20},{20,24},{24,28},{1,5},{5,9},{9,... | collective-permute-start | bytes 589832 | tf_op jit(solution)/shard_map/ppermute | solution.py:17
  11.5 3.8 %collective-permute-start.3 = (bf16[64,1536]{0,1:T(8,128)(2,1)S(1)}, bf16[64,1536]{0,1:T(8,128)(2,1)S(1)}, u32[]{:S(2)}, u32[]{:S(2)}) collective-permute-start(bf16[64,1536]{0,1:T(8,128)(2,1)S(1)} %slice.13), channel_id=1, source_target_pairs={{0,4},{4,8},{8,12},{12,16},{16,20},{20,24},{24,28},{1,5},{5,9},{9,... | collective-permute-start | bytes 589832 | tf_op jit(solution)/shard_map/ppermute | solution.py:17
  15.3 0.6 gather_fusion
  15.9 0.6 gather_fusion.1
  17.2 0.7 reshape_reshape.7
  18.8 1.3 concatenate.12
  20.7 0.6 fusion.52
  21.6 0.4 convolution_bitcast_fusion.1
  22.0 0.6 fusion.24
  22.6 0.9 fusion.19
  23.5 66.0 %while.23 = (s32[]{:T(128)}, f32[1,12,128,1]{2,1,3,0:T(8,128)S(1)}, f32[1,12,128,1]{2,1,3,0:T(8,128)S(1)}, f32[1,12,128,128]{3,2,1,0:T(8,128)S(1)}, bf16[16,1536...) while((s32[]{:T(128)}, f32[1,12,128,1]{2,1,3,0:T(8,128)S(1)}, ...), condition=%wide.region_7.9_spmd, body=%wide.region_4.8_spmd.sunk | while | flops 13202228 | bytes 3047701 | solution.py:116
  23.5 3.4 %collective-permute-start = (bf16[16,1536]{1,0:T(8,128)(2,1)S(1)}, bf16[16,1536]{1,0:T(8,128)(2,1)S(1)}, u32[]{:S(2)}, u32[]{:S(2)}) collective-permute-start(bf16[16,1536]{1,0:T(8,128)(2,1)S(1)} %get-tuple-element.317), channel_id=1, source_target_pairs={{0,4},{4,8},{8,12},{12,16},{16,20},{20,24},{24,28},{1,5},{5,9},{9,... | collective-permute-start | bytes 147464 | tf_op jit(solution)/shard_map/while/body/eval_jaxpr/ppermute | solution.py:17
  26.9 4.4 %collective-permute-start.1 = (bf16[16,1536]{1,0:T(8,128)(2,1)S(1)}, bf16[16,1536]{1,0:T(8,128)(2,1)S(1)}, u32[]{:S(2)}, u32[]{:S(2)}) collective-permute-start(bf16[16,1536]{1,0:T(8,128)(2,1)S(1)} %get-tuple-element.318), channel_id=1, source_target_pairs={{0,4},{4,8},{8,12},{12,16},{16,20},{20,24},{24,28},{1,5},{5,9},{9,... | collective-permute-start | bytes 147464 | tf_op jit(solution)/shard_map/while/body/eval_jaxpr/ppermute | solution.py:17
  31.4 0.3 fusion.72
  31.9 0.3 collective-permute-done.1
  32.2 0.6 fusion.75
  32.8 3.1 %collective-permute-start = (bf16[16,1536]{1,0:T(8,128)(2,1)S(1)}, bf16[16,1536]{1,0:T(8,128)(2,1)S(1)}, u32[]{:S(2)}, u32[]{:S(2)}) collective-permute-start(bf16[16,1536]{1,0:T(8,128)(2,1)S(1)} %get-tuple-element.317), channel_id=1, source_target_pairs={{0,4},{4,8},{8,12},{12,16},{16,20},{20,24},{24,28},{1,5},{5,9},{9,... | collective-permute-start | bytes 147464 | tf_op jit(solution)/shard_map/while/body/eval_jaxpr/ppermute | solution.py:17
  35.9 4.4 %collective-permute-start.1 = (bf16[16,1536]{1,0:T(8,128)(2,1)S(1)}, bf16[16,1536]{1,0:T(8,128)(2,1)S(1)}, u32[]{:S(2)}, u32[]{:S(2)}) collective-permute-start(bf16[16,1536]{1,0:T(8,128)(2,1)S(1)} %get-tuple-element.318), channel_id=1, source_target_pairs={{0,4},{4,8},{8,12},{12,16},{16,20},{20,24},{24,28},{1,5},{5,9},{9,... | collective-permute-start | bytes 147464 | tf_op jit(solution)/shard_map/while/body/eval_jaxpr/ppermute | solution.py:17
  40.4 0.3 fusion.72
  40.9 0.3 collective-permute-done.1
  41.2 0.6 fusion.75
  41.9 3.1 %collective-permute-start = (bf16[16,1536]{1,0:T(8,128)(2,1)S(1)}, bf16[16,1536]{1,0:T(8,128)(2,1)S(1)}, u32[]{:S(2)}, u32[]{:S(2)}) collective-permute-start(bf16[16,1536]{1,0:T(8,128)(2,1)S(1)} %get-tuple-element.317), channel_id=1, source_target_pairs={{0,4},{4,8},{8,12},{12,16},{16,20},{20,24},{24,28},{1,5},{5,9},{9,... | collective-permute-start | bytes 147464 | tf_op jit(solution)/shard_map/while/body/eval_jaxpr/ppermute | solution.py:17
  45.0 4.4 %collective-permute-start.1 = (bf16[16,1536]{1,0:T(8,128)(2,1)S(1)}, bf16[16,1536]{1,0:T(8,128)(2,1)S(1)}, u32[]{:S(2)}, u32[]{:S(2)}) collective-permute-start(bf16[16,1536]{1,0:T(8,128)(2,1)S(1)} %get-tuple-element.318), channel_id=1, source_target_pairs={{0,4},{4,8},{8,12},{12,16},{16,20},{20,24},{24,28},{1,5},{5,9},{9,... | collective-permute-start | bytes 147464 | tf_op jit(solution)/shard_map/while/body/eval_jaxpr/ppermute | solution.py:17
  49.4 0.3 fusion.72
  49.9 0.3 collective-permute-done.1
  50.3 0.6 fusion.75
  50.9 3.1 %collective-permute-start = (bf16[16,1536]{1,0:T(8,128)(2,1)S(1)}, bf16[16,1536]{1,0:T(8,128)(2,1)S(1)}, u32[]{:S(2)}, u32[]{:S(2)}) collective-permute-start(bf16[16,1536]{1,0:T(8,128)(2,1)S(1)} %get-tuple-element.317), channel_id=1, source_target_pairs={{0,4},{4,8},{8,12},{12,16},{16,20},{20,24},{24,28},{1,5},{5,9},{9,... | collective-permute-start | bytes 147464 | tf_op jit(solution)/shard_map/while/body/eval_jaxpr/ppermute | solution.py:17
  54.0 5.0 %collective-permute-start.1 = (bf16[16,1536]{1,0:T(8,128)(2,1)S(1)}, bf16[16,1536]{1,0:T(8,128)(2,1)S(1)}, u32[]{:S(2)}, u32[]{:S(2)}) collective-permute-start(bf16[16,1536]{1,0:T(8,128)(2,1)S(1)} %get-tuple-element.318), channel_id=1, source_target_pairs={{0,4},{4,8},{8,12},{12,16},{16,20},{20,24},{24,28},{1,5},{5,9},{9,... | collective-permute-start | bytes 147464 | tf_op jit(solution)/shard_map/while/body/eval_jaxpr/ppermute | solution.py:17
  59.1 0.3 fusion.72
  59.6 0.4 collective-permute-done.1
  59.9 0.6 fusion.75
  60.6 3.4 %collective-permute-start = (bf16[16,1536]{1,0:T(8,128)(2,1)S(1)}, bf16[16,1536]{1,0:T(8,128)(2,1)S(1)}, u32[]{:S(2)}, u32[]{:S(2)}) collective-permute-start(bf16[16,1536]{1,0:T(8,128)(2,1)S(1)} %get-tuple-element.317), channel_id=1, source_target_pairs={{0,4},{4,8},{8,12},{12,16},{16,20},{20,24},{24,28},{1,5},{5,9},{9,... | collective-permute-start | bytes 147464 | tf_op jit(solution)/shard_map/while/body/eval_jaxpr/ppermute | solution.py:17
  64.0 4.4 %collective-permute-start.1 = (bf16[16,1536]{1,0:T(8,128)(2,1)S(1)}, bf16[16,1536]{1,0:T(8,128)(2,1)S(1)}, u32[]{:S(2)}, u32[]{:S(2)}) collective-permute-start(bf16[16,1536]{1,0:T(8,128)(2,1)S(1)} %get-tuple-element.318), channel_id=1, source_target_pairs={{0,4},{4,8},{8,12},{12,16},{16,20},{20,24},{24,28},{1,5},{5,9},{9,... | collective-permute-start | bytes 147464 | tf_op jit(solution)/shard_map/while/body/eval_jaxpr/ppermute | solution.py:17
  68.4 0.3 fusion.72
  68.9 0.3 collective-permute-done.1
  69.2 0.6 fusion.75
  69.9 3.8 %collective-permute-start = (bf16[16,1536]{1,0:T(8,128)(2,1)S(1)}, bf16[16,1536]{1,0:T(8,128)(2,1)S(1)}, u32[]{:S(2)}, u32[]{:S(2)}) collective-permute-start(bf16[16,1536]{1,0:T(8,128)(2,1)S(1)} %get-tuple-element.317), channel_id=1, source_target_pairs={{0,4},{4,8},{8,12},{12,16},{16,20},{20,24},{24,28},{1,5},{5,9},{9,... | collective-permute-start | bytes 147464 | tf_op jit(solution)/shard_map/while/body/eval_jaxpr/ppermute | solution.py:17
  73.7 4.4 %collective-permute-start.1 = (bf16[16,1536]{1,0:T(8,128)(2,1)S(1)}, bf16[16,1536]{1,0:T(8,128)(2,1)S(1)}, u32[]{:S(2)}, u32[]{:S(2)}) collective-permute-start(bf16[16,1536]{1,0:T(8,128)(2,1)S(1)} %get-tuple-element.318), channel_id=1, source_target_pairs={{0,4},{4,8},{8,12},{12,16},{16,20},{20,24},{24,28},{1,5},{5,9},{9,... | collective-permute-start | bytes 147464 | tf_op jit(solution)/shard_map/while/body/eval_jaxpr/ppermute | solution.py:17
  78.6 0.3 collective-permute-done.1
  79.0 0.6 fusion.75
  79.6 4.0 %collective-permute-start = (bf16[16,1536]{1,0:T(8,128)(2,1)S(1)}, bf16[16,1536]{1,0:T(8,128)(2,1)S(1)}, u32[]{:S(2)}, u32[]{:S(2)}) collective-permute-start(bf16[16,1536]{1,0:T(8,128)(2,1)S(1)} %get-tuple-element.317), channel_id=1, source_target_pairs={{0,4},{4,8},{8,12},{12,16},{16,20},{20,24},{24,28},{1,5},{5,9},{9,... | collective-permute-start | bytes 147464 | tf_op jit(solution)/shard_map/while/body/eval_jaxpr/ppermute | solution.py:17
  83.6 4.4 %collective-permute-start.1 = (bf16[16,1536]{1,0:T(8,128)(2,1)S(1)}, bf16[16,1536]{1,0:T(8,128)(2,1)S(1)}, u32[]{:S(2)}, u32[]{:S(2)}) collective-permute-start(bf16[16,1536]{1,0:T(8,128)(2,1)S(1)} %get-tuple-element.318), channel_id=1, source_target_pairs={{0,4},{4,8},{8,12},{12,16},{16,20},{20,24},{24,28},{1,5},{5,9},{9,... | collective-permute-start | bytes 147464 | tf_op jit(solution)/shard_map/while/body/eval_jaxpr/ppermute | solution.py:17
  88.5 0.3 collective-permute-done.1
  88.9 0.6 fusion.75
  89.9 26.4 %all-gather.2.cloned.1.call-done = bf16[6144,1536]{1,0:T(8,128)(2,1)} async-done(((bf16[768,1536]{1,0:T(8,128)(2,1)}), bf16[6144,1536]{1,0:T(8,128)(2,1)}) %all-gather.2.cloned.1.call-update) | async-done | bytes 18874384 | tf_op jit(solution)/shard_map/all_gather | solution.py:126
  116.3 13.7 %convolution_convert_fusion = bf16[128,6144]{1,0:T(8,128)(2,1)} fusion(bf16[128,1536]{0,1:T(8,128)(2,1)S(1)} %bitcast.157, bf16[6144,1536]{1,0:T(8,128)(2,1)} %all-gather.2.cloned.1.call-done), kind=kOutput, calls=%fused_computation.30 | convolution fusion | flops 2416705536 | bytes 20840448 | tf_op jit(solution)/shard_map/dot_general | solution.py:124
  130.0 35.4 %reduce-scatter.2.cloned.1.call-done = bf16[32,6144]{1,0:T(8,128)(2,1)} async-done(((bf16[128,6144]{1,0:T(8,128)(2,1)}), bf16[32,6144]{1,0:T(8,128)(2,1)}) %reduce-scatter.2.cloned.1.call-update) | async-done | bytes 393232 | tf_op jit(solution)/shard_map/reduce_scatter | solution.py:130
  (111 shorter events, 5.5 us)
Async XLA Ops:
  6.5 1.0 copy-start
  6.5 4.5 %copy-start.1 = (bf16[128,1536]{1,0:T(8,128)(2,1)S(1)}, bf16[128,1536]{1,0:T(8,128)(2,1)}, u32[]{:S(2)}) copy-start(bf16[128,1536]{1,0:T(8,128)(2,1)} %param.12) | copy-start | bytes 1179652
  6.5 109.7 %all-gather.2.cloned.1.call-start = ((), (), s32[]{:S(2)}) async-start(), calls=%async_computation.1 | async-start | bytes 21233664 | tf_op jit(solution)/shard_map/all_gather | solution.py:126
  7.3 8.0 %copy-start.9 = (s32[1,16]{1,0:T(1,128)S(1)}, s32[1,16]{1,0:T(1,128)}, u32[]{:S(2)}) copy-start(s32[1,16]{1,0:T(1,128)} %param.14) | copy-start | bytes 196
  7.3 158.1 %reduce-scatter.2.cloned.1.call-start = ((), (), s32[]{:S(2)}) async-start(), calls=%async_computation.2 | async-start | bytes 1966080 | tf_op jit(solution)/shard_map/reduce_scatter | solution.py:130
  7.8 8.8 %copy-start.2 = (bf16[128,1536]{1,0:T(8,128)(2,1)S(1)}, bf16[128,1536]{1,0:T(8,128)(2,1)}, u32[]{:S(2)}) copy-start(bf16[128,1536]{1,0:T(8,128)(2,1)} %param.10) | copy-start | bytes 1179652
  7.9 10.9 %collective-permute-start.2 = (bf16[64,1536]{0,1:T(8,128)(2,1)S(1)}, bf16[64,1536]{0,1:T(8,128)(2,1)}, u32[]{:S(2)}, u32[]{:S(2)}) collective-permute-start(bf16[64,1536]{0,1:T(8,128)(2,1)S(1)} %slice.12), channel_id=1, source_target_pairs={{0,4},{4,8},{8,12},{12,16},{16,20},{20,24},{24,28},{1,5},{5,9},{9,... | collective-permute-start | bytes 589832 | tf_op jit(solution)/shard_map/ppermute | solution.py:17
  11.5 8.9 %collective-permute-start.3 = (bf16[64,1536]{0,1:T(8,128)(2,1)S(1)}, bf16[64,1536]{0,1:T(8,128)(2,1)S(1)}, u32[]{:S(2)}, u32[]{:S(2)}) collective-permute-start(bf16[64,1536]{0,1:T(8,128)(2,1)S(1)} %slice.13), channel_id=1, source_target_pairs={{0,4},{4,8},{8,12},{12,16},{16,20},{20,24},{24,28},{1,5},{5,9},{9,... | collective-permute-start | bytes 589832 | tf_op jit(solution)/shard_map/ppermute | solution.py:17
  16.7 2.0 %copy-start.8 = (s32[12]{0:T(128)S(1)}, s32[12]{0:T(128)}, u32[]{:S(2)}) copy-start(s32[12]{0:T(128)} %param.13) | copy-start | bytes 148
  17.1 3.0 %copy-start.4 = (bf16[1,16,1536]{2,1,0:T(8,128)(2,1)}, bf16[1,16,1536]{2,1,0:T(8,128)(2,1)S(1)}, u32[]{:S(2)}) copy-start(bf16[1,16,1536]{2,1,0:T(8,128)(2,1)S(1)} %get-tuple-element.240) | copy-start | bytes 147460
  17.1 3.0 %copy-start.6 = (bf16[1,16,1536]{2,1,0:T(8,128)(2,1)}, bf16[1,16,1536]{2,1,0:T(8,128)(2,1)S(1)}, u32[]{:S(2)}) copy-start(bf16[1,16,1536]{2,1,0:T(8,128)(2,1)S(1)} %get-tuple-element.241) | copy-start | bytes 147460
  20.7 0.9 copy-start.3
  22.6 0.9 copy-start.5
  22.6 0.9 copy-start.7
  23.5 7.9 %collective-permute-start = (bf16[16,1536]{1,0:T(8,128)(2,1)S(1)}, bf16[16,1536]{1,0:T(8,128)(2,1)S(1)}, u32[]{:S(2)}, u32[]{:S(2)}) collective-permute-start(bf16[16,1536]{1,0:T(8,128)(2,1)S(1)} %get-tuple-element.317), channel_id=1, source_target_pairs={{0,4},{4,8},{8,12},{12,16},{16,20},{20,24},{24,28},{1,5},{5,9},{9,... | collective-permute-start | bytes 147464 | tf_op jit(solution)/shard_map/while/body/eval_jaxpr/ppermute | solution.py:17
  26.9 5.3 %collective-permute-start.1 = (bf16[16,1536]{1,0:T(8,128)(2,1)S(1)}, bf16[16,1536]{1,0:T(8,128)(2,1)S(1)}, u32[]{:S(2)}, u32[]{:S(2)}) collective-permute-start(bf16[16,1536]{1,0:T(8,128)(2,1)S(1)} %get-tuple-element.318), channel_id=1, source_target_pairs={{0,4},{4,8},{8,12},{12,16},{16,20},{20,24},{24,28},{1,5},{5,9},{9,... | collective-permute-start | bytes 147464 | tf_op jit(solution)/shard_map/while/body/eval_jaxpr/ppermute | solution.py:17
  32.8 7.5 %collective-permute-start = (bf16[16,1536]{1,0:T(8,128)(2,1)S(1)}, bf16[16,1536]{1,0:T(8,128)(2,1)S(1)}, u32[]{:S(2)}, u32[]{:S(2)}) collective-permute-start(bf16[16,1536]{1,0:T(8,128)(2,1)S(1)} %get-tuple-element.317), channel_id=1, source_target_pairs={{0,4},{4,8},{8,12},{12,16},{16,20},{20,24},{24,28},{1,5},{5,9},{9,... | collective-permute-start | bytes 147464 | tf_op jit(solution)/shard_map/while/body/eval_jaxpr/ppermute | solution.py:17
  35.9 5.3 %collective-permute-start.1 = (bf16[16,1536]{1,0:T(8,128)(2,1)S(1)}, bf16[16,1536]{1,0:T(8,128)(2,1)S(1)}, u32[]{:S(2)}, u32[]{:S(2)}) collective-permute-start(bf16[16,1536]{1,0:T(8,128)(2,1)S(1)} %get-tuple-element.318), channel_id=1, source_target_pairs={{0,4},{4,8},{8,12},{12,16},{16,20},{20,24},{24,28},{1,5},{5,9},{9,... | collective-permute-start | bytes 147464 | tf_op jit(solution)/shard_map/while/body/eval_jaxpr/ppermute | solution.py:17
  41.9 7.6 %collective-permute-start = (bf16[16,1536]{1,0:T(8,128)(2,1)S(1)}, bf16[16,1536]{1,0:T(8,128)(2,1)S(1)}, u32[]{:S(2)}, u32[]{:S(2)}) collective-permute-start(bf16[16,1536]{1,0:T(8,128)(2,1)S(1)} %get-tuple-element.317), channel_id=1, source_target_pairs={{0,4},{4,8},{8,12},{12,16},{16,20},{20,24},{24,28},{1,5},{5,9},{9,... | collective-permute-start | bytes 147464 | tf_op jit(solution)/shard_map/while/body/eval_jaxpr/ppermute | solution.py:17
  45.0 5.3 %collective-permute-start.1 = (bf16[16,1536]{1,0:T(8,128)(2,1)S(1)}, bf16[16,1536]{1,0:T(8,128)(2,1)S(1)}, u32[]{:S(2)}, u32[]{:S(2)}) collective-permute-start(bf16[16,1536]{1,0:T(8,128)(2,1)S(1)} %get-tuple-element.318), channel_id=1, source_target_pairs={{0,4},{4,8},{8,12},{12,16},{16,20},{20,24},{24,28},{1,5},{5,9},{9,... | collective-permute-start | bytes 147464 | tf_op jit(solution)/shard_map/while/body/eval_jaxpr/ppermute | solution.py:17
  50.9 8.1 %collective-permute-start = (bf16[16,1536]{1,0:T(8,128)(2,1)S(1)}, bf16[16,1536]{1,0:T(8,128)(2,1)S(1)}, u32[]{:S(2)}, u32[]{:S(2)}) collective-permute-start(bf16[16,1536]{1,0:T(8,128)(2,1)S(1)} %get-tuple-element.317), channel_id=1, source_target_pairs={{0,4},{4,8},{8,12},{12,16},{16,20},{20,24},{24,28},{1,5},{5,9},{9,... | collective-permute-start | bytes 147464 | tf_op jit(solution)/shard_map/while/body/eval_jaxpr/ppermute | solution.py:17
  54.0 5.9 %collective-permute-start.1 = (bf16[16,1536]{1,0:T(8,128)(2,1)S(1)}, bf16[16,1536]{1,0:T(8,128)(2,1)S(1)}, u32[]{:S(2)}, u32[]{:S(2)}) collective-permute-start(bf16[16,1536]{1,0:T(8,128)(2,1)S(1)} %get-tuple-element.318), channel_id=1, source_target_pairs={{0,4},{4,8},{8,12},{12,16},{16,20},{20,24},{24,28},{1,5},{5,9},{9,... | collective-permute-start | bytes 147464 | tf_op jit(solution)/shard_map/while/body/eval_jaxpr/ppermute | solution.py:17
  60.6 7.8 %collective-permute-start = (bf16[16,1536]{1,0:T(8,128)(2,1)S(1)}, bf16[16,1536]{1,0:T(8,128)(2,1)S(1)}, u32[]{:S(2)}, u32[]{:S(2)}) collective-permute-start(bf16[16,1536]{1,0:T(8,128)(2,1)S(1)} %get-tuple-element.317), channel_id=1, source_target_pairs={{0,4},{4,8},{8,12},{12,16},{16,20},{20,24},{24,28},{1,5},{5,9},{9,... | collective-permute-start | bytes 147464 | tf_op jit(solution)/shard_map/while/body/eval_jaxpr/ppermute | solution.py:17
  64.0 5.3 %collective-permute-start.1 = (bf16[16,1536]{1,0:T(8,128)(2,1)S(1)}, bf16[16,1536]{1,0:T(8,128)(2,1)S(1)}, u32[]{:S(2)}, u32[]{:S(2)}) collective-permute-start(bf16[16,1536]{1,0:T(8,128)(2,1)S(1)} %get-tuple-element.318), channel_id=1, source_target_pairs={{0,4},{4,8},{8,12},{12,16},{16,20},{20,24},{24,28},{1,5},{5,9},{9,... | collective-permute-start | bytes 147464 | tf_op jit(solution)/shard_map/while/body/eval_jaxpr/ppermute | solution.py:17
  69.9 8.2 %collective-permute-start = (bf16[16,1536]{1,0:T(8,128)(2,1)S(1)}, bf16[16,1536]{1,0:T(8,128)(2,1)S(1)}, u32[]{:S(2)}, u32[]{:S(2)}) collective-permute-start(bf16[16,1536]{1,0:T(8,128)(2,1)S(1)} %get-tuple-element.317), channel_id=1, source_target_pairs={{0,4},{4,8},{8,12},{12,16},{16,20},{20,24},{24,28},{1,5},{5,9},{9,... | collective-permute-start | bytes 147464 | tf_op jit(solution)/shard_map/while/body/eval_jaxpr/ppermute | solution.py:17
  73.7 5.3 %collective-permute-start.1 = (bf16[16,1536]{1,0:T(8,128)(2,1)S(1)}, bf16[16,1536]{1,0:T(8,128)(2,1)S(1)}, u32[]{:S(2)}, u32[]{:S(2)}) collective-permute-start(bf16[16,1536]{1,0:T(8,128)(2,1)S(1)} %get-tuple-element.318), channel_id=1, source_target_pairs={{0,4},{4,8},{8,12},{12,16},{16,20},{20,24},{24,28},{1,5},{5,9},{9,... | collective-permute-start | bytes 147464 | tf_op jit(solution)/shard_map/while/body/eval_jaxpr/ppermute | solution.py:17
  79.6 8.4 %collective-permute-start = (bf16[16,1536]{1,0:T(8,128)(2,1)S(1)}, bf16[16,1536]{1,0:T(8,128)(2,1)S(1)}, u32[]{:S(2)}, u32[]{:S(2)}) collective-permute-start(bf16[16,1536]{1,0:T(8,128)(2,1)S(1)} %get-tuple-element.317), channel_id=1, source_target_pairs={{0,4},{4,8},{8,12},{12,16},{16,20},{20,24},{24,28},{1,5},{5,9},{9,... | collective-permute-start | bytes 147464 | tf_op jit(solution)/shard_map/while/body/eval_jaxpr/ppermute | solution.py:17
  83.6 5.3 %collective-permute-start.1 = (bf16[16,1536]{1,0:T(8,128)(2,1)S(1)}, bf16[16,1536]{1,0:T(8,128)(2,1)S(1)}, u32[]{:S(2)}, u32[]{:S(2)}) collective-permute-start(bf16[16,1536]{1,0:T(8,128)(2,1)S(1)} %get-tuple-element.318), channel_id=1, source_target_pairs={{0,4},{4,8},{8,12},{12,16},{16,20},{20,24},{24,28},{1,5},{5,9},{9,... | collective-permute-start | bytes 147464 | tf_op jit(solution)/shard_map/while/body/eval_jaxpr/ppermute | solution.py:17
Sparse Core Ops, SparseCore 0:
  9.2 106.9 all-gather.1
  130.1 35.1 reduce-scatter.1
where the time goes:
time: 173 us; the launch traced here: 172 us
  waiting for transfers between devices  64.9 us (38%)
  starting transfers between devices  62.2 us (36%)
  matrix products  22.5 us (13%)
  between operations  13.7 us (8%)
  local copies, waits for them, and re-layouts  6.26 us (4%)
  other arithmetic  1.96 us (1%)
    ppermute x16, starting transfers between devices, passed_along(): lax.ppermute(value, axis, [(source, source + steps) for source in range(f...  62.2 us
    reduce_scatter x1, waiting for transfers between devices, local(): lax.psum_scatter(partial_value.astype(jnp.bfloat16), 'head', scatter_dime...  35.4 us
    all_gather x1, waiting for transfers between devices, local(): lax.all_gather(w_out, 'seq', axis=0, tiled=True)  26.4 us
    dot_general x1, matrix products, local(): lax.dot_general(attention, lax.all_gather(w_out, 'seq', axis=0, tiled=Tru...  13.7 us
    dot_general x8, matrix products, absorb(): jnp.einsum('nhus,shd->nhud', far_weights.astype(jnp.bfloat16), shaped_val...  4.76 us
  transfers between devices with their start and end apart: 18, of which 9 were waited for; matrix products, arithmetic and copies ran while one was open for 10% of the time, Pallas kernels for 0%

commit v1 on v0

v1 whole, which is shorter than its diff:
```python
import math

import jax
import jax.numpy as jnp
from jax import lax
from jax.experimental import pallas as pl
from jax.experimental.pallas import tpu as pltpu
from jax.sharding import PartitionSpec as P

BLOCK = 128
HALO = 64
NEGATIVE_FILL = -1e30
LAST = (((1,), (1,)), ((), ()))


def vmem():
    return pl.BlockSpec(memory_space=pltpu.VMEM)


def smem():
    return pl.BlockSpec(memory_space=pltpu.SMEM)


def pick_kernel(picks_ref, keys_ref, values_ref, summary_ref, halo_ref):
    per_block = picks_ref.shape[1]
    row = lax.broadcasted_iota(jnp.int32, (per_block, BLOCK), 0)
    wanted = jnp.zeros((per_block, BLOCK), jnp.int32)
    for r in range(per_block):
        wanted = jnp.where(row == r, picks_ref[0, r], wanted)
    column = lax.broadcasted_iota(jnp.int32, (per_block, BLOCK), 1)
    chosen = jnp.where(column == wanted, 1.0, 0.0).astype(jnp.bfloat16)
    for part, ref in enumerate((keys_ref, values_ref)):
        taken = jnp.dot(chosen, ref[...], preferred_element_type=jnp.float32)
        summary_ref[part] = taken.astype(jnp.bfloat16)
        halo_ref[part] = ref[BLOCK - HALO :, :]


def attend_kernel(band_ref, q_ref, k_ref, v_ref, halo_ref, far_ref, out_ref):
    heads = band_ref.shape[0]
    size = q_ref.shape[1] // heads
    sources, unused, per_block, feat = far_ref.shape
    far_rows = sources * per_block
    place = lax.axis_index("seq")
    scale = 1.0 / math.sqrt(size)
    own_q = lax.broadcasted_iota(jnp.int32, (BLOCK, BLOCK), 0)
    own_k = lax.broadcasted_iota(jnp.int32, (BLOCK, BLOCK), 1)
    own_gap = own_q - own_k
    back_q = lax.broadcasted_iota(jnp.int32, (BLOCK, HALO), 0)
    back_k = lax.broadcasted_iota(jnp.int32, (BLOCK, HALO), 1) - HALO
    back_gap = jnp.where(place > 0, back_q - back_k, BLOCK * 4)
    far_owner = lax.broadcasted_iota(jnp.int32, (BLOCK, far_rows), 1) // per_block
    far_ok = far_owner < place
    for h in range(heads):
        cols = slice(h * size, (h + 1) * size)
        query = q_ref[:, cols]
        all_keys = jnp.concatenate(
            [k_ref[:, cols], far_ref[:, 0, :, cols].reshape(far_rows, size), halo_ref[0, :, cols]], 0
        )
        all_values = jnp.concatenate(
            [v_ref[:, cols], far_ref[:, 1, :, cols].reshape(far_rows, size), halo_ref[1, :, cols]], 0
        )
        scores = lax.dot_general(query, all_keys, LAST, preferred_element_type=jnp.float32) * scale
        own_ok = (own_gap >= 0) & (own_gap < band_ref[h])
        back_ok = back_gap < band_ref[h]
        valid = jnp.concatenate([own_ok, far_ok, back_ok], 1)
        scores = jnp.where(valid, scores, NEGATIVE_FILL)
        largest = jnp.max(scores, axis=1, keepdims=True)
        weights = jnp.where(valid, jnp.exp(scores - largest), 0.0)
        total = jnp.sum(weights, axis=1, keepdims=True)
        mixed = jnp.dot(weights.astype(jnp.bfloat16), all_values, preferred_element_type=jnp.float32)
        out_ref[:, cols] = (mixed / total).astype(jnp.bfloat16)


def project_kernel(att_ref, w_ref, out_ref):
    parts, unused, rows, wide = out_ref.shape
    found = lax.dot_general(att_ref[...], w_ref[...], LAST, preferred_element_type=jnp.float32)
    out_ref[...] = found.astype(jnp.bfloat16).reshape(parts, 1, rows, wide)


def local(queries, keys, values, band, picks, w_out):
    heads = band.shape[0]
    tok_rows, feat = queries.shape
    per_block = picks.shape[1]
    seq = lax.axis_size("seq")
    groups = lax.axis_size("head")
    wide = w_out.shape[0]
    rows = tok_rows // groups
    bf16 = jnp.bfloat16
    summary, halo = pl.pallas_call(
        pick_kernel,
        out_shape=(
            jax.ShapeDtypeStruct((2, per_block, feat), bf16),
            jax.ShapeDtypeStruct((2, HALO, feat), bf16),
        ),
        in_specs=[smem(), vmem(), vmem()],
        out_specs=(vmem(), vmem()),
    )(picks, keys, values)
    far = lax.all_gather(summary, "seq", axis=0, tiled=False)
    halo = lax.ppermute(halo, "seq", [(i, i + 1) for i in range(seq - 1)])
    attention = pl.pallas_call(
        attend_kernel,
        out_shape=jax.ShapeDtypeStruct((tok_rows, feat), bf16),
        in_specs=[smem()] + [vmem()] * 5,
        out_specs=vmem(),
        compiler_params=pltpu.CompilerParams(vmem_limit_bytes=40 << 20),
    )(band, queries, keys, values, halo, far)
    gathered = lax.all_gather(attention, "seq", axis=0, tiled=True)
    partial_value = pl.pallas_call(
        project_kernel,
        grid=(seq,),
        out_shape=jax.ShapeDtypeStruct((groups, seq, rows, wide), bf16),
        in_specs=[
            pl.BlockSpec((tok_rows, feat), lambda s: (s, 0)),
            pl.BlockSpec((wide, feat), lambda s: (0, 0)),
        ],
        out_specs=pl.BlockSpec((groups, 1, rows, wide), lambda s: (0, s, 0, 0)),
        compiler_params=pltpu.CompilerParams(vmem_limit_bytes=40 << 20),
    )(gathered, w_out)
    summed = lax.psum_scatter(
        partial_value.reshape(groups * seq * rows, wide), "head", scatter_dimension=0, tiled=True
    )
    moved = lax.all_to_all(summed.reshape(seq, rows, wide), "seq", 0, 0, tiled=False)
    return moved.transpose(1, 0, 2).reshape(rows, seq * wide)


def solution(mesh):
    placed = (
        P("seq", "head"),
        P("seq", "head"),
        P("seq", "head"),
        P("head"),
        P("seq", None),
        P("seq", "head"),
    )
    return jax.shard_map(
        local, mesh=mesh, in_specs=placed, out_specs=P(("seq", "head"), None), check_vma=False
    )
```

time: 173 us -> 133 us (0.77)
  starting transfers between devices: 62.2 us -> 2.41 us
  blocking collectives: 0 us -> 27.8 us
  matrix products: 22.5 us -> 0 us
  Pallas kernels: 0 us -> 14.4 us
  waiting for transfers between devices: 64.9 us -> 68.2 us
  other arithmetic: 1.96 us -> 0 us
    ppermute x16 -> x1, starting transfers between devices: 62.2 us -> 2.37 us  [local(): halo = lax.ppermute(halo, 'seq', [(i, i + 1) for i in range(seq - 1)])]
    dot_general x19 -> x0, matrix products: 22.5 us -> none  [the longest x1 13.7 us: local(): lax.dot_general(attention, lax.all_gather(w_out, 'seq', axis=0, tiled=Tru...]
    all_gather x0 -> x1, blocking collectives: none -> 15.8 us  [local(): far = lax.all_gather(summary, 'seq', axis=0, tiled=False)]
    pallas_call x0 -> x3, Pallas kernels: none -> 14.4 us  [the longest x1 7.75 us: local(): pl.pallas_call(project_kernel, grid=(seq,), out_shape=jax.ShapeDtypeStruc...]
    all_to_all x0 -> x1, blocking collectives: none -> 12 us  [local(): lax.all_to_all(summed.reshape(seq, rows, wide), 'seq', 0, 0, tiled=False)]
    all_gather x1, waiting for transfers between devices: 26.4 us -> 32.7 us  [local(): gathered = lax.all_gather(attention, 'seq', axis=0, tiled=True)]
    unnamed x23 -> x12, local copies, waits for them, and re-layouts: 1.07 us -> 5.53 us
    ppermute x16 -> x1, waiting for transfers between devices: 2.44 us -> 0.01 us  [local(): halo = lax.ppermute(halo, 'seq', [(i, i + 1) for i in range(seq - 1)])]
  transfers between devices with their start and end apart: 18 -> 3, of which waited for: 9 -> 2; matrix products, arithmetic and copies ran while one was open for 10% -> 0% of each run, Pallas kernels for 0% -> 0%
where the time goes in v1:
time: 133 us
  waiting for transfers between devices  68.2 us (51%)
  blocking collectives  27.8 us (21%)
  Pallas kernels  14.4 us (11%)
  between operations  13.4 us (10%)
  local copies, waits for them, and re-layouts  6.31 us (5%)
  starting transfers between devices  2.41 us (2%)
    reduce_scatter x1, waiting for transfers between devices, local(): lax.psum_scatter(partial_value.reshape(groups * seq * rows, wide), 'head'...  35.4 us
    all_gather x1, waiting for transfers between devices, local(): gathered = lax.all_gather(attention, 'seq', axis=0, tiled=True)  32.7 us
    all_gather x1, blocking collectives, local(): far = lax.all_gather(summary, 'seq', axis=0, tiled=False)  15.8 us
    all_to_all x1, blocking collectives, local(): lax.all_to_all(summed.reshape(seq, rows, wide), 'seq', 0, 0, tiled=False)  12 us
    pallas_call x1, Pallas kernels, local(): pl.pallas_call(project_kernel, grid=(seq,), out_shape=jax.ShapeDtypeStruc...  7.75 us
    unnamed x12, local copies, waits for them, and re-layouts  5.53 us
    pallas_call x1, Pallas kernels, local(): pl.pallas_call(attend_kernel, out_shape=jax.ShapeDtypeStruct((tok_rows, f...  4.54 us
  transfers between devices with their start and end apart: 3, of which 2 were waited for; matrix products, arithmetic and copies ran while one was open for 0% of the time, Pallas kernels for 0%

profile of v1, /device:TPU:0, one launch (start us, length us, event | category | flops | bytes accessed | tf_op | source)
XLA Modules:
  0.0 132.6 jit_solution(15050788723817457534)
XLA Ops:
  6.5 0.0 copy-start.1
  6.5 0.0 all-gather.3.cloned.1.call-start
  6.5 2.1 %shard_map.64 = (bf16[2,16,1536]{2,1,0:T(8,128)(2,1)}, bf16[2,64,1536]{2,1,0:T(8,128)(2,1)}) custom-call(s32[1,16]{1,0:T(1,128)} %picks_ref.1, bf16[128,1536]{1,0:T(8,128)(2,1)} %k_ref.1, bf16[128,1536]{1,0:T(8,128)(2,1)} %v_ref.1), custom_call_target="tpu_custom_call" | custom-call | tf_op jit(solution)/shard_map/pallas_call | solution.py:89
  8.7 2.4 %collective-permute-start = (bf16[2,64,1536]{2,1,0:T(8,128)(2,1)}, bf16[2,64,1536]{2,1,0:T(8,128)(2,1)S(1)}, u32[]{:S(2)}, u32[]{:S(2)}) collective-permute-start(bf16[2,64,1536]{2,1,0:T(8,128)(2,1)} %get-tuple-element.7), channel_id=1, source_target_pairs={{0,4},{4,8},{8,12},{12,16},{16,20},{20,24},{24,28},{1,5},{5,9},{9,... | collective-permute-start | bytes 1179656 | tf_op jit(solution)/shard_map/ppermute | solution.py:99
  11.1 15.8 %all-gather = bf16[16,16,1536]{2,1,0:T(8,128)(2,1)S(1)} all-gather(bf16[2,16,1536]{2,1,0:T(8,128)(2,1)} %get-tuple-element.8), channel_id=2, replica_groups=mesh['seq'=8,'head'=4] {'seq'}, dimensions={0}, use_global_device_ids=true | all-gather | bytes 884736 | tf_op jit(solution)/shard_map/all_gather | solution.py:98
  26.9 0.0 collective-permute-done.halo_ref
  26.9 0.0 copy-start.2
  26.9 1.0 copy-done.2
  27.9 0.0 copy-start.3
  27.9 1.0 copy-done.3
  28.9 0.0 copy-start.4
  28.9 1.0 copy-done.4
  29.9 0.0 copy-start.5
  29.9 0.7 copy-done.5
  30.5 4.5 %shard_map.65 = bf16[128,1536]{1,0:T(8,128)(2,1)} custom-call(s32[12]{0:T(128)S(1)} %copy-done.5, bf16[128,1536]{1,0:T(8,128)(2,1)S(1)} %copy-done.4, bf16[128,1536]{1,0:T(8,128)(2,1)S(1)} %copy-done.2, bf16[128,1536]{1,0:T(8,128)(2,1)S(1)} %copy-done.3, bf16[2,64,1536]{2,1,0:T(8,128)(2,1)S(1)} %collective-permute-done.halo_ref, ...), custom_call_target="tpu_custom_call" | custom-call | tf_op jit(solution)/shard_map/pallas_call | solution.py:100
  35.1 0.0 all-gather.3.cloned.1.call-update
  35.1 0.0 reduce-scatter.2.cloned.1.call-start
  35.2 32.7 %all-gather.3.cloned.1.call-done.att_ref = bf16[1024,1536]{1,0:T(8,128)(2,1)} async-done(((bf16[128,1536]{1,0:T(8,128)(2,1)}), bf16[1024,1536]{1,0:T(8,128)(2,1)}) %all-gather.3.cloned.1.call-update) | async-done | bytes 3145744 | tf_op jit(solution)/shard_map/all_gather | solution.py:107
  67.9 0.0 copy-done.1
  67.9 0.0 copy-start
  67.9 1.9 %copy-done = bf16[1024,1536]{1,0:T(8,128)(2,1)S(1)} copy-done((bf16[1024,1536]{1,0:T(8,128)(2,1)S(1)}, bf16[1024,1536]{1,0:T(8,128)(2,1)}, u32[]{:S(2)}) %copy-start) | copy-done | bytes 3145752
  69.8 7.7 %shard_map.66 = bf16[4,8,32,768]{3,2,1,0:T(8,128)(2,1)} custom-call(bf16[1024,1536]{1,0:T(8,128)(2,1)S(1)} %copy-done, bf16[768,1536]{1,0:T(8,128)(2,1)S(1)} %copy-done.1), custom_call_target="tpu_custom_call" | custom-call | tf_op jit(solution)/shard_map/pallas_call | solution.py:108
  77.5 0.0 reduce-scatter.2.cloned.1.call-update
  77.5 35.4 %reduce-scatter.2.cloned.1.call-done = bf16[256,768]{1,0:T(8,128)(2,1)} async-done(((bf16[1024,768]{1,0:T(8,128)(2,1)}), bf16[256,768]{1,0:T(8,128)(2,1)}) %reduce-scatter.2.cloned.1.call-update) | async-done | bytes 393232 | tf_op jit(solution)/shard_map/reduce_scatter | solution.py:119
  113.0 12.0 %all_to_all.5 = bf16[8,32,768]{2,1,0:T(8,128)(2,1)S(1)} all-to-all(bf16[8,32,768]{2,1,0:T(8,128)(2,1)} %bitcast.8), channel_id=1, replica_groups=mesh['seq'=8,'head'=4] {'seq'}, dimensions={0} | all-to-all | bytes 786432 | tf_op jit(solution)/shard_map/all_to_all | solution.py:122
  125.0 0.8 copy.9
Async XLA Ops:
  6.5 61.4 %copy-start.1 = (bf16[768,1536]{1,0:T(8,128)(2,1)S(1)}, bf16[768,1536]{1,0:T(8,128)(2,1)}, u32[]{:S(2)}) copy-start(bf16[768,1536]{1,0:T(8,128)(2,1)} %w_ref.1) | copy-start | bytes 7077892
  6.5 61.3 %all-gather.3.cloned.1.call-start = ((), (), s32[]{:S(2)}) async-start(), calls=%async_computation.2 | async-start | bytes 3538944 | tf_op jit(solution)/shard_map/all_gather | solution.py:107
  8.7 18.2 %collective-permute-start = (bf16[2,64,1536]{2,1,0:T(8,128)(2,1)}, bf16[2,64,1536]{2,1,0:T(8,128)(2,1)S(1)}, u32[]{:S(2)}, u32[]{:S(2)}) collective-permute-start(bf16[2,64,1536]{2,1,0:T(8,128)(2,1)} %get-tuple-element.7), channel_id=1, source_target_pairs={{0,4},{4,8},{8,12},{12,16},{16,20},{20,24},{24,28},{1,5},{5,9},{9,... | collective-permute-start | bytes 1179656 | tf_op jit(solution)/shard_map/ppermute | solution.py:99
  26.9 1.0 copy-start.2
  27.9 1.0 copy-start.3
  28.9 1.0 copy-start.4
  29.9 0.7 copy-start.5
  35.1 77.9 %reduce-scatter.2.cloned.1.call-start = ((), (), s32[]{:S(2)}) async-start(), calls=%async_computation.3 | async-start | bytes 1966080 | tf_op jit(solution)/shard_map/reduce_scatter | solution.py:119
  67.9 1.9 %copy-start = (bf16[1024,1536]{1,0:T(8,128)(2,1)S(1)}, bf16[1024,1536]{1,0:T(8,128)(2,1)}, u32[]{:S(2)}) copy-start(bf16[1024,1536]{1,0:T(8,128)(2,1)} %all-gather.3.cloned.1.call-done.att_ref) | copy-start | bytes 9437188
Sparse Core Ops, SparseCore 0:
  35.2 32.6 all-gather.2
  77.7 35.2 reduce-scatter.1

commit v2 on v1

v2 whole, which is shorter than its diff:
```python
import math

import jax
import jax.numpy as jnp
from jax import lax
from jax.experimental import pallas as pl
from jax.experimental.pallas import tpu as pltpu
from jax.sharding import PartitionSpec as P

BLOCK = 128
HALO = 64
NEGATIVE_FILL = -1e30
LAST = (((1,), (1,)), ((), ()))
BF16 = jnp.bfloat16
PARAMS = pltpu.CompilerParams(vmem_limit_bytes=40 << 20)
WHOLE = pltpu.CompilerParams(vmem_limit_bytes=62 << 20)


def vmem():
    return pl.BlockSpec(memory_space=pltpu.VMEM)


def smem():
    return pl.BlockSpec(memory_space=pltpu.SMEM)


def hbm():
    return pl.BlockSpec(memory_space=pltpu.HBM)


def shaped(*shape):
    return jax.ShapeDtypeStruct(shape, BF16)


def pick_kernel(picks_ref, keys_ref, values_ref, summary_ref, halo_ref, rows_ref, sems):
    per_block = picks_ref.shape[1]
    copies = [
        pltpu.make_async_copy(ref, rows_ref.at[part], sems.at[part])
        for part, ref in enumerate((keys_ref, values_ref))
    ]
    for copy in copies:
        copy.start()
    row = lax.broadcasted_iota(jnp.int32, (per_block, BLOCK), 0)
    wanted = jnp.zeros((per_block, BLOCK), jnp.int32)
    for r in range(per_block):
        wanted = jnp.where(row == r, picks_ref[0, r], wanted)
    column = lax.broadcasted_iota(jnp.int32, (per_block, BLOCK), 1)
    chosen = jnp.where(column == wanted, 1.0, 0.0).astype(BF16)
    for part, copy in enumerate(copies):
        copy.wait()
        taken = jnp.dot(chosen, rows_ref[part], preferred_element_type=jnp.float32)
        summary_ref[part] = taken.astype(BF16)
        halo_ref[part] = rows_ref[part, BLOCK - HALO :, :]


def attend_kernel(band_ref, q_hbm, k_hbm, v_hbm, halo_ref, far_ref, out_ref, q_ref, k_ref, v_ref, sems):
    size = BLOCK
    feat = q_ref.shape[1]
    heads = feat // size
    sources, unused, per_block, unused = far_ref.shape
    far_rows = sources * per_block
    some = 3 if heads % 3 == 0 else 1
    span = some * size
    copies = []
    for g in range(heads // some):
        cols = slice(g * span, (g + 1) * span)
        copies.append(
            [
                pltpu.make_async_copy(ref.at[:, cols], into.at[:, cols], sems.at[g, part])
                for part, (ref, into) in enumerate(((q_hbm, q_ref), (k_hbm, k_ref), (v_hbm, v_ref)))
            ]
        )
        for copy in copies[-1]:
            copy.start()
    place = lax.axis_index("seq")
    scale = 1.0 / math.sqrt(size)
    own_q = lax.broadcasted_iota(jnp.int32, (BLOCK, BLOCK), 0)
    own_k = lax.broadcasted_iota(jnp.int32, (BLOCK, BLOCK), 1)
    own_gap = own_q - own_k
    back_q = lax.broadcasted_iota(jnp.int32, (BLOCK, HALO), 0)
    back_k = lax.broadcasted_iota(jnp.int32, (BLOCK, HALO), 1) - HALO
    back_gap = jnp.where(place > 0, back_q - back_k, BLOCK * 4)
    far_owner = lax.broadcasted_iota(jnp.int32, (BLOCK, far_rows), 1) // per_block
    far_ok = far_owner < place
    for h in range(heads):
        if h % some == 0:
            for copy in copies[h // some]:
                copy.wait()
        cols = slice(h * size, (h + 1) * size)
        query = q_ref[:, cols]
        all_keys = jnp.concatenate(
            [k_ref[:, cols], far_ref[:, 0, :, cols].reshape(far_rows, size), halo_ref[0, :, cols]], 0
        )
        all_values = jnp.concatenate(
            [v_ref[:, cols], far_ref[:, 1, :, cols].reshape(far_rows, size), halo_ref[1, :, cols]], 0
        )
        scores = lax.dot_general(query, all_keys, LAST, preferred_element_type=jnp.float32) * scale
        width = band_ref[h]
        own_ok = (own_gap >= 0) & (own_gap < width)
        back_ok = back_gap < width
        valid = jnp.concatenate([own_ok, far_ok, back_ok], 1)
        scores = jnp.where(valid, scores, NEGATIVE_FILL)
        largest = jnp.max(scores, axis=1, keepdims=True)
        weights = jnp.where(valid, jnp.exp(scores - largest), 0.0)
        total = jnp.sum(weights, axis=1, keepdims=True)
        mixed = jnp.dot(weights.astype(BF16), all_values, preferred_element_type=jnp.float32)
        out_ref[:, cols] = (mixed / total).astype(BF16)


def project_kernel(att_ref, mine_ref, other_ref, *refs):
    send_ref, keep_ref, acc_ref = refs[-3:]
    wide = mine_ref.shape[0]
    unused, half, rows, unused = keep_ref.shape
    core = lax.rem(lax.axis_index("seq"), 2)
    side = lax.rem(lax.axis_index("head"), 2)
    step = acc_ref.shape[-1]
    for which, ref in ((core, mine_ref), (1 - core, other_ref)):

        @pl.loop(0, wide // step)
        def _(n):
            tile = ref[pl.ds(n * step, step), :]
            found = lax.dot_general(att_ref[...], tile, LAST, preferred_element_type=jnp.float32)
            acc_ref[...] = found.reshape(half, 2, rows, step)
            cols = slice(None) if step == wide else pl.ds(pl.multiple_of(n * step, step), step)
            keep_ref[which, :, :, cols] = acc_ref[:, side].astype(BF16)
            send_ref[which, :, :, cols] = acc_ref[:, 1 - side].astype(BF16)


def split_kernel(came_ref, keep_ref, away_ref, stay_ref):
    side = lax.axis_index("head") // 2
    for ref, which in ((away_ref, 1 - side), (stay_ref, side)):
        total = came_ref[:, which].astype(jnp.float32) + keep_ref[:, which].astype(jnp.float32)
        ref[...] = total.astype(BF16)


def join_kernel(*refs):
    out_ref = refs[-1]
    wide = refs[0].shape[-1]
    chip = lax.axis_index("seq") // 2
    for k in range(len(refs) // 2):
        total = refs[2 * k][...].astype(jnp.float32) + refs[2 * k + 1][...].astype(jnp.float32)
        total = total.astype(BF16)
        if len(out_ref.shape) == 4:
            out_ref[chip ^ k] = total
            continue
        for c in range(2):
            start = pl.multiple_of((chip ^ k) * (2 * wide), 128)
            out_ref[:, pl.ds(start + c * wide, wide)] = total[c]


def local(queries, keys, values, band, picks, w_out):
    heads = band.shape[0]
    tok_rows, feat = queries.shape
    per_block = picks.shape[1]
    seq = lax.axis_size("seq")
    groups = lax.axis_size("head")
    wide = w_out.shape[0]
    rows = tok_rows // groups
    chips = seq // 2
    half = groups // 2

    def swap(value, k, z):
        if k == 0:
            return lax.ppermute(value, "head", [(i, i ^ z) for i in range(groups)])
        if z == 0:
            return lax.ppermute(value, "seq", [(i, i ^ k) for i in range(seq)])
        pairs = [
            (s * groups + h, (s ^ k) * groups + (h ^ z)) for s in range(seq) for h in range(groups)
        ]
        return lax.ppermute(value, ("seq", "head"), pairs)

    summary, halo = pl.pallas_call(
        pick_kernel,
        out_shape=(shaped(2, per_block, feat), shaped(2, HALO, feat)),
        in_specs=[smem(), hbm(), hbm()],
        out_specs=(vmem(), vmem()),
        scratch_shapes=[pltpu.VMEM((2, tok_rows, feat), BF16), pltpu.SemaphoreType.DMA((2,))],
        compiler_params=WHOLE,
    )(picks, keys, values)
    halo = lax.ppermute(halo, "seq", [(i, i + 1) for i in range(seq - 1)])
    other_w = swap(w_out, 1, 0)
    far = lax.all_gather(summary, "seq", axis=0, tiled=False)
    attention = pl.pallas_call(
        attend_kernel,
        out_shape=shaped(tok_rows, feat),
        in_specs=[smem(), hbm(), hbm(), hbm(), vmem(), vmem()],
        out_specs=vmem(),
        scratch_shapes=[pltpu.VMEM((tok_rows, feat), BF16)] * 3 + [pltpu.SemaphoreType.DMA((heads, 3))],
        compiler_params=WHOLE,
    )(band, queries, keys, values, halo, far)
    step = 256 if wide % 256 == 0 else wide
    pieces = []
    before = ()
    for k in range(chips):
        part = swap(attention, 2 * k, 0) if k else attention
        send, keep = pl.pallas_call(
            project_kernel,
            out_shape=(shaped(2, half, rows, wide), shaped(2, half, rows, wide)),
            in_specs=[vmem()] * 3 + [pl.BlockSpec(memory_space=pl.ANY)] * len(before),
            out_specs=(vmem(), vmem()),
            scratch_shapes=[pltpu.VMEM((half, 2, rows, step), jnp.float32)],
            compiler_params=PARAMS,
        )(part, w_out, other_w, *before)
        before = (send,)
        came = swap(send, 0, 1)
        away, stay = pl.pallas_call(
            split_kernel,
            out_shape=(shaped(2, rows, wide), shaped(2, rows, wide)),
            in_specs=[vmem()] * 2,
            out_specs=(vmem(), vmem()),
        )(came, keep)
        pieces.append(swap(away, 2 * k, 2))
        pieces.append(swap(stay, 2 * k, 0) if k else stay)
    flat = wide % 128 == 0
    joined = pl.pallas_call(
        join_kernel,
        out_shape=shaped(rows, seq * wide) if flat else shaped(chips, 2, rows, wide),
        in_specs=[vmem()] * len(pieces),
        out_specs=vmem(),
        compiler_params=PARAMS,
    )(*pieces)
    return joined if flat else joined.transpose(2, 0, 1, 3).reshape(rows, seq * wide)


def solution(mesh):
    placed = (
        P("seq", "head"),
        P("seq", "head"),
        P("seq", "head"),
        P("head"),
        P("seq", None),
        P("seq", "head"),
    )
    return jax.shard_map(
        local, mesh=mesh, in_specs=placed, out_specs=P(("seq", "head"), None), check_vma=False
    )
```

time: 133 us -> 89.3 us (0.67)
  waiting for transfers between devices: 68.2 us -> 6.86 us
  starting transfers between devices: 2.41 us -> 22.4 us
  Pallas kernels: 14.4 us -> 34.2 us
  between operations: 13.4 us -> 0.12 us
  blocking collectives: 27.8 us -> 16.5 us
  local copies, waits for them, and re-layouts: 6.31 us -> 8.67 us
    reduce_scatter x1 -> x0, waiting for transfers between devices: 35.4 us -> none  [local(): lax.psum_scatter(partial_value.reshape(groups * seq * rows, wide), 'head'...]
    all_gather x1 -> x0, waiting for transfers between devices: 32.7 us -> none  [local(): gathered = lax.all_gather(attention, 'seq', axis=0, tiled=True)]
    ppermute x0 -> x15, starting transfers between devices: none -> 20.4 us  [the longest x5 7.83 us: swap(): return lax.ppermute(value, 'head', [(i, i ^ z) for i in range(groups)])]
    pallas_call x3 -> x11, Pallas kernels: 14.4 us -> 34.2 us  [the longest x4 16.8 us: local(): pl.pallas_call(project_kernel, out_shape=(shaped(2, half, rows, wide), sh...]
    all_to_all x1 -> x0, blocking collectives: 12 us -> none  [local(): lax.all_to_all(summed.reshape(seq, rows, wide), 'seq', 0, 0, tiled=False)]
    ppermute x0 -> x15, waiting for transfers between devices: none -> 6.85 us  [the longest x3 4.92 us: swap(): return lax.ppermute(value, ('seq', 'head'), pairs)]
    unnamed x12 -> x26, local copies, waits for them, and re-layouts: 5.53 us -> 8.67 us
  transfers between devices with their start and end apart: 3 -> 16, of which waited for: 2 -> 4; matrix products, arithmetic and copies ran while one was open for 0% -> 0% of each run, Pallas kernels for 0% -> 38%
where the time goes in v2:
time: 89.3 us; the launch traced here: 88.7 us
  Pallas kernels  34.2 us (38%)
  starting transfers between devices  22.4 us (25%)
  blocking collectives  16.5 us (18%)
  local copies, waits for them, and re-layouts  8.67 us (10%)
  waiting for transfers between devices  6.86 us (8%)
    pallas_call x4, Pallas kernels, local(): pl.pallas_call(project_kernel, out_shape=(shaped(2, half, rows, wide), sh...  16.8 us
    all_gather x1, blocking collectives, local(): far = lax.all_gather(summary, 'seq', axis=0, tiled=False)  16.5 us
    unnamed x26, local copies, waits for them, and re-layouts  8.67 us
    ppermute x5, starting transfers between devices, swap(): return lax.ppermute(value, 'head', [(i, i ^ z) for i in range(groups)])  7.83 us
    pallas_call x1, Pallas kernels, local(): pl.pallas_call(attend_kernel, out_shape=shaped(tok_rows, feat), in_specs=...  7.04 us
    pallas_call x4, Pallas kernels, local(): pl.pallas_call(split_kernel, out_shape=(shaped(2, rows, wide), shaped(2,...  6.9 us
    ppermute x3, starting transfers between devices, swap(): return lax.ppermute(value, ('seq', 'head'), pairs)  6.38 us
    ppermute x7, starting transfers between devices, swap(): return lax.ppermute(value, 'seq', [(i, i ^ k) for i in range(seq)])  6.19 us
  transfers between devices with their start and end apart: 16, of which 4 were waited for; matrix products, arithmetic and copies ran while one was open for 0% of the time, Pallas kernels for 38%

profile of v2, /device:TPU:0, one launch (start us, length us, event | category | flops | bytes accessed | tf_op | source)
XLA Modules:
  0.0 88.7 jit_solution(1446680169020616601)
XLA Ops:
  0.0 0.5 collective-permute-start.1
  0.5 2.7 %shard_map.64 = (bf16[2,16,1536]{2,1,0:T(8,128)(2,1)}, bf16[2,64,1536]{2,1,0:T(8,128)(2,1)}) custom-call(s32[1,16]{1,0:T(1,128)} %picks_ref.1, bf16[128,1536]{1,0:T(8,128)(2,1)} %k_hbm.1, bf16[128,1536]{1,0:T(8,128)(2,1)} %v_hbm.1), custom_call_target="tpu_custom_call" | custom-call | tf_op jit(solution)/shard_map/pallas_call | solution.py:172
  3.1 2.0 %collective-permute-start = (bf16[2,64,1536]{2,1,0:T(8,128)(2,1)}, bf16[2,64,1536]{2,1,0:T(8,128)(2,1)S(1)}, u32[]{:S(2)}, u32[]{:S(2)}) collective-permute-start(bf16[2,64,1536]{2,1,0:T(8,128)(2,1)} %get-tuple-element.23), channel_id=1, source_target_pairs={{0,4},{4,8},{8,12},{12,16},{16,20},{20,24},{24,28},{1,5},{5,9},{9,... | collective-permute-start | bytes 1179656 | tf_op jit(solution)/shard_map/ppermute | solution.py:180
  5.1 16.5 %all-gather = bf16[16,16,1536]{2,1,0:T(8,128)(2,1)} all-gather(bf16[2,16,1536]{2,1,0:T(8,128)(2,1)} %get-tuple-element.24), channel_id=2, replica_groups=mesh['seq'=8,'head'=4] {'seq'}, dimensions={0}, use_global_device_ids=true | all-gather | bytes 884736 | tf_op jit(solution)/shard_map/all_gather | solution.py:182
  21.6 0.0 collective-permute-done.halo_ref
  21.6 0.7 copy-done.8
  22.4 7.0 %shard_map.65.att_ref = bf16[128,1536]{1,0:T(8,128)(2,1)} custom-call(s32[12]{0:T(128)} %band_ref.1, bf16[128,1536]{1,0:T(8,128)(2,1)} %q_hbm.1, bf16[128,1536]{1,0:T(8,128)(2,1)} %k_hbm.1, bf16[128,1536]{1,0:T(8,128)(2,1)} %v_hbm.1, bf16[2,64,1536]{2,1,0:T(8,128)(2,1)} %copy-done.8, bf16[8,2,16,1536]{3,2,1,0:T(8,128)(2,1)} %bitcast.1), custom_call_target="tpu_custom_call" | custom-call | tf_op jit(solution)/shard_map/pallas_call | solution.py:183
  29.4 0.1 collective-permute-start.4
  29.5 2.0 %collective-permute-start.8 = (bf16[128,1536]{1,0:T(8,128)(2,1)}, bf16[128,1536]{1,0:T(8,128)(2,1)S(1)}, u32[]{:S(2)}, u32[]{:S(2)}) collective-permute-start(bf16[128,1536]{1,0:T(8,128)(2,1)} %shard_map.65.att_ref), channel_id=1, source_target_pairs={{0,16},{4,20},{8,24},{12,28},{16,0},{20,4},{24,8},{28,12},{1,17},{... | collective-permute-start | bytes 1179656 | tf_op jit(solution)/shard_map/ppermute | solution.py:166
  31.5 1.5 %collective-permute-start.12 = (bf16[128,1536]{1,0:T(8,128)(2,1)}, bf16[128,1536]{1,0:T(8,128)(2,1)S(1)}, u32[]{:S(2)}, u32[]{:S(2)}) collective-permute-start(bf16[128,1536]{1,0:T(8,128)(2,1)} %shard_map.65.att_ref), channel_id=1, source_target_pairs={{0,24},{4,28},{8,16},{12,20},{16,8},{20,12},{24,0},{28,4},{1,25},{... | collective-permute-start | bytes 1179656 | tf_op jit(solution)/shard_map/ppermute | solution.py:166
  33.0 0.0 collective-permute-done.1.other_ref
  33.0 1.7 %copy-done = bf16[768,1536]{1,0:T(8,128)(2,1)S(1)} copy-done((bf16[768,1536]{1,0:T(8,128)(2,1)S(1)}, bf16[768,1536]{1,0:T(8,128)(2,1)}, u32[]{:S(2)}) %copy-start) | copy-done | bytes 2359320
  34.6 1.0 %copy-done.2 = bf16[128,1536]{1,0:T(8,128)(2,1)S(1)} copy-done((bf16[128,1536]{1,0:T(8,128)(2,1)S(1)}, bf16[128,1536]{1,0:T(8,128)(2,1)}, u32[]{:S(2)}) %copy-start.2) | copy-done | bytes 393240
  35.6 4.3 %shard_map.66 = (bf16[2,2,32,768]{3,2,1,0:T(8,128)(2,1)S(1)}, bf16[2,2,32,768]{3,2,1,0:T(8,128)(2,1)S(1)}) custom-call(bf16[128,1536]{1,0:T(8,128)(2,1)S(1)} %copy-done.2, bf16[768,1536]{1,0:T(8,128)(2,1)S(1)} %copy-done, bf16[768,1536]{1,0:T(8,128)(2,1)} %collective-permute-done.1.other_ref), custom_call_target="tpu_custom_call" | custom-call | tf_op jit(solution)/shard_map/pallas_call | solution.py:196
  40.0 1.6 %collective-permute-start.2 = (bf16[2,2,32,768]{3,2,1,0:T(8,128)(2,1)S(1)}, bf16[2,2,32,768]{3,2,1,0:T(8,128)(2,1)S(1)}, u32[]{:S(2)}, u32[]{:S(2)}) collective-permute-start(bf16[2,2,32,768]{3,2,1,0:T(8,128)(2,1)S(1)} %get-tuple-element.25.refs_0_), channel_id=1, source_target_pairs={{0,1},{1,0},{2,3},{3,2},{4,5},{5,4},{6,7},{7,6},{8,9},{9,8},{10,11... | collective-permute-start | bytes 589832 | tf_op jit(solution)/shard_map/ppermute | solution.py:164
  41.6 0.0 collective-permute-done.4.att_ref
  41.6 4.2 %shard_map.68 = (bf16[2,2,32,768]{3,2,1,0:T(8,128)(2,1)S(1)}, bf16[2,2,32,768]{3,2,1,0:T(8,128)(2,1)S(1)}) custom-call(bf16[128,1536]{1,0:T(8,128)(2,1)S(1)} %collective-permute-done.4.att_ref, bf16[768,1536]{1,0:T(8,128)(2,1)S(1)} %copy-done.1, bf16[768,1536]{1,0:T(8,128)(2,1)} %collective-permute-done.1.other_ref, ...), custom_call_target="tpu_custom_call" | custom-call | tf_op jit(solution)/shard_map/pallas_call | solution.py:196
  45.8 0.7 copy-done.5
  46.5 1.6 %collective-permute-start.5 = (bf16[2,2,32,768]{3,2,1,0:T(8,128)(2,1)S(1)}, bf16[2,2,32,768]{3,2,1,0:T(8,128)(2,1)S(1)}, u32[]{:S(2)}, u32[]{:S(2)}) collective-permute-start(bf16[2,2,32,768]{3,2,1,0:T(8,128)(2,1)S(1)} %get-tuple-element.29.refs_0_), channel_id=1, source_target_pairs={{0,1},{1,0},{2,3},{3,2},{4,5},{5,4},{6,7},{7,6},{8,9},{9,8},{10,11... | collective-permute-start | bytes 589832 | tf_op jit(solution)/shard_map/ppermute | solution.py:164
  48.1 1.5 %collective-permute-done.8.att_ref = bf16[128,1536]{1,0:T(8,128)(2,1)S(1)} collective-permute-done((bf16[128,1536]{1,0:T(8,128)(2,1)}, bf16[128,1536]{1,0:T(8,128)(2,1)S(1)}, u32[]{:S(2)}, u32[]{:S(2)}) %collective-permute-start.8) | collective-permute-done | bytes 393248 | tf_op jit(solution)/shard_map/ppermute | solution.py:166
  49.6 4.2 %shard_map.70 = (bf16[2,2,32,768]{3,2,1,0:T(8,128)(2,1)S(1)}, bf16[2,2,32,768]{3,2,1,0:T(8,128)(2,1)S(1)}) custom-call(bf16[128,1536]{1,0:T(8,128)(2,1)S(1)} %collective-permute-done.8.att_ref, bf16[768,1536]{1,0:T(8,128)(2,1)S(1)} %copy-done.1, bf16[768,1536]{1,0:T(8,128)(2,1)} %collective-permute-done.1.other_ref, ...), custom_call_target="tpu_custom_call" | custom-call | tf_op jit(solution)/shard_map/pallas_call | solution.py:196
  53.7 0.7 copy-done.4
  54.4 1.6 %collective-permute-start.9 = (bf16[2,2,32,768]{3,2,1,0:T(8,128)(2,1)S(1)}, bf16[2,2,32,768]{3,2,1,0:T(8,128)(2,1)S(1)}, u32[]{:S(2)}, u32[]{:S(2)}) collective-permute-start(bf16[2,2,32,768]{3,2,1,0:T(8,128)(2,1)S(1)} %get-tuple-element.33.refs_0_), channel_id=1, source_target_pairs={{0,1},{1,0},{2,3},{3,2},{4,5},{5,4},{6,7},{7,6},{8,9},{9,8},{10,11... | collective-permute-start | bytes 589832 | tf_op jit(solution)/shard_map/ppermute | solution.py:164
  56.0 0.0 collective-permute-done.12.att_ref
  56.0 4.2 %shard_map.72 = (bf16[2,2,32,768]{3,2,1,0:T(8,128)(2,1)S(1)}, bf16[2,2,32,768]{3,2,1,0:T(8,128)(2,1)S(1)}) custom-call(bf16[128,1536]{1,0:T(8,128)(2,1)S(1)} %collective-permute-done.12.att_ref, bf16[768,1536]{1,0:T(8,128)(2,1)S(1)} %copy-done.1, bf16[768,1536]{1,0:T(8,128)(2,1)} %collective-permute-done.1.other_ref, ...), custom_call_target="tpu_custom_call" | custom-call | tf_op jit(solution)/shard_map/pallas_call | solution.py:196
  60.2 0.7 copy-done.3
  60.8 0.4 collective-permute-start.13
  61.3 0.0 collective-permute-done.2.came_ref
  61.3 0.7 copy-done.12
  62.0 1.7 %shard_map.67 = (bf16[2,32,768]{2,1,0:T(8,128)(2,1)}, bf16[2,32,768]{2,1,0:T(8,128)(2,1)}) custom-call(bf16[2,2,32,768]{3,2,1,0:T(8,128)(2,1)} %copy-done.12, bf16[2,2,32,768]{3,2,1,0:T(8,128)(2,1)} %copy-done.6), custom_call_target="tpu_custom_call" | custom-call | tf_op jit(solution)/shard_map/pallas_call | solution.py:206
  63.7 2.6 %collective-permute-start.3 = (bf16[2,32,768]{2,1,0:T(8,128)(2,1)}, bf16[2,32,768]{2,1,0:T(8,128)(2,1)S(1)}, u32[]{:S(2)}, u32[]{:S(2)}) collective-permute-start(bf16[2,32,768]{2,1,0:T(8,128)(2,1)} %get-tuple-element.27), channel_id=1, source_target_pairs={{0,2},{1,3},{2,0},{3,1},{4,6},{5,7},{6,4},{7,5},{8,10},{9,11},{10,... | collective-permute-start | bytes 294920 | tf_op jit(solution)/shard_map/ppermute | solution.py:164
  66.3 0.7 copy-done.11
  67.0 1.7 %shard_map.69 = (bf16[2,32,768]{2,1,0:T(8,128)(2,1)}, bf16[2,32,768]{2,1,0:T(8,128)(2,1)}) custom-call(bf16[2,2,32,768]{3,2,1,0:T(8,128)(2,1)} %copy-done.11, bf16[2,2,32,768]{3,2,1,0:T(8,128)(2,1)} %copy-done.5), custom_call_target="tpu_custom_call" | custom-call | tf_op jit(solution)/shard_map/pallas_call | solution.py:206
  68.7 1.4 %collective-permute-start.6 = (bf16[2,32,768]{2,1,0:T(8,128)(2,1)}, bf16[2,32,768]{2,1,0:T(8,128)(2,1)S(1)}, u32[]{:S(2)}, u32[]{:S(2)}) collective-permute-start(bf16[2,32,768]{2,1,0:T(8,128)(2,1)} %get-tuple-element.31), channel_id=1, source_target_pairs={{0,10},{1,11},{2,8},{3,9},{4,14},{5,15},{6,12},{7,13},{8,2},{9,3},... | collective-permute-start | bytes 294920 | tf_op jit(solution)/shard_map/ppermute | solution.py:170
  70.1 0.4 collective-permute-start.7
  70.5 0.7 copy-done.10
  71.2 1.7 %shard_map.71 = (bf16[2,32,768]{2,1,0:T(8,128)(2,1)}, bf16[2,32,768]{2,1,0:T(8,128)(2,1)}) custom-call(bf16[2,2,32,768]{3,2,1,0:T(8,128)(2,1)} %copy-done.10, bf16[2,2,32,768]{3,2,1,0:T(8,128)(2,1)} %copy-done.4), custom_call_target="tpu_custom_call" | custom-call | tf_op jit(solution)/shard_map/pallas_call | solution.py:206
  72.9 3.7 %collective-permute-start.10 = (bf16[2,32,768]{2,1,0:T(8,128)(2,1)}, bf16[2,32,768]{2,1,0:T(8,128)(2,1)S(1)}, u32[]{:S(2)}, u32[]{:S(2)}) collective-permute-start(bf16[2,32,768]{2,1,0:T(8,128)(2,1)} %get-tuple-element.35), channel_id=1, source_target_pairs={{0,18},{1,19},{2,16},{3,17},{4,22},{5,23},{6,20},{7,21},{8,26},{9,... | collective-permute-start | bytes 294920 | tf_op jit(solution)/shard_map/ppermute | solution.py:170
  76.6 0.4 collective-permute-start.11
  76.9 0.3 copy-done.9
  77.2 1.7 %shard_map.73 = (bf16[2,32,768]{2,1,0:T(8,128)(2,1)}, bf16[2,32,768]{2,1,0:T(8,128)(2,1)}) custom-call(bf16[2,2,32,768]{3,2,1,0:T(8,128)(2,1)} %copy-done.9, bf16[2,2,32,768]{3,2,1,0:T(8,128)(2,1)} %copy-done.3), custom_call_target="tpu_custom_call" | custom-call | tf_op jit(solution)/shard_map/pallas_call | solution.py:206
  79.0 1.2 %collective-permute-start.14 = (bf16[2,32,768]{2,1,0:T(8,128)(2,1)}, bf16[2,32,768]{2,1,0:T(8,128)(2,1)S(1)}, u32[]{:S(2)}, u32[]{:S(2)}) collective-permute-start(bf16[2,32,768]{2,1,0:T(8,128)(2,1)} %get-tuple-element.39), channel_id=1, source_target_pairs={{0,26},{1,27},{2,24},{3,25},{4,30},{5,31},{6,28},{7,29},{8,18},{9,... | collective-permute-start | bytes 294920 | tf_op jit(solution)/shard_map/ppermute | solution.py:170
  80.2 1.5 %collective-permute-start.15 = (bf16[2,32,768]{2,1,0:T(8,128)(2,1)}, bf16[2,32,768]{2,1,0:T(8,128)(2,1)S(1)}, u32[]{:S(2)}, u32[]{:S(2)}) collective-permute-start(bf16[2,32,768]{2,1,0:T(8,128)(2,1)} %get-tuple-element.40), channel_id=1, source_target_pairs={{0,24},{4,28},{8,16},{12,20},{16,8},{20,12},{24,0},{28,4},{1,25},{... | collective-permute-start | bytes 294920 | tf_op jit(solution)/shard_map/ppermute | solution.py:166
  81.7 0.6 collective-permute-done.10.refs_4_
  82.3 4.3 %collective-permute-done.14.refs_6_ = bf16[2,32,768]{2,1,0:T(8,128)(2,1)S(1)} collective-permute-done((bf16[2,32,768]{2,1,0:T(8,128)(2,1)}, bf16[2,32,768]{2,1,0:T(8,128)(2,1)S(1)}, u32[]{:S(2)}, u32[]{:S(2)}) %collective-permute-start.14) | collective-permute-done | bytes 98336 | tf_op jit(solution)/shard_map/ppermute | solution.py:170
  86.6 0.4 collective-permute-done.15.refs_7_
  87.0 0.9 %copy-done.7 = bf16[2,32,768]{2,1,0:T(8,128)(2,1)S(1)} copy-done((bf16[2,32,768]{2,1,0:T(8,128)(2,1)S(1)}, bf16[2,32,768]{2,1,0:T(8,128)(2,1)}, u32[]{:S(2)}) %copy-start.7) | copy-done | bytes 98328
  87.9 0.8 shard_map.74
  (22 shorter events, 0.0 us)
Async XLA Ops:
  0.0 33.0 %collective-permute-start.1 = (bf16[768,1536]{1,0:T(8,128)(2,1)}, bf16[768,1536]{1,0:T(8,128)(2,1)}, u32[]{:S(2)}, u32[]{:S(2)}) collective-permute-start(bf16[768,1536]{1,0:T(8,128)(2,1)} %mine_ref.7), channel_id=1, source_target_pairs={{0,4},{4,0},{8,12},{12,8},{16,20},{20,16},{24,28},{28,24},{1,5},{5... | collective-permute-start | bytes 7077896 | tf_op jit(solution)/shard_map/ppermute | solution.py:166
  3.1 18.5 %collective-permute-start = (bf16[2,64,1536]{2,1,0:T(8,128)(2,1)}, bf16[2,64,1536]{2,1,0:T(8,128)(2,1)S(1)}, u32[]{:S(2)}, u32[]{:S(2)}) collective-permute-start(bf16[2,64,1536]{2,1,0:T(8,128)(2,1)} %get-tuple-element.23), channel_id=1, source_target_pairs={{0,4},{4,8},{8,12},{12,16},{16,20},{20,24},{24,28},{1,5},{5,9},{9,... | collective-permute-start | bytes 1179656 | tf_op jit(solution)/shard_map/ppermute | solution.py:180
  21.6 0.7 copy-start.8
  29.4 12.2 %collective-permute-start.4 = (bf16[128,1536]{1,0:T(8,128)(2,1)}, bf16[128,1536]{1,0:T(8,128)(2,1)S(1)}, u32[]{:S(2)}, u32[]{:S(2)}) collective-permute-start(bf16[128,1536]{1,0:T(8,128)(2,1)} %shard_map.65.att_ref), channel_id=1, source_target_pairs={{0,8},{4,12},{8,0},{12,4},{16,24},{20,28},{24,16},{28,20},{1,9},{5... | collective-permute-start | bytes 1179656 | tf_op jit(solution)/shard_map/ppermute | solution.py:166
  29.5 20.1 %collective-permute-start.8 = (bf16[128,1536]{1,0:T(8,128)(2,1)}, bf16[128,1536]{1,0:T(8,128)(2,1)S(1)}, u32[]{:S(2)}, u32[]{:S(2)}) collective-permute-start(bf16[128,1536]{1,0:T(8,128)(2,1)} %shard_map.65.att_ref), channel_id=1, source_target_pairs={{0,16},{4,20},{8,24},{12,28},{16,0},{20,4},{24,8},{28,12},{1,17},{... | collective-permute-start | bytes 1179656 | tf_op jit(solution)/shard_map/ppermute | solution.py:166
  31.5 24.5 %collective-permute-start.12 = (bf16[128,1536]{1,0:T(8,128)(2,1)}, bf16[128,1536]{1,0:T(8,128)(2,1)S(1)}, u32[]{:S(2)}, u32[]{:S(2)}) collective-permute-start(bf16[128,1536]{1,0:T(8,128)(2,1)} %shard_map.65.att_ref), channel_id=1, source_target_pairs={{0,24},{4,28},{8,16},{12,20},{16,8},{20,12},{24,0},{28,4},{1,25},{... | collective-permute-start | bytes 1179656 | tf_op jit(solution)/shard_map/ppermute | solution.py:166
  33.0 1.7 %copy-start = (bf16[768,1536]{1,0:T(8,128)(2,1)S(1)}, bf16[768,1536]{1,0:T(8,128)(2,1)}, u32[]{:S(2)}) copy-start(bf16[768,1536]{1,0:T(8,128)(2,1)} %mine_ref.7) | copy-start | bytes 7077892
  34.6 1.0 %copy-start.2 = (bf16[128,1536]{1,0:T(8,128)(2,1)S(1)}, bf16[128,1536]{1,0:T(8,128)(2,1)}, u32[]{:S(2)}) copy-start(bf16[128,1536]{1,0:T(8,128)(2,1)} %shard_map.65.att_ref) | copy-start | bytes 1179652
  35.6 6.0 %copy-start.1 = (bf16[768,1536]{1,0:T(8,128)(2,1)S(1)}, bf16[768,1536]{1,0:T(8,128)(2,1)}, u32[]{:S(2)}) copy-start(bf16[768,1536]{1,0:T(8,128)(2,1)} %mine_ref.7) | copy-start | bytes 7077892
  39.9 5.8 %copy-start.6 = (bf16[2,2,32,768]{3,2,1,0:T(8,128)(2,1)}, bf16[2,2,32,768]{3,2,1,0:T(8,128)(2,1)S(1)}, u32[]{:S(2)}) copy-start(bf16[2,2,32,768]{3,2,1,0:T(8,128)(2,1)S(1)} %get-tuple-element.26.keep_ref) | copy-start | bytes 589828
  40.0 21.3 %collective-permute-start.2 = (bf16[2,2,32,768]{3,2,1,0:T(8,128)(2,1)S(1)}, bf16[2,2,32,768]{3,2,1,0:T(8,128)(2,1)S(1)}, u32[]{:S(2)}, u32[]{:S(2)}) collective-permute-start(bf16[2,2,32,768]{3,2,1,0:T(8,128)(2,1)S(1)} %get-tuple-element.25.refs_0_), channel_id=1, source_target_pairs={{0,1},{1,0},{2,3},{3,2},{4,5},{5,4},{6,7},{7,6},{8,9},{9,8},{10,11... | collective-permute-start | bytes 589832 | tf_op jit(solution)/shard_map/ppermute | solution.py:164
  45.8 0.7 copy-start.5
  46.5 19.8 %collective-permute-start.5 = (bf16[2,2,32,768]{3,2,1,0:T(8,128)(2,1)S(1)}, bf16[2,2,32,768]{3,2,1,0:T(8,128)(2,1)S(1)}, u32[]{:S(2)}, u32[]{:S(2)}) collective-permute-start(bf16[2,2,32,768]{3,2,1,0:T(8,128)(2,1)S(1)} %get-tuple-element.29.refs_0_), channel_id=1, source_target_pairs={{0,1},{1,0},{2,3},{3,2},{4,5},{5,4},{6,7},{7,6},{8,9},{9,8},{10,11... | collective-permute-start | bytes 589832 | tf_op jit(solution)/shard_map/ppermute | solution.py:164
  53.7 0.7 copy-start.4
  54.4 16.1 %collective-permute-start.9 = (bf16[2,2,32,768]{3,2,1,0:T(8,128)(2,1)S(1)}, bf16[2,2,32,768]{3,2,1,0:T(8,128)(2,1)S(1)}, u32[]{:S(2)}, u32[]{:S(2)}) collective-permute-start(bf16[2,2,32,768]{3,2,1,0:T(8,128)(2,1)S(1)} %get-tuple-element.33.refs_0_), channel_id=1, source_target_pairs={{0,1},{1,0},{2,3},{3,2},{4,5},{5,4},{6,7},{7,6},{8,9},{9,8},{10,11... | collective-permute-start | bytes 589832 | tf_op jit(solution)/shard_map/ppermute | solution.py:164
  60.2 0.7 copy-start.3
  60.8 15.7 %collective-permute-start.13 = (bf16[2,2,32,768]{3,2,1,0:T(8,128)(2,1)S(1)}, bf16[2,2,32,768]{3,2,1,0:T(8,128)(2,1)S(1)}, u32[]{:S(2)}, u32[]{:S(2)}) collective-permute-start(bf16[2,2,32,768]{3,2,1,0:T(8,128)(2,1)S(1)} %get-tuple-element.37), channel_id=1, source_target_pairs={{0,1},{1,0},{2,3},{3,2},{4,5},{5,4},{6,7},{7,6},{8,9},{9,8},{10,11... | collective-permute-start | bytes 589832 | tf_op jit(solution)/shard_map/ppermute | solution.py:164
  61.3 0.7 copy-start.12
  63.7 15.3 %collective-permute-start.3 = (bf16[2,32,768]{2,1,0:T(8,128)(2,1)}, bf16[2,32,768]{2,1,0:T(8,128)(2,1)S(1)}, u32[]{:S(2)}, u32[]{:S(2)}) collective-permute-start(bf16[2,32,768]{2,1,0:T(8,128)(2,1)} %get-tuple-element.27), channel_id=1, source_target_pairs={{0,2},{1,3},{2,0},{3,1},{4,6},{5,7},{6,4},{7,5},{8,10},{9,11},{10,... | collective-permute-start | bytes 294920 | tf_op jit(solution)/shard_map/ppermute | solution.py:164
  66.3 0.7 copy-start.11
  68.7 11.6 %collective-permute-start.6 = (bf16[2,32,768]{2,1,0:T(8,128)(2,1)}, bf16[2,32,768]{2,1,0:T(8,128)(2,1)S(1)}, u32[]{:S(2)}, u32[]{:S(2)}) collective-permute-start(bf16[2,32,768]{2,1,0:T(8,128)(2,1)} %get-tuple-element.31), channel_id=1, source_target_pairs={{0,10},{1,11},{2,8},{3,9},{4,14},{5,15},{6,12},{7,13},{8,2},{9,3},... | collective-permute-start | bytes 294920 | tf_op jit(solution)/shard_map/ppermute | solution.py:170
  70.1 11.6 %collective-permute-start.7 = (bf16[2,32,768]{2,1,0:T(8,128)(2,1)}, bf16[2,32,768]{2,1,0:T(8,128)(2,1)S(1)}, u32[]{:S(2)}, u32[]{:S(2)}) collective-permute-start(bf16[2,32,768]{2,1,0:T(8,128)(2,1)} %get-tuple-element.32), channel_id=1, source_target_pairs={{0,8},{4,12},{8,0},{12,4},{16,24},{20,28},{24,16},{28,20},{1,9},{5... | collective-permute-start | bytes 294920 | tf_op jit(solution)/shard_map/ppermute | solution.py:166
  70.5 0.7 copy-start.10
  72.9 9.4 %collective-permute-start.10 = (bf16[2,32,768]{2,1,0:T(8,128)(2,1)}, bf16[2,32,768]{2,1,0:T(8,128)(2,1)S(1)}, u32[]{:S(2)}, u32[]{:S(2)}) collective-permute-start(bf16[2,32,768]{2,1,0:T(8,128)(2,1)} %get-tuple-element.35), channel_id=1, source_target_pairs={{0,18},{1,19},{2,16},{3,17},{4,22},{5,23},{6,20},{7,21},{8,26},{9,... | collective-permute-start | bytes 294920 | tf_op jit(solution)/shard_map/ppermute | solution.py:170
  76.6 0.7 copy-start.9
  76.6 5.7 %collective-permute-start.11 = (bf16[2,32,768]{2,1,0:T(8,128)(2,1)}, bf16[2,32,768]{2,1,0:T(8,128)(2,1)S(1)}, u32[]{:S(2)}, u32[]{:S(2)}) collective-permute-start(bf16[2,32,768]{2,1,0:T(8,128)(2,1)} %get-tuple-element.36), channel_id=1, source_target_pairs={{0,16},{4,20},{8,24},{12,28},{16,0},{20,4},{24,8},{28,12},{1,17},{... | collective-permute-start | bytes 294920 | tf_op jit(solution)/shard_map/ppermute | solution.py:166
  79.0 7.6 %collective-permute-start.14 = (bf16[2,32,768]{2,1,0:T(8,128)(2,1)}, bf16[2,32,768]{2,1,0:T(8,128)(2,1)S(1)}, u32[]{:S(2)}, u32[]{:S(2)}) collective-permute-start(bf16[2,32,768]{2,1,0:T(8,128)(2,1)} %get-tuple-element.39), channel_id=1, source_target_pairs={{0,26},{1,27},{2,24},{3,25},{4,30},{5,31},{6,28},{7,29},{8,18},{9,... | collective-permute-start | bytes 294920 | tf_op jit(solution)/shard_map/ppermute | solution.py:170
  80.2 6.8 %collective-permute-start.15 = (bf16[2,32,768]{2,1,0:T(8,128)(2,1)}, bf16[2,32,768]{2,1,0:T(8,128)(2,1)S(1)}, u32[]{:S(2)}, u32[]{:S(2)}) collective-permute-start(bf16[2,32,768]{2,1,0:T(8,128)(2,1)} %get-tuple-element.40), channel_id=1, source_target_pairs={{0,24},{4,28},{8,16},{12,20},{16,8},{20,12},{24,0},{28,4},{1,25},{... | collective-permute-start | bytes 294920 | tf_op jit(solution)/shard_map/ppermute | solution.py:166
  87.0 0.9 %copy-start.7 = (bf16[2,32,768]{2,1,0:T(8,128)(2,1)S(1)}, bf16[2,32,768]{2,1,0:T(8,128)(2,1)}, u32[]{:S(2)}) copy-start(bf16[2,32,768]{2,1,0:T(8,128)(2,1)} %get-tuple-element.28.refs_1_) | copy-start | bytes 294916

commit v3 on v2

v3 whole, which is shorter than its diff:
```python
import math

import jax
import jax.numpy as jnp
from jax import lax
from jax.experimental import pallas as pl
from jax.experimental.pallas import tpu as pltpu
from jax.sharding import PartitionSpec as P

BLOCK = 128
HALO = 64
NEGATIVE_FILL = -1e30
LAST = (((1,), (1,)), ((), ()))
BF16 = jnp.bfloat16
PARAMS = pltpu.CompilerParams(vmem_limit_bytes=32 << 20)


def vmem():
    return pl.BlockSpec(memory_space=pltpu.VMEM)


def smem():
    return pl.BlockSpec(memory_space=pltpu.SMEM)


def hbm():
    return pl.BlockSpec(memory_space=pltpu.HBM)


def shaped(*shape):
    return pltpu.VMEM(shape, BF16)


def far_away(*arrays):
    return [pltpu.with_memory_space_constraint(array, pltpu.HBM) for array in arrays]


def column_of(count, width, number):
    row = lax.broadcasted_iota(jnp.int32, (count, width), 0)
    found = jnp.zeros((count, width), jnp.int32)
    for r in range(count):
        found = jnp.where(row == r, number(r), found)
    return found


def pick_kernel(
    picks_ref, band_ref, q_hbm, k_hbm, v_hbm, summary_ref, halo_ref, width_ref, q_ref, k_ref, v_ref, sems
):
    per_block = picks_ref.shape[1]
    copies = [
        pltpu.make_async_copy(ref, into, sems.at[part])
        for part, (ref, into) in enumerate(((k_hbm, k_ref), (v_hbm, v_ref), (q_hbm, q_ref)))
    ]
    for copy in copies:
        copy.start()
    wanted = column_of(per_block, BLOCK, lambda r: picks_ref[0, r])
    width_ref[...] = column_of(*width_ref.shape, lambda r: band_ref[r])
    column = lax.broadcasted_iota(jnp.int32, (per_block, BLOCK), 1)
    chosen = jnp.where(column == wanted, 1.0, 0.0).astype(BF16)
    for part, ref in enumerate((k_ref, v_ref)):
        copies[part].wait()
        taken = jnp.dot(chosen, ref[...], preferred_element_type=jnp.float32)
        summary_ref[part] = taken.astype(BF16)
        halo_ref[part] = ref[BLOCK - HALO :, :]
    copies[2].wait()


def stack_kernel(*refs):
    for k, ref in enumerate(refs[:-1]):
        refs[-1][k] = ref[...]


def attend_kernel(width_ref, q_ref, k_ref, v_ref, halo_ref, mine_ref, other_ref, out_ref):
    size = BLOCK
    heads = q_ref.shape[1] // size
    chips, unused, per_block, unused = mine_ref.shape
    far_rows = chips * per_block
    place = lax.axis_index("seq")
    chip = place // 2
    core = lax.rem(place, 2)
    scale = 1.0 / math.sqrt(size)
    never = 4 * BLOCK
    own_gap = lax.broadcasted_iota(jnp.int32, (BLOCK, BLOCK), 0) - lax.broadcasted_iota(
        jnp.int32, (BLOCK, BLOCK), 1
    )
    own_gap = jnp.where(own_gap >= 0, own_gap, never)
    back_gap = lax.broadcasted_iota(jnp.int32, (BLOCK, HALO), 0) - lax.broadcasted_iota(
        jnp.int32, (BLOCK, HALO), 1
    )
    back_gap = jnp.where(place > 0, back_gap + HALO, never)
    far_chip = (lax.broadcasted_iota(jnp.int32, (BLOCK, far_rows), 1) // per_block) ^ chip
    mine_gap = jnp.where(far_chip * 2 + core < place, 0, never)
    other_gap = jnp.where(far_chip * 2 + (1 - core) < place, 0, never)
    gap = jnp.concatenate([own_gap, mine_gap, other_gap, back_gap], 1)
    for h in range(heads):
        cols = slice(h * size, (h + 1) * size)
        query = q_ref[:, cols]
        joined = [
            jnp.concatenate(
                [
                    own[:, cols],
                    mine_ref[:, part, :, cols].reshape(far_rows, size),
                    other_ref[:, part, :, cols].reshape(far_rows, size),
                    halo_ref[part, :, cols],
                ],
                0,
            )
            for part, own in enumerate((k_ref, v_ref))
        ]
        scores = lax.dot_general(query, joined[0], LAST, preferred_element_type=jnp.float32) * scale
        valid = gap < width_ref[h : h + 1, :]
        scores = jnp.where(valid, scores, NEGATIVE_FILL)
        largest = jnp.max(scores, axis=1, keepdims=True)
        weights = jnp.where(valid, jnp.exp(scores - largest), 0.0)
        total = jnp.sum(weights, axis=1, keepdims=True)
        mixed = jnp.dot(weights.astype(BF16), joined[1], preferred_element_type=jnp.float32)
        out_ref[:, cols] = (mixed / total).astype(BF16)


def project_kernel(att_ref, mine_ref, other_ref, *refs):
    send_ref, keep_ref = refs[-2:]
    half, unused, rows, feat = att_ref.shape
    count = half * rows
    core = lax.rem(lax.axis_index("seq"), 2)
    side = lax.rem(lax.axis_index("head"), 2)
    rows_in = jnp.concatenate(
        [att_ref[:, 1 - side].reshape(count, feat), att_ref[:, side].reshape(count, feat)], 0
    )
    for which, ref in ((core, mine_ref), (1 - core, other_ref)):
        found = lax.dot_general(rows_in, ref[...], LAST, preferred_element_type=jnp.float32)
        found = found.astype(BF16).reshape(2, half, rows, ref.shape[0])
        send_ref[which] = found[0]
        keep_ref[which] = found[1]


def split_kernel(came_ref, keep_ref, away_ref, stay_ref):
    side = lax.axis_index("head") // 2
    for ref, which in ((away_ref, 1 - side), (stay_ref, side)):
        total = came_ref[:, which].astype(jnp.float32) + keep_ref[:, which].astype(jnp.float32)
        ref[...] = total.astype(BF16)


def join_kernel(*refs):
    out_ref = refs[-1]
    wide = refs[0].shape[-1]
    chip = lax.axis_index("seq") // 2
    for k in range(len(refs) // 2):
        total = refs[2 * k][...].astype(jnp.float32) + refs[2 * k + 1][...].astype(jnp.float32)
        total = total.astype(BF16)
        if len(out_ref.shape) == 4:
            out_ref[chip ^ k] = total
            continue
        for c in range(2):
            start = pl.multiple_of((chip ^ k) * (2 * wide), 128)
            out_ref[:, pl.ds(start + c * wide, wide)] = total[c]


def local(queries, keys, values, band, picks, w_out):
    heads = band.shape[0]
    tok_rows, feat = queries.shape
    per_block = picks.shape[1]
    seq = lax.axis_size("seq")
    groups = lax.axis_size("head")
    wide = w_out.shape[0]
    rows = tok_rows // groups
    chips = seq // 2
    half = groups // 2

    def swap(value, k, z):
        if k == 0:
            return lax.ppermute(value, "head", [(i, i ^ z) for i in range(groups)])
        if z == 0:
            return lax.ppermute(value, "seq", [(i, i ^ k) for i in range(seq)])
        pairs = [
            (s * groups + h, (s ^ k) * groups + (h ^ z)) for s in range(seq) for h in range(groups)
        ]
        return lax.ppermute(value, ("seq", "head"), pairs)

    other_w = swap(w_out, 1, 0)
    listed = BLOCK + HALO + seq * per_block
    summary, halo, width, queries, keys, values = pl.pallas_call(
        pick_kernel,
        out_shape=(
            shaped(2, per_block, feat),
            shaped(2, HALO, feat),
            pltpu.VMEM((heads, listed), jnp.int32),
        )
        + (shaped(tok_rows, feat),) * 3,
        in_specs=[smem(), smem(), hbm(), hbm(), hbm()],
        out_specs=(vmem(),) * 6,
        scratch_shapes=[pltpu.SemaphoreType.DMA((3,))],
        compiler_params=PARAMS,
    )(*far_away(picks, band, queries, keys, values))
    far = [summary] + [swap(summary, 2 * k, 0) for k in range(1, chips)]
    halo = lax.ppermute(halo, "seq", [(i, i + 1) for i in range(seq - 1)])
    mine = pl.pallas_call(
        stack_kernel,
        out_shape=shaped(chips, 2, per_block, feat),
        in_specs=[vmem()] * chips,
        out_specs=vmem(),
        compiler_params=PARAMS,
    )(*far)
    other = swap(mine, 1, 0)
    attention = pl.pallas_call(
        attend_kernel,
        out_shape=shaped(tok_rows, feat),
        in_specs=[vmem()] * 7,
        out_specs=vmem(),
        compiler_params=PARAMS,
    )(width, queries, keys, values, halo, mine, other)
    pieces = []
    before = ()
    for k in range(chips):
        part = swap(attention, 2 * k, 0) if k else attention
        send, keep = pl.pallas_call(
            project_kernel,
            out_shape=(shaped(2, half, rows, wide), shaped(2, half, rows, wide)),
            in_specs=[vmem()] * 3 + [pl.BlockSpec(memory_space=pl.ANY)] * len(before),
            out_specs=(vmem(), vmem()),
            compiler_params=PARAMS,
        )(part.reshape(half, 2, rows, feat), w_out, other_w, *before)
        before = (send,)
        came = swap(send, 0, 1)
        away, stay = pl.pallas_call(
            split_kernel,
            out_shape=(shaped(2, rows, wide), shaped(2, rows, wide)),
            in_specs=[vmem()] * 2,
            out_specs=(vmem(), vmem()),
            compiler_params=PARAMS,
        )(came, keep)
        pieces.append(swap(away, 2 * k, 2))
        pieces.append(swap(stay, 2 * k, 0) if k else stay)
    flat = wide % 128 == 0
    joined = pl.pallas_call(
        join_kernel,
        out_shape=jax.ShapeDtypeStruct((rows, seq * wide) if flat else (chips, 2, rows, wide), BF16),
        in_specs=[vmem()] * len(pieces),
        out_specs=vmem(),
        compiler_params=PARAMS,
    )(*pieces)
    return joined if flat else joined.transpose(2, 0, 1, 3).reshape(rows, seq * wide)


def solution(mesh):
    placed = (
        P("seq", "head"),
        P("seq", "head"),
        P("seq", "head"),
        P("head"),
        P("seq", None),
        P("seq", "head"),
    )
    return jax.shard_map(
        local, mesh=mesh, in_specs=placed, out_specs=P(("seq", "head"), None), check_vma=False
    )
```

time: 89.3 us -> 65.5 us (0.73)
  Pallas kernels: 34.2 us -> 13 us
  blocking collectives: 16.5 us -> 0 us
  waiting for transfers between devices: 6.86 us -> 21 us
  starting transfers between devices: 22.4 us -> 31.2 us
  local copies, waits for them, and re-layouts: 8.67 us -> 0.01 us
    all_gather x1 -> x0, blocking collectives: 16.5 us -> none  [local(): far = lax.all_gather(summary, 'seq', axis=0, tiled=False)]
    ppermute x7 -> x11, waiting for transfers between devices: 1.93 us -> 17.7 us  [swap(): return lax.ppermute(value, 'seq', [(i, i ^ k) for i in range(seq)])]
    pallas_call x4, Pallas kernels: 16.8 us -> 6.53 us  [local(): pl.pallas_call(project_kernel, out_shape=(shaped(2, half, rows, wide), sh...]
    ppermute x7 -> x11, starting transfers between devices: 6.19 us -> 15.1 us  [swap(): return lax.ppermute(value, 'seq', [(i, i ^ k) for i in range(seq)])]
    unnamed x26 -> x2, local copies, waits for them, and re-layouts: 8.67 us -> 0.01 us
    pallas_call x4, Pallas kernels: 6.9 us -> 0.19 us  [local(): pl.pallas_call(split_kernel, out_shape=(shaped(2, rows, wide), shaped(2,...]
    pallas_call x1, Pallas kernels: 7.04 us -> 3.23 us  [local(): pl.pallas_call(attend_kernel, out_shape=shaped(tok_rows, feat), in_specs=...]
    ppermute x3, waiting for transfers between devices: 4.92 us -> 2.67 us  [swap(): return lax.ppermute(value, ('seq', 'head'), pairs)]
  transfers between devices with their start and end apart: 16 -> 20, of which waited for: 4 -> 10; matrix products, arithmetic and copies ran while one was open for 0% -> 0% of each run, Pallas kernels for 38% -> 19%
where the time goes in v3:
time: 65.5 us; the launch traced here: 65.3 us
  starting transfers between devices  31.2 us (48%)
  waiting for transfers between devices  21 us (32%)
  Pallas kernels  13 us (20%)
    ppermute x11, waiting for transfers between devices, swap(): return lax.ppermute(value, 'seq', [(i, i ^ k) for i in range(seq)])  17.7 us
    ppermute x11, starting transfers between devices, swap(): return lax.ppermute(value, 'seq', [(i, i ^ k) for i in range(seq)])  15.1 us
    ppermute x5, starting transfers between devices, swap(): return lax.ppermute(value, 'head', [(i, i ^ z) for i in range(groups)])  8.07 us
    pallas_call x4, Pallas kernels, local(): pl.pallas_call(project_kernel, out_shape=(shaped(2, half, rows, wide), sh...  6.53 us
    ppermute x3, starting transfers between devices, swap(): return lax.ppermute(value, ('seq', 'head'), pairs)  6.19 us
    pallas_call x1, Pallas kernels, local(): pl.pallas_call(attend_kernel, out_shape=shaped(tok_rows, feat), in_specs=...  3.23 us
    ppermute x3, waiting for transfers between devices, swap(): return lax.ppermute(value, ('seq', 'head'), pairs)  2.67 us
    pallas_call x1, Pallas kernels, local(): pl.pallas_call(pick_kernel, out_shape=(shaped(2, per_block, feat), shaped...  2.19 us
  transfers between devices with their start and end apart: 20, of which 10 were waited for; matrix products, arithmetic and copies ran while one was open for 0% of the time, Pallas kernels for 19%

profile of v3, /device:TPU:0, one launch (start us, length us, event | category | flops | bytes accessed | tf_op | source)
XLA Modules:
  0.0 65.3 jit_solution(1064223667622372814)
XLA Ops:
  0.0 0.5 collective-permute-start.5
  0.5 2.2 %shard_map.64 = (bf16[2,16,1536]{2,1,0:T(8,128)(2,1)S(1)}, bf16[2,64,1536]{2,1,0:T(8,128)(2,1)S(1)}, s32[12,320]{1,0:T(8,128)S(1)}, bf16[128,1536]{1,0:T(8,128)(...) custom-call(s32[1,16]{1,0:T(1,128)} %picks_ref.1, s32[12]{0:T(128)} %band_ref.1, ...), custom_call_target="tpu_custom_call" | custom-call | tf_op jit(solution)/shard_map/pallas_call | solution.py:181
  2.6 2.6 %collective-permute-start.1 = (bf16[2,16,1536]{2,1,0:T(8,128)(2,1)S(1)}, bf16[2,16,1536]{2,1,0:T(8,128)(2,1)S(1)}, u32[]{:S(2)}, u32[]{:S(2)}) collective-permute-start(bf16[2,16,1536]{2,1,0:T(8,128)(2,1)S(1)} %get-tuple-element.32.refs_0_), channel_id=1, source_target_pairs={{0,8},{4,12},{8,0},{12,4},{16,24},{20,28},{24,16},{28,20},{1,9},{5... | collective-permute-start | bytes 294920 | tf_op jit(solution)/shard_map/ppermute | solution.py:173
  5.2 1.5 %collective-permute-start.2 = (bf16[2,16,1536]{2,1,0:T(8,128)(2,1)S(1)}, bf16[2,16,1536]{2,1,0:T(8,128)(2,1)S(1)}, u32[]{:S(2)}, u32[]{:S(2)}) collective-permute-start(bf16[2,16,1536]{2,1,0:T(8,128)(2,1)S(1)} %get-tuple-element.32.refs_0_), channel_id=1, source_target_pairs={{0,16},{4,20},{8,24},{12,28},{16,0},{20,4},{24,8},{28,12},{1,17},{... | collective-permute-start | bytes 294920 | tf_op jit(solution)/shard_map/ppermute | solution.py:173
  6.7 0.0 collective-permute-start.3
  6.7 1.9 %collective-permute-start = (bf16[2,64,1536]{2,1,0:T(8,128)(2,1)S(1)}, bf16[2,64,1536]{2,1,0:T(8,128)(2,1)S(1)}, u32[]{:S(2)}, u32[]{:S(2)}) collective-permute-start(bf16[2,64,1536]{2,1,0:T(8,128)(2,1)S(1)} %get-tuple-element.31), channel_id=1, source_target_pairs={{0,4},{4,8},{8,12},{12,16},{16,20},{20,24},{24,28},{1,5},{5,9},{9,... | collective-permute-start | bytes 1179656 | tf_op jit(solution)/shard_map/ppermute | solution.py:195
  8.6 0.1 collective-permute-done.1.refs_1_
  8.7 2.6 %collective-permute-done.2.refs_2_ = bf16[2,16,1536]{2,1,0:T(8,128)(2,1)S(1)} collective-permute-done((bf16[2,16,1536]{2,1,0:T(8,128)(2,1)S(1)}, bf16[2,16,1536]{2,1,0:T(8,128)(2,1)S(1)}, u32[]{:S(2)}, u32[]{:S(2)}) %collective-permute-start.2) | collective-permute-done | bytes 98336 | tf_op jit(solution)/shard_map/ppermute | solution.py:173
  11.3 1.0 %collective-permute-done.3.refs_3_ = bf16[2,16,1536]{2,1,0:T(8,128)(2,1)S(1)} collective-permute-done((bf16[2,16,1536]{2,1,0:T(8,128)(2,1)S(1)}, bf16[2,16,1536]{2,1,0:T(8,128)(2,1)S(1)}, u32[]{:S(2)}, u32[]{:S(2)}) %collective-permute-start.3) | collective-permute-done | bytes 98336 | tf_op jit(solution)/shard_map/ppermute | solution.py:173
  12.3 0.1 collective-permute-start.4
  12.4 0.0 collective-permute-done.halo_ref
  12.4 1.7 %collective-permute-done.4.other_ref = bf16[4,2,16,1536]{3,2,1,0:T(8,128)(2,1)S(1)} collective-permute-done((bf16[4,2,16,1536]{3,2,1,0:T(8,128)(2,1)S(1)}, bf16[4,2,16,1536]{3,2,1,0:T(8,128)(2,1)S(1)}, u32[]{:S(2)}, u32[]{:S(2)}) %collective-permute-start.4) | collective-permute-done | bytes 393248 | tf_op jit(solution)/shard_map/ppermute | solution.py:173
  14.1 3.2 %shard_map.66 = bf16[128,1536]{1,0:T(8,128)(2,1)S(1)} custom-call(s32[12,320]{1,0:T(8,128)S(1)} %get-tuple-element.27.width_ref, bf16[128,1536]{1,0:T(8,128)(2,1)S(1)} %get-tuple-element.28.q_ref, bf16[128,1536]{1,0:T(8,128)(2,1)S(1)} %get-tuple-element.29.k_ref, bf16[128,1536]{1,0:T(8,128)(2,1)S(1)} %get-tuple-element.30.v_ref, ...), custom_call_target="tpu_custom_call" | custom-call | tf_op jit(solution)/shard_map/pallas_call | solution.py:204
  17.3 3.8 %collective-permute-start.8 = (bf16[128,1536]{1,0:T(8,128)(2,1)S(1)}, bf16[128,1536]{1,0:T(8,128)(2,1)S(1)}, u32[]{:S(2)}, u32[]{:S(2)}) collective-permute-start(bf16[128,1536]{1,0:T(8,128)(2,1)S(1)} %shard_map.66), channel_id=1, source_target_pairs={{0,8},{4,12},{8,0},{12,4},{16,24},{20,28},{24,16},{28,20},{1,9},{5... | collective-permute-start | bytes 1179656 | tf_op jit(solution)/shard_map/ppermute | solution.py:173
  21.1 1.5 %collective-permute-start.12 = (bf16[128,1536]{1,0:T(8,128)(2,1)S(1)}, bf16[128,1536]{1,0:T(8,128)(2,1)S(1)}, u32[]{:S(2)}, u32[]{:S(2)}) collective-permute-start(bf16[128,1536]{1,0:T(8,128)(2,1)S(1)} %shard_map.66), channel_id=1, source_target_pairs={{0,16},{4,20},{8,24},{12,28},{16,0},{20,4},{24,8},{28,12},{1,17},{... | collective-permute-start | bytes 1179656 | tf_op jit(solution)/shard_map/ppermute | solution.py:173
  22.6 0.9 %collective-permute-start.16 = (bf16[128,1536]{1,0:T(8,128)(2,1)S(1)}, bf16[128,1536]{1,0:T(8,128)(2,1)S(1)}, u32[]{:S(2)}, u32[]{:S(2)}) collective-permute-start(bf16[128,1536]{1,0:T(8,128)(2,1)S(1)} %shard_map.66), channel_id=1, source_target_pairs={{0,24},{4,28},{8,16},{12,20},{16,8},{20,12},{24,0},{28,4},{1,25},{... | collective-permute-start | bytes 1179656 | tf_op jit(solution)/shard_map/ppermute | solution.py:173
  23.5 0.0 collective-permute-done.5.other_ref
  23.5 1.6 %shard_map.67 = (bf16[2,2,32,768]{3,2,1,0:T(8,128)(2,1)S(1)}, bf16[2,2,32,768]{3,2,1,0:T(8,128)(2,1)S(1)}) custom-call(bf16[2,2,32,1536]{3,2,1,0:T(8,128)(2,1)S(1)} %bitcast.4, bf16[768,1536]{1,0:T(8,128)(2,1)S(1)} %copy-done, bf16[768,1536]{1,0:T(8,128)(2,1)S(1)} %collective-permute-done.5.other_ref), custom_call_target="tpu_custom_call" | custom-call | tf_op jit(solution)/shard_map/pallas_call | solution.py:215
  25.1 1.7 %collective-permute-start.6 = (bf16[2,2,32,768]{3,2,1,0:T(8,128)(2,1)S(1)}, bf16[2,2,32,768]{3,2,1,0:T(8,128)(2,1)S(1)}, u32[]{:S(2)}, u32[]{:S(2)}) collective-permute-start(bf16[2,2,32,768]{3,2,1,0:T(8,128)(2,1)S(1)} %get-tuple-element.33.refs_0_), channel_id=1, source_target_pairs={{0,1},{1,0},{2,3},{3,2},{4,5},{5,4},{6,7},{7,6},{8,9},{9,8},{10,11... | collective-permute-start | bytes 589832 | tf_op jit(solution)/shard_map/ppermute | solution.py:171
  26.8 4.3 %collective-permute-done.8 = bf16[128,1536]{1,0:T(8,128)(2,1)S(1)} collective-permute-done((bf16[128,1536]{1,0:T(8,128)(2,1)S(1)}, bf16[128,1536]{1,0:T(8,128)(2,1)S(1)}, u32[]{:S(2)}, u32[]{:S(2)}) %collective-permute-start.8) | collective-permute-done | bytes 393248 | tf_op jit(solution)/shard_map/ppermute | solution.py:173
  31.1 1.6 %shard_map.69 = (bf16[2,2,32,768]{3,2,1,0:T(8,128)(2,1)S(1)}, bf16[2,2,32,768]{3,2,1,0:T(8,128)(2,1)S(1)}) custom-call(bf16[2,2,32,1536]{3,2,1,0:T(8,128)(2,1)S(1)} %bitcast.7, bf16[768,1536]{1,0:T(8,128)(2,1)S(1)} %copy-done, bf16[768,1536]{1,0:T(8,128)(2,1)S(1)} %collective-permute-done.5.other_ref, bf16[2,2,32,768]{3,2,1,0:T(8,128)(2,1)S(1)} %get-tuple-element.33.refs_0_), custom_call_target="tpu_custom_call" | custom-call | tf_op jit(solution)/shard_map/pallas_call | solution.py:215
  32.7 1.6 %collective-permute-start.9 = (bf16[2,2,32,768]{3,2,1,0:T(8,128)(2,1)S(1)}, bf16[2,2,32,768]{3,2,1,0:T(8,128)(2,1)S(1)}, u32[]{:S(2)}, u32[]{:S(2)}) collective-permute-start(bf16[2,2,32,768]{3,2,1,0:T(8,128)(2,1)S(1)} %get-tuple-element.37.refs_0_), channel_id=1, source_target_pairs={{0,1},{1,0},{2,3},{3,2},{4,5},{5,4},{6,7},{7,6},{8,9},{9,8},{10,11... | collective-permute-start | bytes 589832 | tf_op jit(solution)/shard_map/ppermute | solution.py:171
  34.4 5.0 %collective-permute-done.12 = bf16[128,1536]{1,0:T(8,128)(2,1)S(1)} collective-permute-done((bf16[128,1536]{1,0:T(8,128)(2,1)S(1)}, bf16[128,1536]{1,0:T(8,128)(2,1)S(1)}, u32[]{:S(2)}, u32[]{:S(2)}) %collective-permute-start.12) | collective-permute-done | bytes 393248 | tf_op jit(solution)/shard_map/ppermute | solution.py:173
  39.4 1.6 %shard_map.71 = (bf16[2,2,32,768]{3,2,1,0:T(8,128)(2,1)S(1)}, bf16[2,2,32,768]{3,2,1,0:T(8,128)(2,1)S(1)}) custom-call(bf16[2,2,32,1536]{3,2,1,0:T(8,128)(2,1)S(1)} %bitcast.6, bf16[768,1536]{1,0:T(8,128)(2,1)S(1)} %copy-done, bf16[768,1536]{1,0:T(8,128)(2,1)S(1)} %collective-permute-done.5.other_ref, bf16[2,2,32,768]{3,2,1,0:T(8,128)(2,1)S(1)} %get-tuple-element.37.refs_0_), custom_call_target="tpu_custom_call" | custom-call | tf_op jit(solution)/shard_map/pallas_call | solution.py:215
  41.0 1.6 %collective-permute-start.13 = (bf16[2,2,32,768]{3,2,1,0:T(8,128)(2,1)S(1)}, bf16[2,2,32,768]{3,2,1,0:T(8,128)(2,1)S(1)}, u32[]{:S(2)}, u32[]{:S(2)}) collective-permute-start(bf16[2,2,32,768]{3,2,1,0:T(8,128)(2,1)S(1)} %get-tuple-element.41.refs_0_), channel_id=1, source_target_pairs={{0,1},{1,0},{2,3},{3,2},{4,5},{5,4},{6,7},{7,6},{8,9},{9,8},{10,11... | collective-permute-start | bytes 589832 | tf_op jit(solution)/shard_map/ppermute | solution.py:171
  42.6 0.0 collective-permute-done.16
  42.7 1.6 %shard_map.73 = (bf16[2,2,32,768]{3,2,1,0:T(8,128)(2,1)S(1)}, bf16[2,2,32,768]{3,2,1,0:T(8,128)(2,1)S(1)}) custom-call(bf16[2,2,32,1536]{3,2,1,0:T(8,128)(2,1)S(1)} %bitcast.5, bf16[768,1536]{1,0:T(8,128)(2,1)S(1)} %copy-done, bf16[768,1536]{1,0:T(8,128)(2,1)S(1)} %collective-permute-done.5.other_ref, bf16[2,2,32,768]{3,2,1,0:T(8,128)(2,1)S(1)} %get-tuple-element.41.refs_0_), custom_call_target="tpu_custom_call" | custom-call | tf_op jit(solution)/shard_map/pallas_call | solution.py:215
  44.3 0.5 collective-permute-start.17
  44.8 0.0 collective-permute-done.6.came_ref
  44.8 0.1 shard_map.68
  44.9 2.6 %collective-permute-start.7 = (bf16[2,32,768]{2,1,0:T(8,128)(2,1)S(1)}, bf16[2,32,768]{2,1,0:T(8,128)(2,1)S(1)}, u32[]{:S(2)}, u32[]{:S(2)}) collective-permute-start(bf16[2,32,768]{2,1,0:T(8,128)(2,1)S(1)} %get-tuple-element.35), channel_id=1, source_target_pairs={{0,2},{1,3},{2,0},{3,1},{4,6},{5,7},{6,4},{7,5},{8,10},{9,11},{10,... | collective-permute-start | bytes 294920 | tf_op jit(solution)/shard_map/ppermute | solution.py:171
  47.5 0.0 collective-permute-done.9.came_ref
  47.6 0.4 collective-permute-start.10
  47.9 1.5 %collective-permute-start.11 = (bf16[2,32,768]{2,1,0:T(8,128)(2,1)S(1)}, bf16[2,32,768]{2,1,0:T(8,128)(2,1)S(1)}, u32[]{:S(2)}, u32[]{:S(2)}) collective-permute-start(bf16[2,32,768]{2,1,0:T(8,128)(2,1)S(1)} %get-tuple-element.40), channel_id=1, source_target_pairs={{0,8},{4,12},{8,0},{12,4},{16,24},{20,28},{24,16},{28,20},{1,9},{5... | collective-permute-start | bytes 294920 | tf_op jit(solution)/shard_map/ppermute | solution.py:173
  49.4 0.0 collective-permute-done.13.came_ref
  49.5 2.5 %collective-permute-start.14 = (bf16[2,32,768]{2,1,0:T(8,128)(2,1)S(1)}, bf16[2,32,768]{2,1,0:T(8,128)(2,1)S(1)}, u32[]{:S(2)}, u32[]{:S(2)}) collective-permute-start(bf16[2,32,768]{2,1,0:T(8,128)(2,1)S(1)} %get-tuple-element.43), channel_id=1, source_target_pairs={{0,18},{1,19},{2,16},{3,17},{4,22},{5,23},{6,20},{7,21},{8,26},{9,... | collective-permute-start | bytes 294920 | tf_op jit(solution)/shard_map/ppermute | solution.py:177
  52.0 0.6 collective-permute-done.17.came_ref
  52.6 1.0 %collective-permute-start.15 = (bf16[2,32,768]{2,1,0:T(8,128)(2,1)S(1)}, bf16[2,32,768]{2,1,0:T(8,128)(2,1)S(1)}, u32[]{:S(2)}, u32[]{:S(2)}) collective-permute-start(bf16[2,32,768]{2,1,0:T(8,128)(2,1)S(1)} %get-tuple-element.44), channel_id=1, source_target_pairs={{0,16},{4,20},{8,24},{12,28},{16,0},{20,4},{24,8},{28,12},{1,17},{... | collective-permute-start | bytes 294920 | tf_op jit(solution)/shard_map/ppermute | solution.py:173
  53.7 0.0 collective-permute-done.7.refs_0_
  53.7 3.3 %collective-permute-start.18 = (bf16[2,32,768]{2,1,0:T(8,128)(2,1)S(1)}, bf16[2,32,768]{2,1,0:T(8,128)(2,1)S(1)}, u32[]{:S(2)}, u32[]{:S(2)}) collective-permute-start(bf16[2,32,768]{2,1,0:T(8,128)(2,1)S(1)} %get-tuple-element.47), channel_id=1, source_target_pairs={{0,26},{1,27},{2,24},{3,25},{4,30},{5,31},{6,28},{7,29},{8,18},{9,... | collective-permute-start | bytes 294920 | tf_op jit(solution)/shard_map/ppermute | solution.py:177
  57.0 1.9 %collective-permute-done.10.refs_2_ = bf16[2,32,768]{2,1,0:T(8,128)(2,1)S(1)} collective-permute-done((bf16[2,32,768]{2,1,0:T(8,128)(2,1)S(1)}, bf16[2,32,768]{2,1,0:T(8,128)(2,1)S(1)}, u32[]{:S(2)}, u32[]{:S(2)}) %collective-permute-start.10) | collective-permute-done | bytes 98336 | tf_op jit(solution)/shard_map/ppermute | solution.py:177
  58.9 1.8 %collective-permute-start.19 = (bf16[2,32,768]{2,1,0:T(8,128)(2,1)S(1)}, bf16[2,32,768]{2,1,0:T(8,128)(2,1)S(1)}, u32[]{:S(2)}, u32[]{:S(2)}) collective-permute-start(bf16[2,32,768]{2,1,0:T(8,128)(2,1)S(1)} %get-tuple-element.48), channel_id=1, source_target_pairs={{0,24},{4,28},{8,16},{12,20},{16,8},{20,12},{24,0},{28,4},{1,25},{... | collective-permute-start | bytes 294920 | tf_op jit(solution)/shard_map/ppermute | solution.py:173
  60.7 0.0 collective-permute-done.11.refs_3_
  60.7 0.0 collective-permute-done.14.refs_4_
  60.7 0.0 collective-permute-done.15.refs_5_
  60.7 0.7 %collective-permute-done.18.refs_6_ = bf16[2,32,768]{2,1,0:T(8,128)(2,1)S(1)} collective-permute-done((bf16[2,32,768]{2,1,0:T(8,128)(2,1)S(1)}, bf16[2,32,768]{2,1,0:T(8,128)(2,1)S(1)}, u32[]{:S(2)}, u32[]{:S(2)}) %collective-permute-start.18) | collective-permute-done | bytes 98336 | tf_op jit(solution)/shard_map/ppermute | solution.py:177
  61.5 3.0 %collective-permute-done.19.refs_7_ = bf16[2,32,768]{2,1,0:T(8,128)(2,1)S(1)} collective-permute-done((bf16[2,32,768]{2,1,0:T(8,128)(2,1)S(1)}, bf16[2,32,768]{2,1,0:T(8,128)(2,1)S(1)}, u32[]{:S(2)}, u32[]{:S(2)}) %collective-permute-start.19) | collective-permute-done | bytes 98336 | tf_op jit(solution)/shard_map/ppermute | solution.py:173
  64.5 0.8 %shard_map.75 = bf16[32,6144]{1,0:T(8,128)(2,1)} custom-call(bf16[2,32,768]{2,1,0:T(8,128)(2,1)S(1)} %collective-permute-done.7.refs_0_, bf16[2,32,768]{2,1,0:T(8,128)(2,1)S(1)} %get-tuple-element.36.refs_1_, bf16[2,32,768]{2,1,0:T(8,128)(2,1)S(1)} %collective-permute-done.10.refs_2_, bf16[2,32,768]{2,1,0:T(8,128)(2,1)S(1)} %collective-permute-done.11.refs_3_, ...), custom_call_target="tpu_custom_call" | custom-call | tf_op jit(solution)/shard_map/pallas_call | solution.py:234
  (6 shorter events, 0.2 us)
Async XLA Ops:
  0.0 23.5 %copy-start = (bf16[768,1536]{1,0:T(8,128)(2,1)S(1)}, bf16[768,1536]{1,0:T(8,128)(2,1)}, u32[]{:S(2)}) copy-start(bf16[768,1536]{1,0:T(8,128)(2,1)} %mine_ref.7) | copy-start | bytes 7077892
  0.0 23.5 %collective-permute-start.5 = (bf16[768,1536]{1,0:T(8,128)(2,1)}, bf16[768,1536]{1,0:T(8,128)(2,1)S(1)}, u32[]{:S(2)}, u32[]{:S(2)}) collective-permute-start(bf16[768,1536]{1,0:T(8,128)(2,1)} %mine_ref.7), channel_id=1, source_target_pairs={{0,4},{4,0},{8,12},{12,8},{16,20},{20,16},{24,28},{28,24},{1,5},{5... | collective-permute-start | bytes 7077896 | tf_op jit(solution)/shard_map/ppermute | solution.py:173
  2.6 6.0 %collective-permute-start.1 = (bf16[2,16,1536]{2,1,0:T(8,128)(2,1)S(1)}, bf16[2,16,1536]{2,1,0:T(8,128)(2,1)S(1)}, u32[]{:S(2)}, u32[]{:S(2)}) collective-permute-start(bf16[2,16,1536]{2,1,0:T(8,128)(2,1)S(1)} %get-tuple-element.32.refs_0_), channel_id=1, source_target_pairs={{0,8},{4,12},{8,0},{12,4},{16,24},{20,28},{24,16},{28,20},{1,9},{5... | collective-permute-start | bytes 294920 | tf_op jit(solution)/shard_map/ppermute | solution.py:173
  5.2 6.1 %collective-permute-start.2 = (bf16[2,16,1536]{2,1,0:T(8,128)(2,1)S(1)}, bf16[2,16,1536]{2,1,0:T(8,128)(2,1)S(1)}, u32[]{:S(2)}, u32[]{:S(2)}) collective-permute-start(bf16[2,16,1536]{2,1,0:T(8,128)(2,1)S(1)} %get-tuple-element.32.refs_0_), channel_id=1, source_target_pairs={{0,16},{4,20},{8,24},{12,28},{16,0},{20,4},{24,8},{28,12},{1,17},{... | collective-permute-start | bytes 294920 | tf_op jit(solution)/shard_map/ppermute | solution.py:173
  6.7 5.5 %collective-permute-start.3 = (bf16[2,16,1536]{2,1,0:T(8,128)(2,1)S(1)}, bf16[2,16,1536]{2,1,0:T(8,128)(2,1)S(1)}, u32[]{:S(2)}, u32[]{:S(2)}) collective-permute-start(bf16[2,16,1536]{2,1,0:T(8,128)(2,1)S(1)} %get-tuple-element.32.refs_0_), channel_id=1, source_target_pairs={{0,24},{4,28},{8,16},{12,20},{16,8},{20,12},{24,0},{28,4},{1,25},{... | collective-permute-start | bytes 294920 | tf_op jit(solution)/shard_map/ppermute | solution.py:173
  6.7 5.6 %collective-permute-start = (bf16[2,64,1536]{2,1,0:T(8,128)(2,1)S(1)}, bf16[2,64,1536]{2,1,0:T(8,128)(2,1)S(1)}, u32[]{:S(2)}, u32[]{:S(2)}) collective-permute-start(bf16[2,64,1536]{2,1,0:T(8,128)(2,1)S(1)} %get-tuple-element.31), channel_id=1, source_target_pairs={{0,4},{4,8},{8,12},{12,16},{16,20},{20,24},{24,28},{1,5},{5,9},{9,... | collective-permute-start | bytes 1179656 | tf_op jit(solution)/shard_map/ppermute | solution.py:195
  12.3 1.8 %collective-permute-start.4 = (bf16[4,2,16,1536]{3,2,1,0:T(8,128)(2,1)S(1)}, bf16[4,2,16,1536]{3,2,1,0:T(8,128)(2,1)S(1)}, u32[]{:S(2)}, u32[]{:S(2)}) collective-permute-start(bf16[4,2,16,1536]{3,2,1,0:T(8,128)(2,1)S(1)} %shard_map.65.mine_ref), channel_id=1, source_target_pairs={{0,4},{4,0},{8,12},{12,8},{16,20},{20,16},{24,28},{28,24},{1,5},{5... | collective-permute-start | bytes 1179656 | tf_op jit(solution)/shard_map/ppermute | solution.py:173
  17.3 13.8 %collective-permute-start.8 = (bf16[128,1536]{1,0:T(8,128)(2,1)S(1)}, bf16[128,1536]{1,0:T(8,128)(2,1)S(1)}, u32[]{:S(2)}, u32[]{:S(2)}) collective-permute-start(bf16[128,1536]{1,0:T(8,128)(2,1)S(1)} %shard_map.66), channel_id=1, source_target_pairs={{0,8},{4,12},{8,0},{12,4},{16,24},{20,28},{24,16},{28,20},{1,9},{5... | collective-permute-start | bytes 1179656 | tf_op jit(solution)/shard_map/ppermute | solution.py:173
  21.1 18.3 %collective-permute-start.12 = (bf16[128,1536]{1,0:T(8,128)(2,1)S(1)}, bf16[128,1536]{1,0:T(8,128)(2,1)S(1)}, u32[]{:S(2)}, u32[]{:S(2)}) collective-permute-start(bf16[128,1536]{1,0:T(8,128)(2,1)S(1)} %shard_map.66), channel_id=1, source_target_pairs={{0,16},{4,20},{8,24},{12,28},{16,0},{20,4},{24,8},{28,12},{1,17},{... | collective-permute-start | bytes 1179656 | tf_op jit(solution)/shard_map/ppermute | solution.py:173
  22.6 20.0 %collective-permute-start.16 = (bf16[128,1536]{1,0:T(8,128)(2,1)S(1)}, bf16[128,1536]{1,0:T(8,128)(2,1)S(1)}, u32[]{:S(2)}, u32[]{:S(2)}) collective-permute-start(bf16[128,1536]{1,0:T(8,128)(2,1)S(1)} %shard_map.66), channel_id=1, source_target_pairs={{0,24},{4,28},{8,16},{12,20},{16,8},{20,12},{24,0},{28,4},{1,25},{... | collective-permute-start | bytes 1179656 | tf_op jit(solution)/shard_map/ppermute | solution.py:173
  25.1 19.7 %collective-permute-start.6 = (bf16[2,2,32,768]{3,2,1,0:T(8,128)(2,1)S(1)}, bf16[2,2,32,768]{3,2,1,0:T(8,128)(2,1)S(1)}, u32[]{:S(2)}, u32[]{:S(2)}) collective-permute-start(bf16[2,2,32,768]{3,2,1,0:T(8,128)(2,1)S(1)} %get-tuple-element.33.refs_0_), channel_id=1, source_target_pairs={{0,1},{1,0},{2,3},{3,2},{4,5},{5,4},{6,7},{7,6},{8,9},{9,8},{10,11... | collective-permute-start | bytes 589832 | tf_op jit(solution)/shard_map/ppermute | solution.py:171
  32.7 14.8 %collective-permute-start.9 = (bf16[2,2,32,768]{3,2,1,0:T(8,128)(2,1)S(1)}, bf16[2,2,32,768]{3,2,1,0:T(8,128)(2,1)S(1)}, u32[]{:S(2)}, u32[]{:S(2)}) collective-permute-start(bf16[2,2,32,768]{3,2,1,0:T(8,128)(2,1)S(1)} %get-tuple-element.37.refs_0_), channel_id=1, source_target_pairs={{0,1},{1,0},{2,3},{3,2},{4,5},{5,4},{6,7},{7,6},{8,9},{9,8},{10,11... | collective-permute-start | bytes 589832 | tf_op jit(solution)/shard_map/ppermute | solution.py:171
  41.0 8.4 %collective-permute-start.13 = (bf16[2,2,32,768]{3,2,1,0:T(8,128)(2,1)S(1)}, bf16[2,2,32,768]{3,2,1,0:T(8,128)(2,1)S(1)}, u32[]{:S(2)}, u32[]{:S(2)}) collective-permute-start(bf16[2,2,32,768]{3,2,1,0:T(8,128)(2,1)S(1)} %get-tuple-element.41.refs_0_), channel_id=1, source_target_pairs={{0,1},{1,0},{2,3},{3,2},{4,5},{5,4},{6,7},{7,6},{8,9},{9,8},{10,11... | collective-permute-start | bytes 589832 | tf_op jit(solution)/shard_map/ppermute | solution.py:171
  44.3 8.3 %collective-permute-start.17 = (bf16[2,2,32,768]{3,2,1,0:T(8,128)(2,1)S(1)}, bf16[2,2,32,768]{3,2,1,0:T(8,128)(2,1)S(1)}, u32[]{:S(2)}, u32[]{:S(2)}) collective-permute-start(bf16[2,2,32,768]{3,2,1,0:T(8,128)(2,1)S(1)} %get-tuple-element.45), channel_id=1, source_target_pairs={{0,1},{1,0},{2,3},{3,2},{4,5},{5,4},{6,7},{7,6},{8,9},{9,8},{10,11... | collective-permute-start | bytes 589832 | tf_op jit(solution)/shard_map/ppermute | solution.py:171
  44.9 8.8 %collective-permute-start.7 = (bf16[2,32,768]{2,1,0:T(8,128)(2,1)S(1)}, bf16[2,32,768]{2,1,0:T(8,128)(2,1)S(1)}, u32[]{:S(2)}, u32[]{:S(2)}) collective-permute-start(bf16[2,32,768]{2,1,0:T(8,128)(2,1)S(1)} %get-tuple-element.35), channel_id=1, source_target_pairs={{0,2},{1,3},{2,0},{3,1},{4,6},{5,7},{6,4},{7,5},{8,10},{9,11},{10,... | collective-permute-start | bytes 294920 | tf_op jit(solution)/shard_map/ppermute | solution.py:171
  47.6 11.4 %collective-permute-start.10 = (bf16[2,32,768]{2,1,0:T(8,128)(2,1)S(1)}, bf16[2,32,768]{2,1,0:T(8,128)(2,1)S(1)}, u32[]{:S(2)}, u32[]{:S(2)}) collective-permute-start(bf16[2,32,768]{2,1,0:T(8,128)(2,1)S(1)} %get-tuple-element.39), channel_id=1, source_target_pairs={{0,10},{1,11},{2,8},{3,9},{4,14},{5,15},{6,12},{7,13},{8,2},{9,3},... | collective-permute-start | bytes 294920 | tf_op jit(solution)/shard_map/ppermute | solution.py:177
  47.9 12.8 %collective-permute-start.11 = (bf16[2,32,768]{2,1,0:T(8,128)(2,1)S(1)}, bf16[2,32,768]{2,1,0:T(8,128)(2,1)S(1)}, u32[]{:S(2)}, u32[]{:S(2)}) collective-permute-start(bf16[2,32,768]{2,1,0:T(8,128)(2,1)S(1)} %get-tuple-element.40), channel_id=1, source_target_pairs={{0,8},{4,12},{8,0},{12,4},{16,24},{20,28},{24,16},{28,20},{1,9},{5... | collective-permute-start | bytes 294920 | tf_op jit(solution)/shard_map/ppermute | solution.py:173
  49.5 11.2 %collective-permute-start.14 = (bf16[2,32,768]{2,1,0:T(8,128)(2,1)S(1)}, bf16[2,32,768]{2,1,0:T(8,128)(2,1)S(1)}, u32[]{:S(2)}, u32[]{:S(2)}) collective-permute-start(bf16[2,32,768]{2,1,0:T(8,128)(2,1)S(1)} %get-tuple-element.43), channel_id=1, source_target_pairs={{0,18},{1,19},{2,16},{3,17},{4,22},{5,23},{6,20},{7,21},{8,26},{9,... | collective-permute-start | bytes 294920 | tf_op jit(solution)/shard_map/ppermute | solution.py:177
  52.6 8.1 %collective-permute-start.15 = (bf16[2,32,768]{2,1,0:T(8,128)(2,1)S(1)}, bf16[2,32,768]{2,1,0:T(8,128)(2,1)S(1)}, u32[]{:S(2)}, u32[]{:S(2)}) collective-permute-start(bf16[2,32,768]{2,1,0:T(8,128)(2,1)S(1)} %get-tuple-element.44), channel_id=1, source_target_pairs={{0,16},{4,20},{8,24},{12,28},{16,0},{20,4},{24,8},{28,12},{1,17},{... | collective-permute-start | bytes 294920 | tf_op jit(solution)/shard_map/ppermute | solution.py:173
  53.7 7.8 %collective-permute-start.18 = (bf16[2,32,768]{2,1,0:T(8,128)(2,1)S(1)}, bf16[2,32,768]{2,1,0:T(8,128)(2,1)S(1)}, u32[]{:S(2)}, u32[]{:S(2)}) collective-permute-start(bf16[2,32,768]{2,1,0:T(8,128)(2,1)S(1)} %get-tuple-element.47), channel_id=1, source_target_pairs={{0,26},{1,27},{2,24},{3,25},{4,30},{5,31},{6,28},{7,29},{8,18},{9,... | collective-permute-start | bytes 294920 | tf_op jit(solution)/shard_map/ppermute | solution.py:177
  58.9 5.5 %collective-permute-start.19 = (bf16[2,32,768]{2,1,0:T(8,128)(2,1)S(1)}, bf16[2,32,768]{2,1,0:T(8,128)(2,1)S(1)}, u32[]{:S(2)}, u32[]{:S(2)}) collective-permute-start(bf16[2,32,768]{2,1,0:T(8,128)(2,1)S(1)} %get-tuple-element.48), channel_id=1, source_target_pairs={{0,24},{4,28},{8,16},{12,20},{16,8},{20,12},{24,0},{28,4},{1,25},{... | collective-permute-start | bytes 294920 | tf_op jit(solution)/shard_map/ppermute | solution.py:173

commit v4 on v3

--- a/solution.py
+++ b/solution.py
@@ -1,3 +1,4 @@
+import functools
 import math
 
 import jax
@@ -117,27 +118,40 @@
         out_ref[:, cols] = (mixed / total).astype(BF16)
 
 
-def project_kernel(att_ref, mine_ref, other_ref, *refs):
-    send_ref, keep_ref = refs[-2:]
-    half, unused, rows, feat = att_ref.shape
-    count = half * rows
+def cut_kernel(first_ref, second_ref, *refs):
+    low_ref, high_ref = refs[-2:]
+    half = low_ref.shape[0]
+    low_ref[...] = first_ref[:half]
+    high_ref[...] = second_ref[half:]
+
+
+def project_kernel(count, chunks, *refs):
+    pieces, (mine_ref, other_ref) = refs[:count], refs[count : count + 2]
+    send_refs, keep_refs = refs[-2 * chunks : -chunks], refs[-chunks:]
     core = lax.rem(lax.axis_index("seq"), 2)
     side = lax.rem(lax.axis_index("head"), 2)
-    rows_in = jnp.concatenate(
-        [att_ref[:, 1 - side].reshape(count, feat), att_ref[:, side].reshape(count, feat)], 0
-    )
+    rows_in = []
+    for parity in (1 - side, side):
+        for ref in pieces:
+            for j in range(ref.shape[0] // 2):
+                rows_in.append(ref[2 * j + parity])
+    rows_in = jnp.concatenate(rows_in, 0)
     for which, ref in ((core, mine_ref), (1 - core, other_ref)):
         found = lax.dot_general(rows_in, ref[...], LAST, preferred_element_type=jnp.float32)
-        found = found.astype(BF16).reshape(2, half, rows, ref.shape[0])
-        send_ref[which] = found[0]
-        keep_ref[which] = found[1]
-
-
-def split_kernel(came_ref, keep_ref, away_ref, stay_ref):
+        found = found.astype(BF16).reshape((2, chunks) + send_refs[0].shape[1:])
+        for k in range(chunks):
+            send_refs[k][which] = found[0, k]
+            keep_refs[k][which] = found[1, k]
+
+
+def split_kernel(late, came_ref, keep_ref, *refs):
+    away_ref, stay_ref = refs[-2 - late : len(refs) - late]
     side = lax.axis_index("head") // 2
     for ref, which in ((away_ref, 1 - side), (stay_ref, side)):
         total = came_ref[:, which].astype(jnp.float32) + keep_ref[:, which].astype(jnp.float32)
         ref[...] = total.astype(BF16)
+    if late:
+        refs[-1][...] = refs[0][...]
 
 
 def join_kernel(*refs):
@@ -208,36 +222,73 @@
         out_specs=vmem(),
         compiler_params=PARAMS,
     )(width, queries, keys, values, halo, mine, other)
-    pieces = []
-    before = ()
-    for k in range(chips):
-        part = swap(attention, 2 * k, 0) if k else attention
-        send, keep = pl.pallas_call(
-            project_kernel,
-            out_shape=(shaped(2, half, rows, wide), shaped(2, half, rows, wide)),
-            in_specs=[vmem()] * 3 + [pl.BlockSpec(memory_space=pl.ANY)] * len(before),
-            out_specs=(vmem(), vmem()),
+    attention = attention.reshape(groups, rows, feat)
+    parts = {k: [swap(attention, 2 * k, 0)] for k in range(1, chips) if k != 3}
+    parts[0] = [attention]
+    found, stays = {}, {}
+
+    def after(*arrays):
+        return [pl.BlockSpec(memory_space=pl.ANY)] * len(arrays), arrays
+
+    def projected(group, order):
+        pieces = [piece for k in group for piece in parts[k]]
+        n = len(group)
+        specs, arrays = after(*order)
+        return pl.pallas_call(
+            functools.partial(project_kernel, len(pieces), n),
+            out_shape=(shaped(2, half, rows, wide),) * (2 * n),
+            in_specs=[vmem()] * (len(pieces) + 2) + specs,
+            out_specs=(vmem(),) * (2 * n),
             compiler_params=PARAMS,
-        )(part.reshape(half, 2, rows, feat), w_out, other_w, *before)
-        before = (send,)
+            cost_estimate=pl.CostEstimate(
+                flops=4 * n * tok_rows * wide * feat, bytes_accessed=4 * wide * feat, transcendentals=0
+            ),
+        )(*pieces, w_out, other_w, *arrays)
+
+    def exchanged(k, send, keep, order=()):
         came = swap(send, 0, 1)
-        away, stay = pl.pallas_call(
-            split_kernel,
-            out_shape=(shaped(2, rows, wide), shaped(2, rows, wide)),
-            in_specs=[vmem()] * 2,
-            out_specs=(vmem(), vmem()),
+        late = k > 1
+        specs, arrays = after(*order)
+        parted = pl.pallas_call(
+            functools.partial(split_kernel, late),
+            out_shape=(shaped(2, rows, wide),) * (2 + late),
+            in_specs=[vmem()] * (2 + late) + specs,
+            out_specs=(vmem(),) * (2 + late),
             compiler_params=PARAMS,
-        )(came, keep)
-        pieces.append(swap(away, 2 * k, 2))
-        pieces.append(swap(stay, 2 * k, 0) if k else stay)
+        )(came, keep, *([stays[k - 1]] if late else []), *arrays)
+        stays[k] = parted[1]
+        found[k] = [swap(parted[0], 2 * k, 2), stays[k]]
+        if late:
+            found[k - 1][1] = swap(parted[2], 2 * (k - 1), 0)
+
+    exchanged(0, *projected([0], ()))
+    pair = [k for k in (1, 2) if k < chips]
+    if pair:
+        results = projected(pair, (stays[0],))
+        for k, send, keep in zip(pair, results, results[len(pair) :]):
+            exchanged(k, send, keep, found[1][:1] if k == 2 else ())
+    if chips > 3:
+        specs, arrays = after(*(results[-1], found[0][0]))
+        low, high = pl.pallas_call(
+            cut_kernel,
+            out_shape=(shaped(half, rows, feat),) * 2,
+            in_specs=[vmem()] * 2 + specs,
+            out_specs=(vmem(),) * 2,
+            compiler_params=PARAMS,
+        )(parts[1][0], parts[2][0], *arrays)
+        parts[3] = [swap(low, 4, 0), swap(high, 2, 0)]
+    for k in range(3, chips):
+        exchanged(k, *projected([k], (stays[1],)), (found[1][1:]) if k == 3 else ())
+    if chips > 1:
+        found[chips - 1][1] = swap(stays[chips - 1], 2 * (chips - 1), 0)
     flat = wide % 128 == 0
     joined = pl.pallas_call(
         join_kernel,
         out_shape=jax.ShapeDtypeStruct((rows, seq * wide) if flat else (chips, 2, rows, wide), BF16),
-        in_specs=[vmem()] * len(pieces),
+        in_specs=[vmem()] * (2 * chips),
         out_specs=vmem(),
         compiler_params=PARAMS,
-    )(*pieces)
+    )(*[piece for k in range(chips) for piece in found[k]])
     return joined if flat else joined.transpose(2, 0, 1, 3).reshape(rows, seq * wide)
 
 

time: 65.5 us -> 65.8 us (level)
  starting transfers between devices: 31.2 us -> 33.1 us
  Pallas kernels: 13 us -> 11.2 us
    ppermute x11 -> x12, waiting for transfers between devices: 17.7 us -> 12.1 us  [swap(): return lax.ppermute(value, 'seq', [(i, i ^ k) for i in range(seq)])]
    ppermute x5, waiting for transfers between devices: 0.63 us -> 5.86 us  [swap(): return lax.ppermute(value, 'head', [(i, i ^ z) for i in range(groups)])]
    ppermute x11 -> x12, starting transfers between devices: 15.1 us -> 17.9 us  [swap(): return lax.ppermute(value, 'seq', [(i, i ^ k) for i in range(seq)])]
    ppermute x3, starting transfers between devices: 6.19 us -> 3.72 us  [swap(): return lax.ppermute(value, ('seq', 'head'), pairs)]
    pallas_call x8, Pallas kernels: 6.72 us -> 4.92 us  [the longest x3 4.68 us: projected(): pl.pallas_call(functools.partial(project_kernel, len(pieces), n), out_sha...]
    ppermute x5, starting transfers between devices: 8.07 us -> 9.64 us  [swap(): return lax.ppermute(value, 'head', [(i, i ^ z) for i in range(groups)])]
  transfers between devices with their start and end apart: 20 -> 21, of which waited for: 10 -> 13; matrix products, arithmetic and copies ran while one was open for 0% -> 0% of each run, Pallas kernels for 19% -> 16%
where the time goes in v4:
time: 65.8 us; the launch traced here: 65.7 us
  starting transfers between devices  33.1 us (50%)
  waiting for transfers between devices  21.2 us (32%)
  Pallas kernels  11.2 us (17%)
    ppermute x12, starting transfers between devices, swap(): return lax.ppermute(value, 'seq', [(i, i ^ k) for i in range(seq)])  17.9 us
    ppermute x12, waiting for transfers between devices, swap(): return lax.ppermute(value, 'seq', [(i, i ^ k) for i in range(seq)])  12.1 us
    ppermute x5, starting transfers between devices, swap(): return lax.ppermute(value, 'head', [(i, i ^ z) for i in range(groups)])  9.64 us
    ppermute x5, waiting for transfers between devices, swap(): return lax.ppermute(value, 'head', [(i, i ^ z) for i in range(groups)])  5.86 us
    pallas_call x3, Pallas kernels, projected(): pl.pallas_call(functools.partial(project_kernel, len(pieces), n), out_sha...  4.68 us
    ppermute x3, starting transfers between devices, swap(): return lax.ppermute(value, ('seq', 'head'), pairs)  3.72 us
    ppermute x3, waiting for transfers between devices, swap(): return lax.ppermute(value, ('seq', 'head'), pairs)  3.31 us
    pallas_call x1, Pallas kernels, local(): pl.pallas_call(attend_kernel, out_shape=shaped(tok_rows, feat), in_specs=...  3.23 us
  transfers between devices with their start and end apart: 21, of which 13 were waited for; matrix products, arithmetic and copies ran while one was open for 0% of the time, Pallas kernels for 16%

profile of v4, /device:TPU:0, one launch (start us, length us, event | category | flops | bytes accessed | tf_op | source)
XLA Modules:
  0.0 65.7 jit_solution(4120267762194814510)
XLA Ops:
  0.0 0.5 collective-permute-start.5
  0.5 2.2 %shard_map.64 = (bf16[2,16,1536]{2,1,0:T(8,128)(2,1)S(1)}, bf16[2,64,1536]{2,1,0:T(8,128)(2,1)S(1)}, s32[12,320]{1,0:T(8,128)S(1)}, bf16[128,1536]{1,0:T(8,128)(...) custom-call(s32[1,16]{1,0:T(1,128)} %picks_ref.1, s32[12]{0:T(128)} %band_ref.1, ...), custom_call_target="tpu_custom_call" | custom-call | tf_op jit(solution)/shard_map/pallas_call | solution.py:195
  2.6 2.6 %collective-permute-start.1 = (bf16[2,16,1536]{2,1,0:T(8,128)(2,1)S(1)}, bf16[2,16,1536]{2,1,0:T(8,128)(2,1)S(1)}, u32[]{:S(2)}, u32[]{:S(2)}) collective-permute-start(bf16[2,16,1536]{2,1,0:T(8,128)(2,1)S(1)} %get-tuple-element.36.refs_0_), channel_id=1, source_target_pairs={{0,8},{4,12},{8,0},{12,4},{16,24},{20,28},{24,16},{28,20},{1,9},{5... | collective-permute-start | bytes 294920 | tf_op jit(solution)/shard_map/ppermute | solution.py:187
  5.2 1.5 %collective-permute-start.2 = (bf16[2,16,1536]{2,1,0:T(8,128)(2,1)S(1)}, bf16[2,16,1536]{2,1,0:T(8,128)(2,1)S(1)}, u32[]{:S(2)}, u32[]{:S(2)}) collective-permute-start(bf16[2,16,1536]{2,1,0:T(8,128)(2,1)S(1)} %get-tuple-element.36.refs_0_), channel_id=1, source_target_pairs={{0,16},{4,20},{8,24},{12,28},{16,0},{20,4},{24,8},{28,12},{1,17},{... | collective-permute-start | bytes 294920 | tf_op jit(solution)/shard_map/ppermute | solution.py:187
  6.7 0.0 collective-permute-start.3
  6.7 1.9 %collective-permute-start = (bf16[2,64,1536]{2,1,0:T(8,128)(2,1)S(1)}, bf16[2,64,1536]{2,1,0:T(8,128)(2,1)S(1)}, u32[]{:S(2)}, u32[]{:S(2)}) collective-permute-start(bf16[2,64,1536]{2,1,0:T(8,128)(2,1)S(1)} %get-tuple-element.35), channel_id=1, source_target_pairs={{0,4},{4,8},{8,12},{12,16},{16,20},{20,24},{24,28},{1,5},{5,9},{9,... | collective-permute-start | bytes 1179656 | tf_op jit(solution)/shard_map/ppermute | solution.py:209
  8.6 0.1 collective-permute-done.1.refs_1_
  8.7 2.6 %collective-permute-done.2.refs_2_ = bf16[2,16,1536]{2,1,0:T(8,128)(2,1)S(1)} collective-permute-done((bf16[2,16,1536]{2,1,0:T(8,128)(2,1)S(1)}, bf16[2,16,1536]{2,1,0:T(8,128)(2,1)S(1)}, u32[]{:S(2)}, u32[]{:S(2)}) %collective-permute-start.2) | collective-permute-done | bytes 98336 | tf_op jit(solution)/shard_map/ppermute | solution.py:187
  11.3 1.0 %collective-permute-done.3.refs_3_ = bf16[2,16,1536]{2,1,0:T(8,128)(2,1)S(1)} collective-permute-done((bf16[2,16,1536]{2,1,0:T(8,128)(2,1)S(1)}, bf16[2,16,1536]{2,1,0:T(8,128)(2,1)S(1)}, u32[]{:S(2)}, u32[]{:S(2)}) %collective-permute-start.3) | collective-permute-done | bytes 98336 | tf_op jit(solution)/shard_map/ppermute | solution.py:187
  12.3 0.1 collective-permute-start.4
  12.4 0.0 collective-permute-done.halo_ref
  12.4 1.7 %collective-permute-done.4.other_ref = bf16[4,2,16,1536]{3,2,1,0:T(8,128)(2,1)S(1)} collective-permute-done((bf16[4,2,16,1536]{3,2,1,0:T(8,128)(2,1)S(1)}, bf16[4,2,16,1536]{3,2,1,0:T(8,128)(2,1)S(1)}, u32[]{:S(2)}, u32[]{:S(2)}) %collective-permute-start.4) | collective-permute-done | bytes 393248 | tf_op jit(solution)/shard_map/ppermute | solution.py:187
  14.1 3.2 %shard_map.66 = bf16[128,1536]{1,0:T(8,128)(2,1)S(1)} custom-call(s32[12,320]{1,0:T(8,128)S(1)} %get-tuple-element.31.width_ref, bf16[128,1536]{1,0:T(8,128)(2,1)S(1)} %get-tuple-element.32.q_ref, bf16[128,1536]{1,0:T(8,128)(2,1)S(1)} %get-tuple-element.33.k_ref, bf16[128,1536]{1,0:T(8,128)(2,1)S(1)} %get-tuple-element.34.v_ref, ...), custom_call_target="tpu_custom_call" | custom-call | tf_op jit(solution)/shard_map/pallas_call | solution.py:218
  17.3 3.8 %collective-permute-start.8 = (bf16[4,32,1536]{2,1,0:T(8,128)(2,1)S(1)}, bf16[4,32,1536]{2,1,0:T(8,128)(2,1)S(1)}, u32[]{:S(2)}, u32[]{:S(2)}) collective-permute-start(bf16[4,32,1536]{2,1,0:T(8,128)(2,1)S(1)} %bitcast.1), channel_id=1, source_target_pairs={{0,8},{4,12},{8,0},{12,4},{16,24},{20,28},{24,16},{28,20},{1,9},{5... | collective-permute-start | bytes 1179656 | tf_op jit(solution)/shard_map/ppermute | solution.py:187
  21.1 1.5 %collective-permute-start.9 = (bf16[4,32,1536]{2,1,0:T(8,128)(2,1)S(1)}, bf16[4,32,1536]{2,1,0:T(8,128)(2,1)S(1)}, u32[]{:S(2)}, u32[]{:S(2)}) collective-permute-start(bf16[4,32,1536]{2,1,0:T(8,128)(2,1)S(1)} %bitcast.2), channel_id=1, source_target_pairs={{0,16},{4,20},{8,24},{12,28},{16,0},{20,4},{24,8},{28,12},{1,17},{... | collective-permute-start | bytes 1179656 | tf_op jit(solution)/shard_map/ppermute | solution.py:187
  22.6 0.0 collective-permute-done.5.refs_2_.refs_3_
  22.6 1.6 %shard_map.67 = (bf16[2,2,32,768]{3,2,1,0:T(8,128)(2,1)S(1)}, bf16[2,2,32,768]{3,2,1,0:T(8,128)(2,1)S(1)}) custom-call(bf16[4,32,1536]{2,1,0:T(8,128)(2,1)S(1)} %bitcast.3, bf16[768,1536]{1,0:T(8,128)(2,1)S(1)} %copy-done, bf16[768,1536]{1,0:T(8,128)(2,1)S(1)} %collective-permute-done.5.refs_2_.refs_3_), custom_call_target="tpu_custom_call" | custom-call | flops 603979776 | bytes 4718592 | tf_op jit(solution)/shard_map/pallas_call | solution.py:237
  24.3 1.6 %collective-permute-start.6 = (bf16[2,2,32,768]{3,2,1,0:T(8,128)(2,1)S(1)}, bf16[2,2,32,768]{3,2,1,0:T(8,128)(2,1)S(1)}, u32[]{:S(2)}, u32[]{:S(2)}) collective-permute-start(bf16[2,2,32,768]{3,2,1,0:T(8,128)(2,1)S(1)} %get-tuple-element.37), channel_id=1, source_target_pairs={{0,1},{1,0},{2,3},{3,2},{4,5},{5,4},{6,7},{7,6},{8,9},{9,8},{10,11... | collective-permute-start | bytes 589832 | tf_op jit(solution)/shard_map/ppermute | solution.py:185
  25.9 4.1 %collective-permute-done.6.came_ref = bf16[2,2,32,768]{3,2,1,0:T(8,128)(2,1)S(1)} collective-permute-done((bf16[2,2,32,768]{3,2,1,0:T(8,128)(2,1)S(1)}, bf16[2,2,32,768]{3,2,1,0:T(8,128)(2,1)S(1)}, u32[]{:S(2)}, u32[]{:S(2)}) %collective-permute-start.6) | collective-permute-done | bytes 196640 | tf_op jit(solution)/shard_map/ppermute | solution.py:185
  30.1 3.4 %collective-permute-start.7 = (bf16[2,32,768]{2,1,0:T(8,128)(2,1)S(1)}, bf16[2,32,768]{2,1,0:T(8,128)(2,1)S(1)}, u32[]{:S(2)}, u32[]{:S(2)}) collective-permute-start(bf16[2,32,768]{2,1,0:T(8,128)(2,1)S(1)} %get-tuple-element.39), channel_id=1, source_target_pairs={{0,2},{1,3},{2,0},{3,1},{4,6},{5,7},{6,4},{7,5},{8,10},{9,11},{10,... | collective-permute-start | bytes 294920 | tf_op jit(solution)/shard_map/ppermute | solution.py:185
  33.5 0.0 collective-permute-done.8.refs_0_.first_ref
  33.5 0.0 collective-permute-done.9.refs_1_.second_ref
  33.5 1.4 %shard_map.69 = (bf16[2,2,32,768]{3,2,1,0:T(8,128)(2,1)S(1)}, bf16[2,2,32,768]{3,2,1,0:T(8,128)(2,1)S(1)}, bf16[2,2,32,768]{3,2,1,0:T(8,128)(2,1)S(1)}, bf16[2,2,32,768]{3,2,1,0:T(8,128)(2,1)S(1)}) custom-call(bf16[4,32,1536]{2,1,0:T(8,128)(2,1)S(1)} %collective-permute-done.8.refs_0_.first_ref, ...), custom_call_target="tpu_custom_call" | custom-call | flops 1207959552 | bytes 4718592 | tf_op jit(solution)/shard_map/pallas_call | solution.py:237
  34.9 0.9 %collective-permute-start.10 = (bf16[2,2,32,768]{3,2,1,0:T(8,128)(2,1)S(1)}, bf16[2,2,32,768]{3,2,1,0:T(8,128)(2,1)S(1)}, u32[]{:S(2)}, u32[]{:S(2)}) collective-permute-start(bf16[2,2,32,768]{3,2,1,0:T(8,128)(2,1)S(1)} %get-tuple-element.41), channel_id=1, source_target_pairs={{0,1},{1,0},{2,3},{3,2},{4,5},{5,4},{6,7},{7,6},{8,9},{9,8},{10,11... | collective-permute-start | bytes 589832 | tf_op jit(solution)/shard_map/ppermute | solution.py:185
  35.8 0.8 %collective-permute-done.7.refs_1_.refs_0_ = bf16[2,32,768]{2,1,0:T(8,128)(2,1)S(1)} collective-permute-done((bf16[2,32,768]{2,1,0:T(8,128)(2,1)S(1)}, bf16[2,32,768]{2,1,0:T(8,128)(2,1)S(1)}, u32[]{:S(2)}, u32[]{:S(2)}) %collective-permute-start.7) | collective-permute-done | bytes 98336 | tf_op jit(solution)/shard_map/ppermute | solution.py:185
  36.6 0.1 collective-permute-start.15
  36.7 1.2 %collective-permute-start.16 = (bf16[2,32,1536]{2,1,0:T(8,128)(2,1)S(1)}, bf16[2,32,1536]{2,1,0:T(8,128)(2,1)S(1)}, u32[]{:S(2)}, u32[]{:S(2)}) collective-permute-start(bf16[2,32,1536]{2,1,0:T(8,128)(2,1)S(1)} %get-tuple-element.50), channel_id=1, source_target_pairs={{0,8},{4,12},{8,0},{12,4},{16,24},{20,28},{24,16},{28,20},{1,9},{5... | collective-permute-start | bytes 589832 | tf_op jit(solution)/shard_map/ppermute | solution.py:187
  37.8 1.9 %collective-permute-start.12 = (bf16[2,2,32,768]{3,2,1,0:T(8,128)(2,1)S(1)}, bf16[2,2,32,768]{3,2,1,0:T(8,128)(2,1)S(1)}, u32[]{:S(2)}, u32[]{:S(2)}) collective-permute-start(bf16[2,2,32,768]{3,2,1,0:T(8,128)(2,1)S(1)} %get-tuple-element.44), channel_id=1, source_target_pairs={{0,1},{1,0},{2,3},{3,2},{4,5},{5,4},{6,7},{7,6},{8,9},{9,8},{10,11... | collective-permute-start | bytes 589832 | tf_op jit(solution)/shard_map/ppermute | solution.py:185
  39.8 1.0 %collective-permute-done.10.came_ref = bf16[2,2,32,768]{3,2,1,0:T(8,128)(2,1)S(1)} collective-permute-done((bf16[2,2,32,768]{3,2,1,0:T(8,128)(2,1)S(1)}, bf16[2,2,32,768]{3,2,1,0:T(8,128)(2,1)S(1)}, u32[]{:S(2)}, u32[]{:S(2)}) %collective-permute-start.10) | collective-permute-done | bytes 196640 | tf_op jit(solution)/shard_map/ppermute | solution.py:185
  40.8 2.3 %collective-permute-start.11 = (bf16[2,32,768]{2,1,0:T(8,128)(2,1)S(1)}, bf16[2,32,768]{2,1,0:T(8,128)(2,1)S(1)}, u32[]{:S(2)}, u32[]{:S(2)}) collective-permute-start(bf16[2,32,768]{2,1,0:T(8,128)(2,1)S(1)} %get-tuple-element.43), channel_id=1, source_target_pairs={{0,10},{1,11},{2,8},{3,9},{4,14},{5,15},{6,12},{7,13},{8,2},{9,3},... | collective-permute-start | bytes 294920 | tf_op jit(solution)/shard_map/ppermute | solution.py:191
  43.1 0.0 collective-permute-done.15.refs_0_
  43.1 0.4 collective-permute-done.16.refs_1_
  43.5 1.6 %shard_map.73 = (bf16[2,2,32,768]{3,2,1,0:T(8,128)(2,1)S(1)}, bf16[2,2,32,768]{3,2,1,0:T(8,128)(2,1)S(1)}) custom-call(bf16[2,32,1536]{2,1,0:T(8,128)(2,1)S(1)} %collective-permute-done.15.refs_0_, bf16[2,32,1536]{2,1,0:T(8,128)(2,1)S(1)} %collective-permute-done.16.refs_1_, bf16[768,1536]{1,0:T(8,128)(2,1)S(1)} %copy-done, ...), custom_call_target="tpu_custom_call" | custom-call | flops 603979776 | bytes 4718592 | tf_op jit(solution)/shard_map/pallas_call | solution.py:237
  45.1 1.8 %collective-permute-start.17 = (bf16[2,2,32,768]{3,2,1,0:T(8,128)(2,1)S(1)}, bf16[2,2,32,768]{3,2,1,0:T(8,128)(2,1)S(1)}, u32[]{:S(2)}, u32[]{:S(2)}) collective-permute-start(bf16[2,2,32,768]{3,2,1,0:T(8,128)(2,1)S(1)} %get-tuple-element.51), channel_id=1, source_target_pairs={{0,1},{1,0},{2,3},{3,2},{4,5},{5,4},{6,7},{7,6},{8,9},{9,8},{10,11... | collective-permute-start | bytes 589832 | tf_op jit(solution)/shard_map/ppermute | solution.py:185
  46.9 0.0 collective-permute-done.12.came_ref
  46.9 0.4 collective-permute-done.11.refs_1_.refs_2_
  47.3 0.1 shard_map.71
  47.4 5.0 %collective-permute-start.13 = (bf16[2,32,768]{2,1,0:T(8,128)(2,1)S(1)}, bf16[2,32,768]{2,1,0:T(8,128)(2,1)S(1)}, u32[]{:S(2)}, u32[]{:S(2)}) collective-permute-start(bf16[2,32,768]{2,1,0:T(8,128)(2,1)S(1)} %get-tuple-element.47), channel_id=1, source_target_pairs={{0,8},{4,12},{8,0},{12,4},{16,24},{20,28},{24,16},{28,20},{1,9},{5... | collective-permute-start | bytes 294920 | tf_op jit(solution)/shard_map/ppermute | solution.py:187
  52.4 4.3 %collective-permute-done.13.refs_1_.refs_3_ = bf16[2,32,768]{2,1,0:T(8,128)(2,1)S(1)} collective-permute-done((bf16[2,32,768]{2,1,0:T(8,128)(2,1)S(1)}, bf16[2,32,768]{2,1,0:T(8,128)(2,1)S(1)}, u32[]{:S(2)}, u32[]{:S(2)}) %collective-permute-start.13) | collective-permute-done | bytes 98336 | tf_op jit(solution)/shard_map/ppermute | solution.py:187
  56.7 0.1 shard_map.74
  56.8 0.1 collective-permute-start.18
  56.9 1.4 %collective-permute-start.19 = (bf16[2,32,768]{2,1,0:T(8,128)(2,1)S(1)}, bf16[2,32,768]{2,1,0:T(8,128)(2,1)S(1)}, u32[]{:S(2)}, u32[]{:S(2)}) collective-permute-start(bf16[2,32,768]{2,1,0:T(8,128)(2,1)S(1)} %get-tuple-element.55), channel_id=1, source_target_pairs={{0,26},{1,27},{2,24},{3,25},{4,30},{5,31},{6,28},{7,29},{8,18},{9,... | collective-permute-start | bytes 294920 | tf_op jit(solution)/shard_map/ppermute | solution.py:191
  58.3 1.6 %collective-permute-start.20 = (bf16[2,32,768]{2,1,0:T(8,128)(2,1)S(1)}, bf16[2,32,768]{2,1,0:T(8,128)(2,1)S(1)}, u32[]{:S(2)}, u32[]{:S(2)}) collective-permute-start(bf16[2,32,768]{2,1,0:T(8,128)(2,1)S(1)} %get-tuple-element.56), channel_id=1, source_target_pairs={{0,24},{4,28},{8,16},{12,20},{16,8},{20,12},{24,0},{28,4},{1,25},{... | collective-permute-start | bytes 294920 | tf_op jit(solution)/shard_map/ppermute | solution.py:187
  59.9 0.0 collective-permute-done.14.refs_4_
  59.9 1.5 %collective-permute-done.18.refs_5_ = bf16[2,32,768]{2,1,0:T(8,128)(2,1)S(1)} collective-permute-done((bf16[2,32,768]{2,1,0:T(8,128)(2,1)S(1)}, bf16[2,32,768]{2,1,0:T(8,128)(2,1)S(1)}, u32[]{:S(2)}, u32[]{:S(2)}) %collective-permute-start.18) | collective-permute-done | bytes 98336 | tf_op jit(solution)/shard_map/ppermute | solution.py:187
  61.5 2.9 %collective-permute-done.19.refs_6_ = bf16[2,32,768]{2,1,0:T(8,128)(2,1)S(1)} collective-permute-done((bf16[2,32,768]{2,1,0:T(8,128)(2,1)S(1)}, bf16[2,32,768]{2,1,0:T(8,128)(2,1)S(1)}, u32[]{:S(2)}, u32[]{:S(2)}) %collective-permute-start.19) | collective-permute-done | bytes 98336 | tf_op jit(solution)/shard_map/ppermute | solution.py:191
  64.4 0.5 collective-permute-done.20.refs_7_
  64.8 0.8 %shard_map.75 = bf16[32,6144]{1,0:T(8,128)(2,1)} custom-call(bf16[2,32,768]{2,1,0:T(8,128)(2,1)S(1)} %collective-permute-done.7.refs_1_.refs_0_, bf16[2,32,768]{2,1,0:T(8,128)(2,1)S(1)} %get-tuple-element.40.refs_4_.refs_1_, bf16[2,32,768]{2,1,0:T(8,128)(2,1)S(1)} %collective-permute-done.11.refs_1_.refs_2_, ...), custom_call_target="tpu_custom_call" | custom-call | tf_op jit(solution)/shard_map/pallas_call | solution.py:285
  (8 shorter events, 0.2 us)
Async XLA Ops:
  0.0 22.6 %copy-start = (bf16[768,1536]{1,0:T(8,128)(2,1)S(1)}, bf16[768,1536]{1,0:T(8,128)(2,1)}, u32[]{:S(2)}) copy-start(bf16[768,1536]{1,0:T(8,128)(2,1)} %refs_2_.3) | copy-start | bytes 7077892
  0.0 22.6 %collective-permute-start.5 = (bf16[768,1536]{1,0:T(8,128)(2,1)}, bf16[768,1536]{1,0:T(8,128)(2,1)S(1)}, u32[]{:S(2)}, u32[]{:S(2)}) collective-permute-start(bf16[768,1536]{1,0:T(8,128)(2,1)} %refs_2_.3), channel_id=1, source_target_pairs={{0,4},{4,0},{8,12},{12,8},{16,20},{20,16},{24,28},{28,24},{1,5},{5... | collective-permute-start | bytes 7077896 | tf_op jit(solution)/shard_map/ppermute | solution.py:187
  2.6 6.0 %collective-permute-start.1 = (bf16[2,16,1536]{2,1,0:T(8,128)(2,1)S(1)}, bf16[2,16,1536]{2,1,0:T(8,128)(2,1)S(1)}, u32[]{:S(2)}, u32[]{:S(2)}) collective-permute-start(bf16[2,16,1536]{2,1,0:T(8,128)(2,1)S(1)} %get-tuple-element.36.refs_0_), channel_id=1, source_target_pairs={{0,8},{4,12},{8,0},{12,4},{16,24},{20,28},{24,16},{28,20},{1,9},{5... | collective-permute-start | bytes 294920 | tf_op jit(solution)/shard_map/ppermute | solution.py:187
  5.2 6.1 %collective-permute-start.2 = (bf16[2,16,1536]{2,1,0:T(8,128)(2,1)S(1)}, bf16[2,16,1536]{2,1,0:T(8,128)(2,1)S(1)}, u32[]{:S(2)}, u32[]{:S(2)}) collective-permute-start(bf16[2,16,1536]{2,1,0:T(8,128)(2,1)S(1)} %get-tuple-element.36.refs_0_), channel_id=1, source_target_pairs={{0,16},{4,20},{8,24},{12,28},{16,0},{20,4},{24,8},{28,12},{1,17},{... | collective-permute-start | bytes 294920 | tf_op jit(solution)/shard_map/ppermute | solution.py:187
  6.7 5.5 %collective-permute-start.3 = (bf16[2,16,1536]{2,1,0:T(8,128)(2,1)S(1)}, bf16[2,16,1536]{2,1,0:T(8,128)(2,1)S(1)}, u32[]{:S(2)}, u32[]{:S(2)}) collective-permute-start(bf16[2,16,1536]{2,1,0:T(8,128)(2,1)S(1)} %get-tuple-element.36.refs_0_), channel_id=1, source_target_pairs={{0,24},{4,28},{8,16},{12,20},{16,8},{20,12},{24,0},{28,4},{1,25},{... | collective-permute-start | bytes 294920 | tf_op jit(solution)/shard_map/ppermute | solution.py:187
  6.7 5.6 %collective-permute-start = (bf16[2,64,1536]{2,1,0:T(8,128)(2,1)S(1)}, bf16[2,64,1536]{2,1,0:T(8,128)(2,1)S(1)}, u32[]{:S(2)}, u32[]{:S(2)}) collective-permute-start(bf16[2,64,1536]{2,1,0:T(8,128)(2,1)S(1)} %get-tuple-element.35), channel_id=1, source_target_pairs={{0,4},{4,8},{8,12},{12,16},{16,20},{20,24},{24,28},{1,5},{5,9},{9,... | collective-permute-start | bytes 1179656 | tf_op jit(solution)/shard_map/ppermute | solution.py:209
  12.3 1.8 %collective-permute-start.4 = (bf16[4,2,16,1536]{3,2,1,0:T(8,128)(2,1)S(1)}, bf16[4,2,16,1536]{3,2,1,0:T(8,128)(2,1)S(1)}, u32[]{:S(2)}, u32[]{:S(2)}) collective-permute-start(bf16[4,2,16,1536]{3,2,1,0:T(8,128)(2,1)S(1)} %shard_map.65.mine_ref), channel_id=1, source_target_pairs={{0,4},{4,0},{8,12},{12,8},{16,20},{20,16},{24,28},{28,24},{1,5},{5... | collective-permute-start | bytes 1179656 | tf_op jit(solution)/shard_map/ppermute | solution.py:187
  17.3 16.1 %collective-permute-start.8 = (bf16[4,32,1536]{2,1,0:T(8,128)(2,1)S(1)}, bf16[4,32,1536]{2,1,0:T(8,128)(2,1)S(1)}, u32[]{:S(2)}, u32[]{:S(2)}) collective-permute-start(bf16[4,32,1536]{2,1,0:T(8,128)(2,1)S(1)} %bitcast.1), channel_id=1, source_target_pairs={{0,8},{4,12},{8,0},{12,4},{16,24},{20,28},{24,16},{28,20},{1,9},{5... | collective-permute-start | bytes 1179656 | tf_op jit(solution)/shard_map/ppermute | solution.py:187
  21.1 12.4 %collective-permute-start.9 = (bf16[4,32,1536]{2,1,0:T(8,128)(2,1)S(1)}, bf16[4,32,1536]{2,1,0:T(8,128)(2,1)S(1)}, u32[]{:S(2)}, u32[]{:S(2)}) collective-permute-start(bf16[4,32,1536]{2,1,0:T(8,128)(2,1)S(1)} %bitcast.2), channel_id=1, source_target_pairs={{0,16},{4,20},{8,24},{12,28},{16,0},{20,4},{24,8},{28,12},{1,17},{... | collective-permute-start | bytes 1179656 | tf_op jit(solution)/shard_map/ppermute | solution.py:187
  24.3 5.7 %collective-permute-start.6 = (bf16[2,2,32,768]{3,2,1,0:T(8,128)(2,1)S(1)}, bf16[2,2,32,768]{3,2,1,0:T(8,128)(2,1)S(1)}, u32[]{:S(2)}, u32[]{:S(2)}) collective-permute-start(bf16[2,2,32,768]{3,2,1,0:T(8,128)(2,1)S(1)} %get-tuple-element.37), channel_id=1, source_target_pairs={{0,1},{1,0},{2,3},{3,2},{4,5},{5,4},{6,7},{7,6},{8,9},{9,8},{10,11... | collective-permute-start | bytes 589832 | tf_op jit(solution)/shard_map/ppermute | solution.py:185
  30.1 6.5 %collective-permute-start.7 = (bf16[2,32,768]{2,1,0:T(8,128)(2,1)S(1)}, bf16[2,32,768]{2,1,0:T(8,128)(2,1)S(1)}, u32[]{:S(2)}, u32[]{:S(2)}) collective-permute-start(bf16[2,32,768]{2,1,0:T(8,128)(2,1)S(1)} %get-tuple-element.39), channel_id=1, source_target_pairs={{0,2},{1,3},{2,0},{3,1},{4,6},{5,7},{6,4},{7,5},{8,10},{9,11},{10,... | collective-permute-start | bytes 294920 | tf_op jit(solution)/shard_map/ppermute | solution.py:185
  34.9 5.8 %collective-permute-start.10 = (bf16[2,2,32,768]{3,2,1,0:T(8,128)(2,1)S(1)}, bf16[2,2,32,768]{3,2,1,0:T(8,128)(2,1)S(1)}, u32[]{:S(2)}, u32[]{:S(2)}) collective-permute-start(bf16[2,2,32,768]{3,2,1,0:T(8,128)(2,1)S(1)} %get-tuple-element.41), channel_id=1, source_target_pairs={{0,1},{1,0},{2,3},{3,2},{4,5},{5,4},{6,7},{7,6},{8,9},{9,8},{10,11... | collective-permute-start | bytes 589832 | tf_op jit(solution)/shard_map/ppermute | solution.py:185
  36.6 6.5 %collective-permute-start.15 = (bf16[2,32,1536]{2,1,0:T(8,128)(2,1)S(1)}, bf16[2,32,1536]{2,1,0:T(8,128)(2,1)S(1)}, u32[]{:S(2)}, u32[]{:S(2)}) collective-permute-start(bf16[2,32,1536]{2,1,0:T(8,128)(2,1)S(1)} %get-tuple-element.49), channel_id=1, source_target_pairs={{0,16},{4,20},{8,24},{12,28},{16,0},{20,4},{24,8},{28,12},{1,17},{... | collective-permute-start | bytes 589832 | tf_op jit(solution)/shard_map/ppermute | solution.py:187
  36.7 6.8 %collective-permute-start.16 = (bf16[2,32,1536]{2,1,0:T(8,128)(2,1)S(1)}, bf16[2,32,1536]{2,1,0:T(8,128)(2,1)S(1)}, u32[]{:S(2)}, u32[]{:S(2)}) collective-permute-start(bf16[2,32,1536]{2,1,0:T(8,128)(2,1)S(1)} %get-tuple-element.50), channel_id=1, source_target_pairs={{0,8},{4,12},{8,0},{12,4},{16,24},{20,28},{24,16},{28,20},{1,9},{5... | collective-permute-start | bytes 589832 | tf_op jit(solution)/shard_map/ppermute | solution.py:187
  37.8 9.1 %collective-permute-start.12 = (bf16[2,2,32,768]{3,2,1,0:T(8,128)(2,1)S(1)}, bf16[2,2,32,768]{3,2,1,0:T(8,128)(2,1)S(1)}, u32[]{:S(2)}, u32[]{:S(2)}) collective-permute-start(bf16[2,2,32,768]{3,2,1,0:T(8,128)(2,1)S(1)} %get-tuple-element.44), channel_id=1, source_target_pairs={{0,1},{1,0},{2,3},{3,2},{4,5},{5,4},{6,7},{7,6},{8,9},{9,8},{10,11... | collective-permute-start | bytes 589832 | tf_op jit(solution)/shard_map/ppermute | solution.py:185
  40.8 6.6 %collective-permute-start.11 = (bf16[2,32,768]{2,1,0:T(8,128)(2,1)S(1)}, bf16[2,32,768]{2,1,0:T(8,128)(2,1)S(1)}, u32[]{:S(2)}, u32[]{:S(2)}) collective-permute-start(bf16[2,32,768]{2,1,0:T(8,128)(2,1)S(1)} %get-tuple-element.43), channel_id=1, source_target_pairs={{0,10},{1,11},{2,8},{3,9},{4,14},{5,15},{6,12},{7,13},{8,2},{9,3},... | collective-permute-start | bytes 294920 | tf_op jit(solution)/shard_map/ppermute | solution.py:191
  45.1 11.6 %collective-permute-start.17 = (bf16[2,2,32,768]{3,2,1,0:T(8,128)(2,1)S(1)}, bf16[2,2,32,768]{3,2,1,0:T(8,128)(2,1)S(1)}, u32[]{:S(2)}, u32[]{:S(2)}) collective-permute-start(bf16[2,2,32,768]{3,2,1,0:T(8,128)(2,1)S(1)} %get-tuple-element.51), channel_id=1, source_target_pairs={{0,1},{1,0},{2,3},{3,2},{4,5},{5,4},{6,7},{7,6},{8,9},{9,8},{10,11... | collective-permute-start | bytes 589832 | tf_op jit(solution)/shard_map/ppermute | solution.py:185
  47.4 9.3 %collective-permute-start.13 = (bf16[2,32,768]{2,1,0:T(8,128)(2,1)S(1)}, bf16[2,32,768]{2,1,0:T(8,128)(2,1)S(1)}, u32[]{:S(2)}, u32[]{:S(2)}) collective-permute-start(bf16[2,32,768]{2,1,0:T(8,128)(2,1)S(1)} %get-tuple-element.47), channel_id=1, source_target_pairs={{0,8},{4,12},{8,0},{12,4},{16,24},{20,28},{24,16},{28,20},{1,9},{5... | collective-permute-start | bytes 294920 | tf_op jit(solution)/shard_map/ppermute | solution.py:187
  52.4 7.5 %collective-permute-start.14 = (bf16[2,32,768]{2,1,0:T(8,128)(2,1)S(1)}, bf16[2,32,768]{2,1,0:T(8,128)(2,1)S(1)}, u32[]{:S(2)}, u32[]{:S(2)}) collective-permute-start(bf16[2,32,768]{2,1,0:T(8,128)(2,1)S(1)} %get-tuple-element.48), channel_id=1, source_target_pairs={{0,18},{1,19},{2,16},{3,17},{4,22},{5,23},{6,20},{7,21},{8,26},{9,... | collective-permute-start | bytes 294920 | tf_op jit(solution)/shard_map/ppermute | solution.py:191
  56.8 4.7 %collective-permute-start.18 = (bf16[2,32,768]{2,1,0:T(8,128)(2,1)S(1)}, bf16[2,32,768]{2,1,0:T(8,128)(2,1)S(1)}, u32[]{:S(2)}, u32[]{:S(2)}) collective-permute-start(bf16[2,32,768]{2,1,0:T(8,128)(2,1)S(1)} %get-tuple-element.54), channel_id=1, source_target_pairs={{0,16},{4,20},{8,24},{12,28},{16,0},{20,4},{24,8},{28,12},{1,17},{... | collective-permute-start | bytes 294920 | tf_op jit(solution)/shard_map/ppermute | solution.py:187
  56.9 7.5 %collective-permute-start.19 = (bf16[2,32,768]{2,1,0:T(8,128)(2,1)S(1)}, bf16[2,32,768]{2,1,0:T(8,128)(2,1)S(1)}, u32[]{:S(2)}, u32[]{:S(2)}) collective-permute-start(bf16[2,32,768]{2,1,0:T(8,128)(2,1)S(1)} %get-tuple-element.55), channel_id=1, source_target_pairs={{0,26},{1,27},{2,24},{3,25},{4,30},{5,31},{6,28},{7,29},{8,18},{9,... | collective-permute-start | bytes 294920 | tf_op jit(solution)/shard_map/ppermute | solution.py:191
  58.3 6.6 %collective-permute-start.20 = (bf16[2,32,768]{2,1,0:T(8,128)(2,1)S(1)}, bf16[2,32,768]{2,1,0:T(8,128)(2,1)S(1)}, u32[]{:S(2)}, u32[]{:S(2)}) collective-permute-start(bf16[2,32,768]{2,1,0:T(8,128)(2,1)S(1)} %get-tuple-element.56), channel_id=1, source_target_pairs={{0,24},{4,28},{8,16},{12,20},{16,8},{20,12},{24,0},{28,4},{1,25},{... | collective-permute-start | bytes 294920 | tf_op jit(solution)/shard_map/ppermute | solution.py:187

commit v5 on v4

--- a/solution.py
+++ b/solution.py
@@ -266,7 +266,7 @@
     if pair:
         results = projected(pair, (stays[0],))
         for k, send, keep in zip(pair, results, results[len(pair) :]):
-            exchanged(k, send, keep, found[1][:1] if k == 2 else ())
+            exchanged(k, send, keep, () if k == 2 else ())
     if chips > 3:
         specs, arrays = after(*(results[-1], found[0][0]))
         low, high = pl.pallas_call(
@@ -278,7 +278,7 @@
         )(parts[1][0], parts[2][0], *arrays)
         parts[3] = [swap(low, 4, 0), swap(high, 2, 0)]
     for k in range(3, chips):
-        exchanged(k, *projected([k], (stays[1],)), (found[1][1:]) if k == 3 else ())
+        exchanged(k, *projected([k], (stays[1],)))
     if chips > 1:
         found[chips - 1][1] = swap(stays[chips - 1], 2 * (chips - 1), 0)
     flat = wide % 128 == 0

time: 65.8 us -> 63.8 us (0.970)
  waiting for transfers between devices: 21.2 us -> 17.7 us
  starting transfers between devices: 33.1 us -> 34.5 us
    ppermute x12, waiting for transfers between devices: 12.1 us -> 8.13 us  [swap(): return lax.ppermute(value, 'seq', [(i, i ^ k) for i in range(seq)])]
    ppermute x3, starting transfers between devices: 3.72 us -> 7.49 us  [swap(): return lax.ppermute(value, ('seq', 'head'), pairs)]
    ppermute x12, starting transfers between devices: 17.9 us -> 15.6 us  [swap(): return lax.ppermute(value, 'seq', [(i, i ^ k) for i in range(seq)])]
  transfers between devices with their start and end apart: 21 -> 21, of which waited for: 13 -> 12; matrix products, arithmetic and copies ran while one was open for 0% -> 0% of each run, Pallas kernels for 16% -> 16%
where the time goes in v5:
time: 63.8 us; the launch traced here: 63.6 us
  starting transfers between devices  34.5 us (54%)
  waiting for transfers between devices  17.7 us (28%)
  Pallas kernels  11.2 us (18%)
    ppermute x12, starting transfers between devices, swap(): return lax.ppermute(value, 'seq', [(i, i ^ k) for i in range(seq)])  15.6 us
    ppermute x5, starting transfers between devices, swap(): return lax.ppermute(value, 'head', [(i, i ^ z) for i in range(groups)])  9.64 us
    ppermute x12, waiting for transfers between devices, swap(): return lax.ppermute(value, 'seq', [(i, i ^ k) for i in range(seq)])  8.13 us
    ppermute x3, starting transfers between devices, swap(): return lax.ppermute(value, ('seq', 'head'), pairs)  7.49 us
    ppermute x5, waiting for transfers between devices, swap(): return lax.ppermute(value, 'head', [(i, i ^ z) for i in range(groups)])  5.77 us
    pallas_call x3, Pallas kernels, projected(): pl.pallas_call(functools.partial(project_kernel, len(pieces), n), out_sha...  4.69 us
    ppermute x3, waiting for transfers between devices, swap(): return lax.ppermute(value, ('seq', 'head'), pairs)  3.82 us
    pallas_call x1, Pallas kernels, local(): pl.pallas_call(attend_kernel, out_shape=shaped(tok_rows, feat), in_specs=...  3.23 us
  transfers between devices with their start and end apart: 21, of which 12 were waited for; matrix products, arithmetic and copies ran while one was open for 0% of the time, Pallas kernels for 16%

profile of v5, /device:TPU:0, one launch (start us, length us, event | category | flops | bytes accessed | tf_op | source)
XLA Modules:
  0.0 63.6 jit_solution(18295335073711629024)
XLA Ops:
  0.0 0.5 collective-permute-start.5
  0.5 2.2 %shard_map.64 = (bf16[2,16,1536]{2,1,0:T(8,128)(2,1)S(1)}, bf16[2,64,1536]{2,1,0:T(8,128)(2,1)S(1)}, s32[12,320]{1,0:T(8,128)S(1)}, bf16[128,1536]{1,0:T(8,128)(...) custom-call(s32[1,16]{1,0:T(1,128)} %picks_ref.1, s32[12]{0:T(128)} %band_ref.1, ...), custom_call_target="tpu_custom_call" | custom-call | tf_op jit(solution)/shard_map/pallas_call | solution.py:195
  2.6 2.6 %collective-permute-start.1 = (bf16[2,16,1536]{2,1,0:T(8,128)(2,1)S(1)}, bf16[2,16,1536]{2,1,0:T(8,128)(2,1)S(1)}, u32[]{:S(2)}, u32[]{:S(2)}) collective-permute-start(bf16[2,16,1536]{2,1,0:T(8,128)(2,1)S(1)} %get-tuple-element.36.refs_0_), channel_id=1, source_target_pairs={{0,8},{4,12},{8,0},{12,4},{16,24},{20,28},{24,16},{28,20},{1,9},{5... | collective-permute-start | bytes 294920 | tf_op jit(solution)/shard_map/ppermute | solution.py:187
  5.2 1.5 %collective-permute-start.2 = (bf16[2,16,1536]{2,1,0:T(8,128)(2,1)S(1)}, bf16[2,16,1536]{2,1,0:T(8,128)(2,1)S(1)}, u32[]{:S(2)}, u32[]{:S(2)}) collective-permute-start(bf16[2,16,1536]{2,1,0:T(8,128)(2,1)S(1)} %get-tuple-element.36.refs_0_), channel_id=1, source_target_pairs={{0,16},{4,20},{8,24},{12,28},{16,0},{20,4},{24,8},{28,12},{1,17},{... | collective-permute-start | bytes 294920 | tf_op jit(solution)/shard_map/ppermute | solution.py:187
  6.7 0.0 collective-permute-start.3
  6.7 1.9 %collective-permute-start = (bf16[2,64,1536]{2,1,0:T(8,128)(2,1)S(1)}, bf16[2,64,1536]{2,1,0:T(8,128)(2,1)S(1)}, u32[]{:S(2)}, u32[]{:S(2)}) collective-permute-start(bf16[2,64,1536]{2,1,0:T(8,128)(2,1)S(1)} %get-tuple-element.35), channel_id=1, source_target_pairs={{0,4},{4,8},{8,12},{12,16},{16,20},{20,24},{24,28},{1,5},{5,9},{9,... | collective-permute-start | bytes 1179656 | tf_op jit(solution)/shard_map/ppermute | solution.py:209
  8.6 0.1 collective-permute-done.1.refs_1_
  8.7 2.6 %collective-permute-done.2.refs_2_ = bf16[2,16,1536]{2,1,0:T(8,128)(2,1)S(1)} collective-permute-done((bf16[2,16,1536]{2,1,0:T(8,128)(2,1)S(1)}, bf16[2,16,1536]{2,1,0:T(8,128)(2,1)S(1)}, u32[]{:S(2)}, u32[]{:S(2)}) %collective-permute-start.2) | collective-permute-done | bytes 98336 | tf_op jit(solution)/shard_map/ppermute | solution.py:187
  11.3 1.0 %collective-permute-done.3.refs_3_ = bf16[2,16,1536]{2,1,0:T(8,128)(2,1)S(1)} collective-permute-done((bf16[2,16,1536]{2,1,0:T(8,128)(2,1)S(1)}, bf16[2,16,1536]{2,1,0:T(8,128)(2,1)S(1)}, u32[]{:S(2)}, u32[]{:S(2)}) %collective-permute-start.3) | collective-permute-done | bytes 98336 | tf_op jit(solution)/shard_map/ppermute | solution.py:187
  12.3 0.1 collective-permute-start.4
  12.4 0.0 collective-permute-done.halo_ref
  12.4 1.7 %collective-permute-done.4.other_ref = bf16[4,2,16,1536]{3,2,1,0:T(8,128)(2,1)S(1)} collective-permute-done((bf16[4,2,16,1536]{3,2,1,0:T(8,128)(2,1)S(1)}, bf16[4,2,16,1536]{3,2,1,0:T(8,128)(2,1)S(1)}, u32[]{:S(2)}, u32[]{:S(2)}) %collective-permute-start.4) | collective-permute-done | bytes 393248 | tf_op jit(solution)/shard_map/ppermute | solution.py:187
  14.1 3.2 %shard_map.66 = bf16[128,1536]{1,0:T(8,128)(2,1)S(1)} custom-call(s32[12,320]{1,0:T(8,128)S(1)} %get-tuple-element.31.width_ref, bf16[128,1536]{1,0:T(8,128)(2,1)S(1)} %get-tuple-element.32.q_ref, bf16[128,1536]{1,0:T(8,128)(2,1)S(1)} %get-tuple-element.33.k_ref, bf16[128,1536]{1,0:T(8,128)(2,1)S(1)} %get-tuple-element.34.v_ref, ...), custom_call_target="tpu_custom_call" | custom-call | tf_op jit(solution)/shard_map/pallas_call | solution.py:218
  17.3 3.8 %collective-permute-start.8 = (bf16[4,32,1536]{2,1,0:T(8,128)(2,1)S(1)}, bf16[4,32,1536]{2,1,0:T(8,128)(2,1)S(1)}, u32[]{:S(2)}, u32[]{:S(2)}) collective-permute-start(bf16[4,32,1536]{2,1,0:T(8,128)(2,1)S(1)} %bitcast.1), channel_id=1, source_target_pairs={{0,8},{4,12},{8,0},{12,4},{16,24},{20,28},{24,16},{28,20},{1,9},{5... | collective-permute-start | bytes 1179656 | tf_op jit(solution)/shard_map/ppermute | solution.py:187
  21.1 1.5 %collective-permute-start.9 = (bf16[4,32,1536]{2,1,0:T(8,128)(2,1)S(1)}, bf16[4,32,1536]{2,1,0:T(8,128)(2,1)S(1)}, u32[]{:S(2)}, u32[]{:S(2)}) collective-permute-start(bf16[4,32,1536]{2,1,0:T(8,128)(2,1)S(1)} %bitcast.2), channel_id=1, source_target_pairs={{0,16},{4,20},{8,24},{12,28},{16,0},{20,4},{24,8},{28,12},{1,17},{... | collective-permute-start | bytes 1179656 | tf_op jit(solution)/shard_map/ppermute | solution.py:187
  22.6 0.0 collective-permute-done.5.refs_2_.refs_3_
  22.6 1.6 %shard_map.67 = (bf16[2,2,32,768]{3,2,1,0:T(8,128)(2,1)S(1)}, bf16[2,2,32,768]{3,2,1,0:T(8,128)(2,1)S(1)}) custom-call(bf16[4,32,1536]{2,1,0:T(8,128)(2,1)S(1)} %bitcast.3, bf16[768,1536]{1,0:T(8,128)(2,1)S(1)} %copy-done, bf16[768,1536]{1,0:T(8,128)(2,1)S(1)} %collective-permute-done.5.refs_2_.refs_3_), custom_call_target="tpu_custom_call" | custom-call | flops 603979776 | bytes 4718592 | tf_op jit(solution)/shard_map/pallas_call | solution.py:237
  24.3 1.6 %collective-permute-start.6 = (bf16[2,2,32,768]{3,2,1,0:T(8,128)(2,1)S(1)}, bf16[2,2,32,768]{3,2,1,0:T(8,128)(2,1)S(1)}, u32[]{:S(2)}, u32[]{:S(2)}) collective-permute-start(bf16[2,2,32,768]{3,2,1,0:T(8,128)(2,1)S(1)} %get-tuple-element.37), channel_id=1, source_target_pairs={{0,1},{1,0},{2,3},{3,2},{4,5},{5,4},{6,7},{7,6},{8,9},{9,8},{10,11... | collective-permute-start | bytes 589832 | tf_op jit(solution)/shard_map/ppermute | solution.py:185
  25.9 4.1 %collective-permute-done.6.came_ref = bf16[2,2,32,768]{3,2,1,0:T(8,128)(2,1)S(1)} collective-permute-done((bf16[2,2,32,768]{3,2,1,0:T(8,128)(2,1)S(1)}, bf16[2,2,32,768]{3,2,1,0:T(8,128)(2,1)S(1)}, u32[]{:S(2)}, u32[]{:S(2)}) %collective-permute-start.6) | collective-permute-done | bytes 196640 | tf_op jit(solution)/shard_map/ppermute | solution.py:185
  30.1 3.4 %collective-permute-start.7 = (bf16[2,32,768]{2,1,0:T(8,128)(2,1)S(1)}, bf16[2,32,768]{2,1,0:T(8,128)(2,1)S(1)}, u32[]{:S(2)}, u32[]{:S(2)}) collective-permute-start(bf16[2,32,768]{2,1,0:T(8,128)(2,1)S(1)} %get-tuple-element.39), channel_id=1, source_target_pairs={{0,2},{1,3},{2,0},{3,1},{4,6},{5,7},{6,4},{7,5},{8,10},{9,11},{10,... | collective-permute-start | bytes 294920 | tf_op jit(solution)/shard_map/ppermute | solution.py:185
  33.5 0.0 collective-permute-done.8.refs_0_.first_ref
  33.5 0.0 collective-permute-done.9.refs_1_.second_ref
  33.5 1.4 %shard_map.69 = (bf16[2,2,32,768]{3,2,1,0:T(8,128)(2,1)S(1)}, bf16[2,2,32,768]{3,2,1,0:T(8,128)(2,1)S(1)}, bf16[2,2,32,768]{3,2,1,0:T(8,128)(2,1)S(1)}, bf16[2,2,32,768]{3,2,1,0:T(8,128)(2,1)S(1)}) custom-call(bf16[4,32,1536]{2,1,0:T(8,128)(2,1)S(1)} %collective-permute-done.8.refs_0_.first_ref, ...), custom_call_target="tpu_custom_call" | custom-call | flops 1207959552 | bytes 4718592 | tf_op jit(solution)/shard_map/pallas_call | solution.py:237
  34.9 0.9 %collective-permute-start.10 = (bf16[2,2,32,768]{3,2,1,0:T(8,128)(2,1)S(1)}, bf16[2,2,32,768]{3,2,1,0:T(8,128)(2,1)S(1)}, u32[]{:S(2)}, u32[]{:S(2)}) collective-permute-start(bf16[2,2,32,768]{3,2,1,0:T(8,128)(2,1)S(1)} %get-tuple-element.41), channel_id=1, source_target_pairs={{0,1},{1,0},{2,3},{3,2},{4,5},{5,4},{6,7},{7,6},{8,9},{9,8},{10,11... | collective-permute-start | bytes 589832 | tf_op jit(solution)/shard_map/ppermute | solution.py:185
  35.8 0.8 %collective-permute-done.7.refs_1_.refs_0_ = bf16[2,32,768]{2,1,0:T(8,128)(2,1)S(1)} collective-permute-done((bf16[2,32,768]{2,1,0:T(8,128)(2,1)S(1)}, bf16[2,32,768]{2,1,0:T(8,128)(2,1)S(1)}, u32[]{:S(2)}, u32[]{:S(2)}) %collective-permute-start.7) | collective-permute-done | bytes 98336 | tf_op jit(solution)/shard_map/ppermute | solution.py:185
  36.6 0.1 collective-permute-start.15
  36.7 1.2 %collective-permute-start.16 = (bf16[2,32,1536]{2,1,0:T(8,128)(2,1)S(1)}, bf16[2,32,1536]{2,1,0:T(8,128)(2,1)S(1)}, u32[]{:S(2)}, u32[]{:S(2)}) collective-permute-start(bf16[2,32,1536]{2,1,0:T(8,128)(2,1)S(1)} %get-tuple-element.50), channel_id=1, source_target_pairs={{0,8},{4,12},{8,0},{12,4},{16,24},{20,28},{24,16},{28,20},{1,9},{5... | collective-permute-start | bytes 589832 | tf_op jit(solution)/shard_map/ppermute | solution.py:187
  37.8 1.9 %collective-permute-start.12 = (bf16[2,2,32,768]{3,2,1,0:T(8,128)(2,1)S(1)}, bf16[2,2,32,768]{3,2,1,0:T(8,128)(2,1)S(1)}, u32[]{:S(2)}, u32[]{:S(2)}) collective-permute-start(bf16[2,2,32,768]{3,2,1,0:T(8,128)(2,1)S(1)} %get-tuple-element.44), channel_id=1, source_target_pairs={{0,1},{1,0},{2,3},{3,2},{4,5},{5,4},{6,7},{7,6},{8,9},{9,8},{10,11... | collective-permute-start | bytes 589832 | tf_op jit(solution)/shard_map/ppermute | solution.py:185
  39.8 0.9 %collective-permute-done.10.came_ref = bf16[2,2,32,768]{3,2,1,0:T(8,128)(2,1)S(1)} collective-permute-done((bf16[2,2,32,768]{3,2,1,0:T(8,128)(2,1)S(1)}, bf16[2,2,32,768]{3,2,1,0:T(8,128)(2,1)S(1)}, u32[]{:S(2)}, u32[]{:S(2)}) %collective-permute-start.10) | collective-permute-done | bytes 196640 | tf_op jit(solution)/shard_map/ppermute | solution.py:185
  40.7 1.7 %collective-permute-done.15.refs_0_ = bf16[2,32,1536]{2,1,0:T(8,128)(2,1)S(1)} collective-permute-done((bf16[2,32,1536]{2,1,0:T(8,128)(2,1)S(1)}, bf16[2,32,1536]{2,1,0:T(8,128)(2,1)S(1)}, u32[]{:S(2)}, u32[]{:S(2)}) %collective-permute-start.15) | collective-permute-done | bytes 196640 | tf_op jit(solution)/shard_map/ppermute | solution.py:187
  42.3 0.1 collective-permute-done.16.refs_1_
  42.4 1.6 %shard_map.73 = (bf16[2,2,32,768]{3,2,1,0:T(8,128)(2,1)S(1)}, bf16[2,2,32,768]{3,2,1,0:T(8,128)(2,1)S(1)}) custom-call(bf16[2,32,1536]{2,1,0:T(8,128)(2,1)S(1)} %collective-permute-done.15.refs_0_, bf16[2,32,1536]{2,1,0:T(8,128)(2,1)S(1)} %collective-permute-done.16.refs_1_, bf16[768,1536]{1,0:T(8,128)(2,1)S(1)} %copy-done, ...), custom_call_target="tpu_custom_call" | custom-call | flops 603979776 | bytes 4718592 | tf_op jit(solution)/shard_map/pallas_call | solution.py:237
  44.0 1.8 %collective-permute-start.17 = (bf16[2,2,32,768]{3,2,1,0:T(8,128)(2,1)S(1)}, bf16[2,2,32,768]{3,2,1,0:T(8,128)(2,1)S(1)}, u32[]{:S(2)}, u32[]{:S(2)}) collective-permute-start(bf16[2,2,32,768]{3,2,1,0:T(8,128)(2,1)S(1)} %get-tuple-element.51), channel_id=1, source_target_pairs={{0,1},{1,0},{2,3},{3,2},{4,5},{5,4},{6,7},{7,6},{8,9},{9,8},{10,11... | collective-permute-start | bytes 589832 | tf_op jit(solution)/shard_map/ppermute | solution.py:185
  45.9 3.3 %collective-permute-start.11 = (bf16[2,32,768]{2,1,0:T(8,128)(2,1)S(1)}, bf16[2,32,768]{2,1,0:T(8,128)(2,1)S(1)}, u32[]{:S(2)}, u32[]{:S(2)}) collective-permute-start(bf16[2,32,768]{2,1,0:T(8,128)(2,1)S(1)} %get-tuple-element.43), channel_id=1, source_target_pairs={{0,10},{1,11},{2,8},{3,9},{4,14},{5,15},{6,12},{7,13},{8,2},{9,3},... | collective-permute-start | bytes 294920 | tf_op jit(solution)/shard_map/ppermute | solution.py:191
  49.1 0.1 shard_map.71
  49.2 1.2 %collective-permute-start.13 = (bf16[2,32,768]{2,1,0:T(8,128)(2,1)S(1)}, bf16[2,32,768]{2,1,0:T(8,128)(2,1)S(1)}, u32[]{:S(2)}, u32[]{:S(2)}) collective-permute-start(bf16[2,32,768]{2,1,0:T(8,128)(2,1)S(1)} %get-tuple-element.47), channel_id=1, source_target_pairs={{0,8},{4,12},{8,0},{12,4},{16,24},{20,28},{24,16},{28,20},{1,9},{5... | collective-permute-start | bytes 294920 | tf_op jit(solution)/shard_map/ppermute | solution.py:187
  50.4 1.3 %collective-permute-start.14 = (bf16[2,32,768]{2,1,0:T(8,128)(2,1)S(1)}, bf16[2,32,768]{2,1,0:T(8,128)(2,1)S(1)}, u32[]{:S(2)}, u32[]{:S(2)}) collective-permute-start(bf16[2,32,768]{2,1,0:T(8,128)(2,1)S(1)} %get-tuple-element.48), channel_id=1, source_target_pairs={{0,18},{1,19},{2,16},{3,17},{4,22},{5,23},{6,20},{7,21},{8,26},{9,... | collective-permute-start | bytes 294920 | tf_op jit(solution)/shard_map/ppermute | solution.py:191
  51.7 0.1 shard_map.74
  51.7 2.3 %collective-permute-start.18 = (bf16[2,32,768]{2,1,0:T(8,128)(2,1)S(1)}, bf16[2,32,768]{2,1,0:T(8,128)(2,1)S(1)}, u32[]{:S(2)}, u32[]{:S(2)}) collective-permute-start(bf16[2,32,768]{2,1,0:T(8,128)(2,1)S(1)} %get-tuple-element.54), channel_id=1, source_target_pairs={{0,16},{4,20},{8,24},{12,28},{16,0},{20,4},{24,8},{28,12},{1,17},{... | collective-permute-start | bytes 294920 | tf_op jit(solution)/shard_map/ppermute | solution.py:187
  54.1 3.0 %collective-permute-start.19 = (bf16[2,32,768]{2,1,0:T(8,128)(2,1)S(1)}, bf16[2,32,768]{2,1,0:T(8,128)(2,1)S(1)}, u32[]{:S(2)}, u32[]{:S(2)}) collective-permute-start(bf16[2,32,768]{2,1,0:T(8,128)(2,1)S(1)} %get-tuple-element.55), channel_id=1, source_target_pairs={{0,26},{1,27},{2,24},{3,25},{4,30},{5,31},{6,28},{7,29},{8,18},{9,... | collective-permute-start | bytes 294920 | tf_op jit(solution)/shard_map/ppermute | solution.py:191
  57.0 0.0 collective-permute-done.11.refs_2_
  57.0 0.9 %collective-permute-start.20 = (bf16[2,32,768]{2,1,0:T(8,128)(2,1)S(1)}, bf16[2,32,768]{2,1,0:T(8,128)(2,1)S(1)}, u32[]{:S(2)}, u32[]{:S(2)}) collective-permute-start(bf16[2,32,768]{2,1,0:T(8,128)(2,1)S(1)} %get-tuple-element.56), channel_id=1, source_target_pairs={{0,24},{4,28},{8,16},{12,20},{16,8},{20,12},{24,0},{28,4},{1,25},{... | collective-permute-start | bytes 294920 | tf_op jit(solution)/shard_map/ppermute | solution.py:187
  57.9 0.0 collective-permute-done.13.refs_3_
  57.9 0.6 collective-permute-done.14.refs_4_
  58.5 0.0 collective-permute-done.18.refs_5_
  58.5 3.3 %collective-permute-done.19.refs_6_ = bf16[2,32,768]{2,1,0:T(8,128)(2,1)S(1)} collective-permute-done((bf16[2,32,768]{2,1,0:T(8,128)(2,1)S(1)}, bf16[2,32,768]{2,1,0:T(8,128)(2,1)S(1)}, u32[]{:S(2)}, u32[]{:S(2)}) %collective-permute-start.19) | collective-permute-done | bytes 98336 | tf_op jit(solution)/shard_map/ppermute | solution.py:191
  61.7 1.0 %collective-permute-done.20.refs_7_ = bf16[2,32,768]{2,1,0:T(8,128)(2,1)S(1)} collective-permute-done((bf16[2,32,768]{2,1,0:T(8,128)(2,1)S(1)}, bf16[2,32,768]{2,1,0:T(8,128)(2,1)S(1)}, u32[]{:S(2)}, u32[]{:S(2)}) %collective-permute-start.20) | collective-permute-done | bytes 98336 | tf_op jit(solution)/shard_map/ppermute | solution.py:187
  62.8 0.8 %shard_map.75 = bf16[32,6144]{1,0:T(8,128)(2,1)} custom-call(bf16[2,32,768]{2,1,0:T(8,128)(2,1)S(1)} %collective-permute-done.7.refs_1_.refs_0_, bf16[2,32,768]{2,1,0:T(8,128)(2,1)S(1)} %get-tuple-element.40.refs_4_.refs_1_, bf16[2,32,768]{2,1,0:T(8,128)(2,1)S(1)} %collective-permute-done.11.refs_2_, ...), custom_call_target="tpu_custom_call" | custom-call | tf_op jit(solution)/shard_map/pallas_call | solution.py:285
  (8 shorter events, 0.2 us)
Async XLA Ops:
  0.0 22.6 %copy-start = (bf16[768,1536]{1,0:T(8,128)(2,1)S(1)}, bf16[768,1536]{1,0:T(8,128)(2,1)}, u32[]{:S(2)}) copy-start(bf16[768,1536]{1,0:T(8,128)(2,1)} %refs_2_.3) | copy-start | bytes 7077892
  0.0 22.6 %collective-permute-start.5 = (bf16[768,1536]{1,0:T(8,128)(2,1)}, bf16[768,1536]{1,0:T(8,128)(2,1)S(1)}, u32[]{:S(2)}, u32[]{:S(2)}) collective-permute-start(bf16[768,1536]{1,0:T(8,128)(2,1)} %refs_2_.3), channel_id=1, source_target_pairs={{0,4},{4,0},{8,12},{12,8},{16,20},{20,16},{24,28},{28,24},{1,5},{5... | collective-permute-start | bytes 7077896 | tf_op jit(solution)/shard_map/ppermute | solution.py:187
  2.6 6.0 %collective-permute-start.1 = (bf16[2,16,1536]{2,1,0:T(8,128)(2,1)S(1)}, bf16[2,16,1536]{2,1,0:T(8,128)(2,1)S(1)}, u32[]{:S(2)}, u32[]{:S(2)}) collective-permute-start(bf16[2,16,1536]{2,1,0:T(8,128)(2,1)S(1)} %get-tuple-element.36.refs_0_), channel_id=1, source_target_pairs={{0,8},{4,12},{8,0},{12,4},{16,24},{20,28},{24,16},{28,20},{1,9},{5... | collective-permute-start | bytes 294920 | tf_op jit(solution)/shard_map/ppermute | solution.py:187
  5.2 6.1 %collective-permute-start.2 = (bf16[2,16,1536]{2,1,0:T(8,128)(2,1)S(1)}, bf16[2,16,1536]{2,1,0:T(8,128)(2,1)S(1)}, u32[]{:S(2)}, u32[]{:S(2)}) collective-permute-start(bf16[2,16,1536]{2,1,0:T(8,128)(2,1)S(1)} %get-tuple-element.36.refs_0_), channel_id=1, source_target_pairs={{0,16},{4,20},{8,24},{12,28},{16,0},{20,4},{24,8},{28,12},{1,17},{... | collective-permute-start | bytes 294920 | tf_op jit(solution)/shard_map/ppermute | solution.py:187
  6.7 5.5 %collective-permute-start.3 = (bf16[2,16,1536]{2,1,0:T(8,128)(2,1)S(1)}, bf16[2,16,1536]{2,1,0:T(8,128)(2,1)S(1)}, u32[]{:S(2)}, u32[]{:S(2)}) collective-permute-start(bf16[2,16,1536]{2,1,0:T(8,128)(2,1)S(1)} %get-tuple-element.36.refs_0_), channel_id=1, source_target_pairs={{0,24},{4,28},{8,16},{12,20},{16,8},{20,12},{24,0},{28,4},{1,25},{... | collective-permute-start | bytes 294920 | tf_op jit(solution)/shard_map/ppermute | solution.py:187
  6.7 5.6 %collective-permute-start = (bf16[2,64,1536]{2,1,0:T(8,128)(2,1)S(1)}, bf16[2,64,1536]{2,1,0:T(8,128)(2,1)S(1)}, u32[]{:S(2)}, u32[]{:S(2)}) collective-permute-start(bf16[2,64,1536]{2,1,0:T(8,128)(2,1)S(1)} %get-tuple-element.35), channel_id=1, source_target_pairs={{0,4},{4,8},{8,12},{12,16},{16,20},{20,24},{24,28},{1,5},{5,9},{9,... | collective-permute-start | bytes 1179656 | tf_op jit(solution)/shard_map/ppermute | solution.py:209
  12.3 1.8 %collective-permute-start.4 = (bf16[4,2,16,1536]{3,2,1,0:T(8,128)(2,1)S(1)}, bf16[4,2,16,1536]{3,2,1,0:T(8,128)(2,1)S(1)}, u32[]{:S(2)}, u32[]{:S(2)}) collective-permute-start(bf16[4,2,16,1536]{3,2,1,0:T(8,128)(2,1)S(1)} %shard_map.65.mine_ref), channel_id=1, source_target_pairs={{0,4},{4,0},{8,12},{12,8},{16,20},{20,16},{24,28},{28,24},{1,5},{5... | collective-permute-start | bytes 1179656 | tf_op jit(solution)/shard_map/ppermute | solution.py:187
  17.3 16.1 %collective-permute-start.8 = (bf16[4,32,1536]{2,1,0:T(8,128)(2,1)S(1)}, bf16[4,32,1536]{2,1,0:T(8,128)(2,1)S(1)}, u32[]{:S(2)}, u32[]{:S(2)}) collective-permute-start(bf16[4,32,1536]{2,1,0:T(8,128)(2,1)S(1)} %bitcast.1), channel_id=1, source_target_pairs={{0,8},{4,12},{8,0},{12,4},{16,24},{20,28},{24,16},{28,20},{1,9},{5... | collective-permute-start | bytes 1179656 | tf_op jit(solution)/shard_map/ppermute | solution.py:187
  21.1 12.4 %collective-permute-start.9 = (bf16[4,32,1536]{2,1,0:T(8,128)(2,1)S(1)}, bf16[4,32,1536]{2,1,0:T(8,128)(2,1)S(1)}, u32[]{:S(2)}, u32[]{:S(2)}) collective-permute-start(bf16[4,32,1536]{2,1,0:T(8,128)(2,1)S(1)} %bitcast.2), channel_id=1, source_target_pairs={{0,16},{4,20},{8,24},{12,28},{16,0},{20,4},{24,8},{28,12},{1,17},{... | collective-permute-start | bytes 1179656 | tf_op jit(solution)/shard_map/ppermute | solution.py:187
  24.3 5.7 %collective-permute-start.6 = (bf16[2,2,32,768]{3,2,1,0:T(8,128)(2,1)S(1)}, bf16[2,2,32,768]{3,2,1,0:T(8,128)(2,1)S(1)}, u32[]{:S(2)}, u32[]{:S(2)}) collective-permute-start(bf16[2,2,32,768]{3,2,1,0:T(8,128)(2,1)S(1)} %get-tuple-element.37), channel_id=1, source_target_pairs={{0,1},{1,0},{2,3},{3,2},{4,5},{5,4},{6,7},{7,6},{8,9},{9,8},{10,11... | collective-permute-start | bytes 589832 | tf_op jit(solution)/shard_map/ppermute | solution.py:185
  30.1 6.5 %collective-permute-start.7 = (bf16[2,32,768]{2,1,0:T(8,128)(2,1)S(1)}, bf16[2,32,768]{2,1,0:T(8,128)(2,1)S(1)}, u32[]{:S(2)}, u32[]{:S(2)}) collective-permute-start(bf16[2,32,768]{2,1,0:T(8,128)(2,1)S(1)} %get-tuple-element.39), channel_id=1, source_target_pairs={{0,2},{1,3},{2,0},{3,1},{4,6},{5,7},{6,4},{7,5},{8,10},{9,11},{10,... | collective-permute-start | bytes 294920 | tf_op jit(solution)/shard_map/ppermute | solution.py:185
  34.9 5.7 %collective-permute-start.10 = (bf16[2,2,32,768]{3,2,1,0:T(8,128)(2,1)S(1)}, bf16[2,2,32,768]{3,2,1,0:T(8,128)(2,1)S(1)}, u32[]{:S(2)}, u32[]{:S(2)}) collective-permute-start(bf16[2,2,32,768]{3,2,1,0:T(8,128)(2,1)S(1)} %get-tuple-element.41), channel_id=1, source_target_pairs={{0,1},{1,0},{2,3},{3,2},{4,5},{5,4},{6,7},{7,6},{8,9},{9,8},{10,11... | collective-permute-start | bytes 589832 | tf_op jit(solution)/shard_map/ppermute | solution.py:185
  36.6 5.7 %collective-permute-start.15 = (bf16[2,32,1536]{2,1,0:T(8,128)(2,1)S(1)}, bf16[2,32,1536]{2,1,0:T(8,128)(2,1)S(1)}, u32[]{:S(2)}, u32[]{:S(2)}) collective-permute-start(bf16[2,32,1536]{2,1,0:T(8,128)(2,1)S(1)} %get-tuple-element.49), channel_id=1, source_target_pairs={{0,16},{4,20},{8,24},{12,28},{16,0},{20,4},{24,8},{28,12},{1,17},{... | collective-permute-start | bytes 589832 | tf_op jit(solution)/shard_map/ppermute | solution.py:187
  36.7 5.7 %collective-permute-start.16 = (bf16[2,32,1536]{2,1,0:T(8,128)(2,1)S(1)}, bf16[2,32,1536]{2,1,0:T(8,128)(2,1)S(1)}, u32[]{:S(2)}, u32[]{:S(2)}) collective-permute-start(bf16[2,32,1536]{2,1,0:T(8,128)(2,1)S(1)} %get-tuple-element.50), channel_id=1, source_target_pairs={{0,8},{4,12},{8,0},{12,4},{16,24},{20,28},{24,16},{28,20},{1,9},{5... | collective-permute-start | bytes 589832 | tf_op jit(solution)/shard_map/ppermute | solution.py:187
  37.8 11.3 %collective-permute-start.12 = (bf16[2,2,32,768]{3,2,1,0:T(8,128)(2,1)S(1)}, bf16[2,2,32,768]{3,2,1,0:T(8,128)(2,1)S(1)}, u32[]{:S(2)}, u32[]{:S(2)}) collective-permute-start(bf16[2,2,32,768]{3,2,1,0:T(8,128)(2,1)S(1)} %get-tuple-element.44), channel_id=1, source_target_pairs={{0,1},{1,0},{2,3},{3,2},{4,5},{5,4},{6,7},{7,6},{8,9},{9,8},{10,11... | collective-permute-start | bytes 589832 | tf_op jit(solution)/shard_map/ppermute | solution.py:185
  44.0 7.6 %collective-permute-start.17 = (bf16[2,2,32,768]{3,2,1,0:T(8,128)(2,1)S(1)}, bf16[2,2,32,768]{3,2,1,0:T(8,128)(2,1)S(1)}, u32[]{:S(2)}, u32[]{:S(2)}) collective-permute-start(bf16[2,2,32,768]{3,2,1,0:T(8,128)(2,1)S(1)} %get-tuple-element.51), channel_id=1, source_target_pairs={{0,1},{1,0},{2,3},{3,2},{4,5},{5,4},{6,7},{7,6},{8,9},{9,8},{10,11... | collective-permute-start | bytes 589832 | tf_op jit(solution)/shard_map/ppermute | solution.py:185
  45.9 11.2 %collective-permute-start.11 = (bf16[2,32,768]{2,1,0:T(8,128)(2,1)S(1)}, bf16[2,32,768]{2,1,0:T(8,128)(2,1)S(1)}, u32[]{:S(2)}, u32[]{:S(2)}) collective-permute-start(bf16[2,32,768]{2,1,0:T(8,128)(2,1)S(1)} %get-tuple-element.43), channel_id=1, source_target_pairs={{0,10},{1,11},{2,8},{3,9},{4,14},{5,15},{6,12},{7,13},{8,2},{9,3},... | collective-permute-start | bytes 294920 | tf_op jit(solution)/shard_map/ppermute | solution.py:191
  49.2 8.7 %collective-permute-start.13 = (bf16[2,32,768]{2,1,0:T(8,128)(2,1)S(1)}, bf16[2,32,768]{2,1,0:T(8,128)(2,1)S(1)}, u32[]{:S(2)}, u32[]{:S(2)}) collective-permute-start(bf16[2,32,768]{2,1,0:T(8,128)(2,1)S(1)} %get-tuple-element.47), channel_id=1, source_target_pairs={{0,8},{4,12},{8,0},{12,4},{16,24},{20,28},{24,16},{28,20},{1,9},{5... | collective-permute-start | bytes 294920 | tf_op jit(solution)/shard_map/ppermute | solution.py:187
  50.4 8.1 %collective-permute-start.14 = (bf16[2,32,768]{2,1,0:T(8,128)(2,1)S(1)}, bf16[2,32,768]{2,1,0:T(8,128)(2,1)S(1)}, u32[]{:S(2)}, u32[]{:S(2)}) collective-permute-start(bf16[2,32,768]{2,1,0:T(8,128)(2,1)S(1)} %get-tuple-element.48), channel_id=1, source_target_pairs={{0,18},{1,19},{2,16},{3,17},{4,22},{5,23},{6,20},{7,21},{8,26},{9,... | collective-permute-start | bytes 294920 | tf_op jit(solution)/shard_map/ppermute | solution.py:191
  51.7 6.7 %collective-permute-start.18 = (bf16[2,32,768]{2,1,0:T(8,128)(2,1)S(1)}, bf16[2,32,768]{2,1,0:T(8,128)(2,1)S(1)}, u32[]{:S(2)}, u32[]{:S(2)}) collective-permute-start(bf16[2,32,768]{2,1,0:T(8,128)(2,1)S(1)} %get-tuple-element.54), channel_id=1, source_target_pairs={{0,16},{4,20},{8,24},{12,28},{16,0},{20,4},{24,8},{28,12},{1,17},{... | collective-permute-start | bytes 294920 | tf_op jit(solution)/shard_map/ppermute | solution.py:187
  54.1 7.6 %collective-permute-start.19 = (bf16[2,32,768]{2,1,0:T(8,128)(2,1)S(1)}, bf16[2,32,768]{2,1,0:T(8,128)(2,1)S(1)}, u32[]{:S(2)}, u32[]{:S(2)}) collective-permute-start(bf16[2,32,768]{2,1,0:T(8,128)(2,1)S(1)} %get-tuple-element.55), channel_id=1, source_target_pairs={{0,26},{1,27},{2,24},{3,25},{4,30},{5,31},{6,28},{7,29},{8,18},{9,... | collective-permute-start | bytes 294920 | tf_op jit(solution)/shard_map/ppermute | solution.py:191
  57.0 5.7 %collective-permute-start.20 = (bf16[2,32,768]{2,1,0:T(8,128)(2,1)S(1)}, bf16[2,32,768]{2,1,0:T(8,128)(2,1)S(1)}, u32[]{:S(2)}, u32[]{:S(2)}) collective-permute-start(bf16[2,32,768]{2,1,0:T(8,128)(2,1)S(1)} %get-tuple-element.56), channel_id=1, source_target_pairs={{0,24},{4,28},{8,16},{12,20},{16,8},{20,12},{24,0},{28,4},{1,25},{... | collective-permute-start | bytes 294920 | tf_op jit(solution)/shard_map/ppermute | solution.py:187
